TPU v7x, 32 devices: a whole 2x2x4 slice. The times are simulated.
32 devices in a mesh: seq: 8 (over z, y), tp: 4 (over x, core).
Axes of the slice: x: 2, y: 2, z: 4, core: 2. Of those that a mesh axis runs over, the one named last changes fastest.
Arguments:
- tokens: bfloat16 [8192, 2048], P('seq', 'tp')
- bounds: int32 [8], P('seq'), may hold values from 0 to 1024, as said below
- cotangent: bfloat16 [8192, 2048], P('seq', 'tp'), may hold values from -6 to 6
- entry_weight: float32 [2048, 3, 2048], P('seq', None, 'tp'), may hold values from -0.125 to 0.125
- entry_first: float32 [2048, 3, 2048], P('seq', None, 'tp'), may hold values from -96 to 96
- entry_second: float32 [2048, 3, 2048], P('seq', None, 'tp'), may hold values from 983.04 to 3932.16
- exit_weight: float32 [2048, 2048], P('seq', 'tp'), may hold values from -0.125 to 0.125
- exit_first: float32 [2048, 2048], P('seq', 'tp'), may hold values from -96 to 96
- exit_second: float32 [2048, 2048], P('seq', 'tp'), may hold values from 983.04 to 3932.16
- expand_weight: float32 [2048, 2, 8192], P('seq', None, 'tp'), may hold values from -0.125 to 0.125
- expand_first: float32 [2048, 2, 8192], P('seq', None, 'tp'), may hold values from -32 to 32
- expand_second: float32 [2048, 2, 8192], P('seq', None, 'tp'), may hold values from 155.648 to 622.592
- shrink_weight: float32 [2048, 8192], P('seq', 'tp'), may hold values from -0.125 to 0.125
- shrink_first: float32 [2048, 8192], P('seq', 'tp'), may hold values from -32 to 32
- shrink_second: float32 [2048, 8192], P('seq', 'tp'), may hold values from 155.648 to 622.592
- conv_kernel: float32 [3, 2048], P(None, ('tp', 'seq')), may hold values from -3 to 3
- conv_first: float32 [3, 2048], P(None, ('tp', 'seq')), may hold values from -128 to 128
- conv_second: float32 [3, 2048], P(None, ('tp', 'seq')), may hold values from 1720.32 to 6881.28
- norm_gains: float32 [2, 2048], P(None, ('tp', 'seq')), may hold values from 0.5 to 1.5
- gain_first: float32 [2, 2048], P(None, ('tp', 'seq')), may hold values from -96 to 96
- gain_second: float32 [2, 2048], P(None, ('tp', 'seq')), may hold values from 983.04 to 3932.16
Outputs:
- mixed: bfloat16 [8192, 2048], P('seq', 'tp')
- tokens_grad: float32 [8192, 2048], P('seq', 'tp')
- entry_next: float32 [2048, 3, 2048], P('seq', None, 'tp')
- entry_first_next: float32 [2048, 3, 2048], P('seq', None, 'tp')
- entry_second_next: float32 [2048, 3, 2048], P('seq', None, 'tp')
- exit_next: float32 [2048, 2048], P('seq', 'tp')
- exit_first_next: float32 [2048, 2048], P('seq', 'tp')
- exit_second_next: float32 [2048, 2048], P('seq', 'tp')
- expand_next: float32 [2048, 2, 8192], P('seq', None, 'tp')
- expand_first_next: float32 [2048, 2, 8192], P('seq', None, 'tp')
- expand_second_next: float32 [2048, 2, 8192], P('seq', None, 'tp')
- shrink_next: float32 [2048, 8192], P('seq', 'tp')
- shrink_first_next: float32 [2048, 8192], P('seq', 'tp')
- shrink_second_next: float32 [2048, 8192], P('seq', 'tp')
- conv_next: float32 [3, 2048], P(None, ('tp', 'seq'))
- conv_first_next: float32 [3, 2048], P(None, ('tp', 'seq'))
- conv_second_next: float32 [3, 2048], P(None, ('tp', 'seq'))
- gains_next: float32 [2, 2048], P(None, ('tp', 'seq'))
- gains_first_next: float32 [2, 2048], P(None, ('tp', 'seq'))
- gains_second_next: float32 [2, 2048], P(None, ('tp', 'seq'))
Inputs may be any that keep to these rules, and one draw needn't show every extreme that they name: bounds[i] is the offset within group i at which a new sequence begins, 1024 where none does; group 0 begins one at offset 0, every other group at an offset of 2 to 1022 or not at all, and some group other than the first holds none.
All inputs are finite; a program needn't handle non-finite values.
Results may differ from a plain program's by a relative error of at most 0.012.
The roundings to bfloat16 on the way count: a program that leaves them out, or rounds other values in their place, can miss the bound.
Values may be sent and summed in bfloat16 or wider, within the bound.
A program may use at most 256 MiB of HBM per device.

v0:
```python
import jax
import jax.numpy as jnp
from jax import lax
from jax.sharding import PartitionSpec as P

D = 2048
STEP = 10


EPSILON = 1e-05
BETA_ONE = 0.9
BETA_TWO = 0.95
ADAM_EPSILON = 1e-08
WEIGHT_DECAY = 0.1
RATE_WIDE = 0.04
RATE_CONV = 0.5
RATE_GAIN = 0.4


def from_behind(block, axis, distance):
    devices = range(lax.axis_size(axis))
    route = [(i - distance, i) for i in devices if i - distance in devices]
    return lax.ppermute(block, axis, route)


def contract_rows(left, right):
    return lax.dot_general(
        left, right, (((0,), (0,)), ((), ())), preferred_element_type=jnp.float32
    )


def contract_cols(left, right):
    return lax.dot_general(
        left, right, (((1,), (1,)), ((), ())), preferred_element_type=jnp.float32
    )


def reduce_branch(term):
    return lax.psum_scatter(term, "tp", scatter_dimension=1, tiled=True)


def gather_rows(rows_low):
    return lax.all_gather(rows_low, "tp", axis=1, tiled=True)


def norm_forward(values, gain_row):
    row_total = lax.psum(jnp.sum(values * values, axis=1, keepdims=True), "tp")
    row_scale = lax.rsqrt(row_total / D + EPSILON)
    own_normed = (values * row_scale * gain_row).astype(jnp.bfloat16)
    return (lax.all_gather(own_normed, "tp", axis=1, tiled=True), row_scale, values, gain_row)


def norm_backward(term, kept_rows, row_scale, kept_gain):
    grad_normed = lax.psum_scatter(term, "tp", scatter_dimension=1, tiled=True)
    inner_sum = lax.psum(jnp.sum(grad_normed * kept_gain * kept_rows, axis=1, keepdims=True), "tp")
    rows_grad = row_scale * kept_gain * grad_normed - kept_rows * row_scale**3 * inner_sum / D
    return (rows_grad, jnp.sum(grad_normed * kept_rows * row_scale, axis=0))


def adam_update(weight, first, second, grad, rate, decay):
    first_next = BETA_ONE * first + (1.0 - BETA_ONE) * grad
    second_next = BETA_TWO * second + (1.0 - BETA_TWO) * grad * grad
    corrected = first_next / (1.0 - BETA_ONE**STEP)
    spread = jnp.sqrt(second_next / (1.0 - BETA_TWO**STEP)) + ADAM_EPSILON
    return (weight - rate * (corrected / spread + decay * weight), first_next, second_next)


def shards(
    tokens,
    bounds,
    cotangent,
    entry_weight,
    entry_first,
    entry_second,
    exit_weight,
    exit_first,
    exit_second,
    expand_weight,
    expand_first,
    expand_second,
    shrink_weight,
    shrink_first,
    shrink_second,
    conv_kernel,
    conv_first,
    conv_second,
    norm_gains,
    gain_first,
    gain_second,
):
    low_weights = (
        entry_weight.astype(jnp.bfloat16),
        exit_weight.astype(jnp.bfloat16),
        expand_weight.astype(jnp.bfloat16),
        shrink_weight.astype(jnp.bfloat16),
        conv_kernel.astype(jnp.bfloat16),
        norm_gains.astype(jnp.bfloat16),
    )
    entry_full, exit_full, expand_full, shrink_full, kernel_low, gains_low = (
        lax.all_gather(low_weights[0], "seq", axis=0, tiled=True),
        lax.all_gather(low_weights[1], "seq", axis=0, tiled=True),
        lax.all_gather(low_weights[2], "seq", axis=0, tiled=True),
        lax.all_gather(low_weights[3], "seq", axis=0, tiled=True),
        lax.all_gather(low_weights[4], "seq", axis=1, tiled=True),
        lax.all_gather(low_weights[5], "seq", axis=1, tiled=True),
    )
    kernel = kernel_low.astype(jnp.float32)
    gains_row = gains_low.astype(jnp.float32)
    rows_dev = tokens.shape[0]
    channels = tokens.shape[1]
    width_full = entry_full.shape[0]
    hidden = shrink_full.shape[1]
    position = jnp.arange(rows_dev, dtype=jnp.int32)[:, None]
    boundary = bounds[0]
    see_one = (position != boundary).astype(jnp.float32)
    see_two = see_one * (position - 1 != boundary).astype(jnp.float32)
    tokens_f = tokens.astype(jnp.float32)
    normed_one, scale_one, kept_one, gain_one = norm_forward(tokens_f, gains_row[0])
    projected = jnp.dot(
        normed_one, entry_full.reshape(width_full, 3 * channels), preferred_element_type=jnp.float32
    ).reshape(rows_dev, 3, channels)
    input_gate = projected[:, 0]
    output_gate = projected[:, 1]
    values_rows = projected[:, 2]
    gated_rows = (input_gate * values_rows).astype(jnp.bfloat16)
    previous = from_behind(gated_rows[-2:], "seq", 1)
    extended = jnp.concatenate([previous, gated_rows], axis=0).astype(jnp.float32)
    conv_out = (
        kernel[2] * extended[2:]
        + kernel[1] * extended[1:-1] * see_one
        + kernel[0] * extended[:-2] * see_two
    )
    mixer_rows = (output_gate * conv_out).astype(jnp.bfloat16)
    residual = tokens_f + reduce_branch(contract_cols(mixer_rows, exit_full))
    normed_two, scale_two, kept_two, gain_two = norm_forward(residual, gains_row[1])
    expanded = jnp.dot(
        normed_two, expand_full.reshape(width_full, 2 * hidden), preferred_element_type=jnp.float32
    ).reshape(rows_dev, 2, hidden)
    gate_rows = expanded[:, 0]
    up_rows = expanded[:, 1]
    sigmoid_gate = jax.nn.sigmoid(gate_rows)
    silu_gate = gate_rows * sigmoid_gate
    activation = (silu_gate * up_rows).astype(jnp.bfloat16)
    mixed = (residual + reduce_branch(contract_cols(activation, shrink_full))).astype(jnp.bfloat16)
    cot_full = gather_rows(cotangent)
    shrink_grad = contract_rows(cot_full, activation)
    act_grad = jnp.dot(cot_full, shrink_full, preferred_element_type=jnp.float32)
    gate_grad = (
        act_grad * up_rows * sigmoid_gate * (1.0 + gate_rows * (1.0 - sigmoid_gate))
    ).astype(jnp.bfloat16)
    up_grad = (act_grad * silu_gate).astype(jnp.bfloat16)
    gate_weight_grad = contract_rows(normed_two, gate_grad)
    up_weight_grad = contract_rows(normed_two, up_grad)
    expanded_grad = jnp.stack([gate_grad, up_grad], axis=1).reshape(rows_dev, 2 * hidden)
    two_term = contract_cols(expanded_grad, expand_full.reshape(width_full, 2 * hidden))
    feed_done = (gate_weight_grad, up_weight_grad, shrink_grad)
    residual_norm_grad, gain_two_grad = norm_backward(two_term, kept_two, scale_two, gain_two)
    residual_grad = cotangent.astype(jnp.float32) + residual_norm_grad
    branch_full = gather_rows(residual_grad.astype(jnp.bfloat16))
    exit_grad = contract_rows(branch_full, mixer_rows)
    mixer_grad = jnp.dot(branch_full, exit_full, preferred_element_type=jnp.float32)
    out_gate_grad = (mixer_grad * conv_out).astype(jnp.bfloat16)
    conv_grad = mixer_grad * output_gate
    lag_zero = conv_grad * kernel[2]
    lag_one = conv_grad * see_one * kernel[1]
    lag_two = conv_grad * see_two * kernel[0]
    padded_grad = (
        jnp.pad(lag_zero, ((2, 0), (0, 0)))
        + jnp.pad(lag_one, ((1, 1), (0, 0)))
        + jnp.pad(lag_two, ((0, 2), (0, 0)))
    )
    returned = from_behind(padded_grad[:2], "seq", -1)
    gated_grad = padded_grad[2:] + jnp.pad(returned, ((rows_dev - 2, 0), (0, 0)))
    kernel_grad = jnp.stack(
        [
            jnp.sum(conv_grad * see_two * extended[:-2], axis=0),
            jnp.sum(conv_grad * see_one * extended[1:-1], axis=0),
            jnp.sum(conv_grad * extended[2:], axis=0),
        ]
    )
    in_gate_grad = (gated_grad * values_rows).astype(jnp.bfloat16)
    values_grad = (gated_grad * input_gate).astype(jnp.bfloat16)
    projected_grad = jnp.stack([in_gate_grad, out_gate_grad, values_grad], axis=1).reshape(
        rows_dev, 3 * channels
    )
    entry_grad = contract_rows(normed_one, projected_grad).reshape(width_full, 3, channels)
    one_term = contract_cols(projected_grad, entry_full.reshape(width_full, 3 * channels))
    tokens_norm_grad, gain_one_grad = norm_backward(one_term, kept_one, scale_one, gain_one)
    tokens_grad = residual_grad + tokens_norm_grad
    gains_grad = jnp.stack([gain_one_grad, gain_two_grad])
    entry_part, exit_part, gate_part, up_part, shrink_part, kernel_part, gains_part = (
        lax.psum_scatter(entry_grad, "seq", scatter_dimension=0, tiled=True),
        lax.psum_scatter(exit_grad, "seq", scatter_dimension=0, tiled=True),
        lax.psum_scatter(feed_done[0], "seq", scatter_dimension=0, tiled=True),
        lax.psum_scatter(feed_done[1], "seq", scatter_dimension=0, tiled=True),
        lax.psum_scatter(feed_done[2], "seq", scatter_dimension=0, tiled=True),
        lax.psum_scatter(kernel_grad, "seq", scatter_dimension=1, tiled=True),
        lax.psum_scatter(gains_grad, "seq", scatter_dimension=1, tiled=True),
    )
    expand_part = jnp.stack([gate_part, up_part], axis=1)
    entry_next, entry_first_next, entry_second_next = adam_update(
        entry_weight, entry_first, entry_second, entry_part, RATE_WIDE, WEIGHT_DECAY
    )
    exit_next, exit_first_next, exit_second_next = adam_update(
        exit_weight, exit_first, exit_second, exit_part, RATE_WIDE, WEIGHT_DECAY
    )
    expand_next, expand_first_next, expand_second_next = adam_update(
        expand_weight, expand_first, expand_second, expand_part, RATE_WIDE, WEIGHT_DECAY
    )
    shrink_next, shrink_first_next, shrink_second_next = adam_update(
        shrink_weight, shrink_first, shrink_second, shrink_part, RATE_WIDE, WEIGHT_DECAY
    )
    conv_next, conv_first_next, conv_second_next = adam_update(
        conv_kernel, conv_first, conv_second, kernel_part, RATE_CONV, 0.0
    )
    gains_next, gains_first_next, gains_second_next = adam_update(
        norm_gains, gain_first, gain_second, gains_part, RATE_GAIN, 0.0
    )
    return (
        mixed,
        tokens_grad,
        entry_next,
        entry_first_next,
        entry_second_next,
        exit_next,
        exit_first_next,
        exit_second_next,
        expand_next,
        expand_first_next,
        expand_second_next,
        shrink_next,
        shrink_first_next,
        shrink_second_next,
        conv_next,
        conv_first_next,
        conv_second_next,
        gains_next,
        gains_first_next,
        gains_second_next,
    )


def solution(mesh):
    placed = (
        P("seq", "tp"),
        P("seq"),
        P("seq", "tp"),
        P("seq", None, "tp"),
        P("seq", None, "tp"),
        P("seq", None, "tp"),
        P("seq", "tp"),
        P("seq", "tp"),
        P("seq", "tp"),
        P("seq", None, "tp"),
        P("seq", None, "tp"),
        P("seq", None, "tp"),
        P("seq", "tp"),
        P("seq", "tp"),
        P("seq", "tp"),
        P(None, ("tp", "seq")),
        P(None, ("tp", "seq")),
        P(None, ("tp", "seq")),
        P(None, ("tp", "seq")),
        P(None, ("tp", "seq")),
        P(None, ("tp", "seq")),
    )
    return jax.shard_map(
        shards,
        mesh=mesh,
        in_specs=placed,
        out_specs=(
            P("seq", "tp"),
            P("seq", "tp"),
            P("seq", None, "tp"),
            P("seq", None, "tp"),
            P("seq", None, "tp"),
            P("seq", "tp"),
            P("seq", "tp"),
            P("seq", "tp"),
            P("seq", None, "tp"),
            P("seq", None, "tp"),
            P("seq", None, "tp"),
            P("seq", "tp"),
            P("seq", "tp"),
            P("seq", "tp"),
            P(None, ("tp", "seq")),
            P(None, ("tp", "seq")),
            P(None, ("tp", "seq")),
            P(None, ("tp", "seq")),
            P(None, ("tp", "seq")),
            P(None, ("tp", "seq")),
        ),
        check_vma=False,
    )
```

profile of v0, /device:TPU:0, one launch (start us, length us, event | category | flops | bytes accessed | tf_op | source)
XLA Modules:
  0.0 2333.4 jit_solution(6993400223803696758)
XLA Ops:
  9.8 22.3 all-gather
  42.0 16.3 all-gather.1
  59.2 53.4 %all-gather.13.cloned.1.call-done = bf16[2048,3,512]{2,0,1:T(8,128)(2,1)} async-done(((bf16[256,3,512]{2,0,1:T(8,128)(2,1)}), bf16[2048,3,512]{2,0,1:T(8,128)(2,1)}) %all-gather.13.cloned.1.call-update) | async-done | bytes 6291472 | tf_op jit(solution)/shard_map/all_gather | solution.py:100
  121.5 25.9 %all-gather.11.cloned.1.call-done = bf16[1024,2048]{1,0:T(8,128)(2,1)} async-done(((bf16[1024,512]{1,0:T(8,128)(2,1)}), bf16[1024,2048]{1,0:T(8,128)(2,1)}) %all-gather.11.cloned.1.call-update) | async-done | bytes 4194320 | tf_op jit(solution)/shard_map/all_gather | solution.py:50
  147.5 10.2 fusion.7
  166.6 32.9 %all-gather.15.cloned.1.call-done = bf16[2048,512]{1,0:T(8,128)(2,1)} async-done(((bf16[256,512]{1,0:T(8,128)(2,1)}), bf16[2048,512]{1,0:T(8,128)(2,1)}) %all-gather.15.cloned.1.call-update) | async-done | bytes 2097168 | tf_op jit(solution)/shard_map/all_gather | solution.py:101
  212.7 64.5 %reduce-scatter.16.cloned.1.call-done = f32[1024,512]{1,0:T(8,128)} async-done(((f32[1024,2048]{1,0:T(8,128)}), f32[1024,512]{1,0:T(8,128)}) %reduce-scatter.16.cloned.1.call-update) | async-done | bytes 2097168 | tf_op jit(solution)/shard_map/reduce_scatter | solution.py:39
  291.5 216.1 %all-gather.19.cloned.1.call-done = bf16[2048,2,2048]{2,0,1:T(8,128)(2,1)} async-done(((bf16[256,2,2048]{2,0,1:T(8,128)(2,1)}), bf16[2048,2,2048]{2,0,1:T(8,128)(2,1)}) %all-gather.19.cloned.1.call-update) | async-done | bytes 16777232 | tf_op jit(solution)/shard_map/all_gather | solution.py:102
  507.7 22.6 copy.103
  530.2 12.2 all-gather.17.cloned.1.call-done
  542.4 23.7 %fusion = f32[1024,2,2048]{2,0,1:T(8,128)} fusion(bf16[2048,2,2048]{0,2,1:T(8,128)(2,1)} %copy.103, bf16[1024,2048]{1,0:T(8,128)(2,1)} %all-gather.17.cloned.1.call-done), kind=kOutput, calls=%fused_computation | convolution fusion | flops 17179869184 | bytes 37748736 | tf_op jit(solution)/shard_map/dot_general | solution.py:136
  566.1 12.5 all-gather.23.cloned.1.call-done
  578.6 127.9 %all-gather.21.cloned.1.call-done = bf16[2048,2048]{1,0:T(8,128)(2,1)} async-done(((bf16[256,2048]{1,0:T(8,128)(2,1)}), bf16[2048,2048]{1,0:T(8,128)(2,1)}) %all-gather.21.cloned.1.call-update) | async-done | bytes 8388624 | tf_op jit(solution)/shard_map/all_gather | solution.py:103
  706.5 20.9 multiply_convert_fusion.1
  729.5 23.4 %fusion.9 = f32[1024,2048]{1,0:T(8,128)} fusion(bf16[2048,2,2048]{2,0,1:T(8,128)(2,1)} %all-gather.19.cloned.1.call-done, bf16[1024,1,2048]{2,0,1:T(8,128)(2,1)S(1)} %bitcast.179, bf16[1024,1,2048]{2,0,1:T(8,128)(2,1)} %bitcast.180), kind=kOutput, calls=%fused_computation.23 | convolution fusion | flops 17184063488 | bytes 33554432 | tf_op jit(solution)/shard_map/dot_general | solution.py:33
  753.0 14.6 fusion.53
  767.7 55.3 %reduce-scatter.20.cloned.1.call-done = f32[1024,512]{1,0:T(8,128)} async-done(((f32[1024,2048]{1,0:T(8,128)}), f32[1024,512]{1,0:T(8,128)}) %reduce-scatter.20.cloned.1.call-update) | async-done | bytes 2097168 | tf_op jit(solution)/shard_map/reduce_scatter | solution.py:54
  831.0 66.2 %reduce-scatter.18.cloned.1.call-done = f32[1024,512]{1,0:T(8,128)} async-done(((f32[1024,2048]{1,0:T(8,128)}), f32[1024,512]{1,0:T(8,128)}) %reduce-scatter.18.cloned.1.call-update) | async-done | bytes 2097168 | tf_op jit(solution)/shard_map/reduce_scatter | solution.py:39
  901.3 34.5 %all-gather.25.cloned.1.call-done = bf16[1024,2048]{1,0:T(8,128)(2,1)} async-done(((bf16[1024,512]{1,0:T(8,128)(2,1)}), bf16[1024,2048]{1,0:T(8,128)(2,1)}) %all-gather.25.cloned.1.call-update) | async-done | bytes 4194320 | tf_op jit(solution)/shard_map/all_gather | solution.py:43
  968.1 16.9 fusion.56
  985.3 15.4 fusion.57
  1000.8 15.3 convolution_bitcast_fusion
  1022.9 9.1 reduce-scatter.22.cloned.1.call-done
  1035.8 12.6 fusion.14
  1056.2 41.0 %reduce-scatter.34.cloned.1.call-done = f32[64,3]{1,0:T(8,128)} async-done(((f32[512,3]{1,0:T(8,128)}), f32[64,3]{1,0:T(8,128)}) %reduce-scatter.34.cloned.1.call-update) | async-done | bytes 784
  1098.6 89.5 %reduce-scatter.26.cloned.1.call-done = f32[256,512]{1,0:T(8,128)} async-done(((f32[2048,512]{1,0:T(8,128)}), f32[256,512]{1,0:T(8,128)}) %reduce-scatter.26.cloned.1.call-update) | async-done | bytes 524304 | tf_op jit(solution)/shard_map/reduce_scatter | solution.py:193
  1191.1 283.9 %reduce-scatter.28.cloned.1.call-done = f32[256,2048]{1,0:T(8,128)} async-done(((f32[2048,2048]{1,0:T(8,128)}), f32[256,2048]{1,0:T(8,128)}) %reduce-scatter.28.cloned.1.call-update) | async-done | bytes 2097168 | tf_op jit(solution)/shard_map/reduce_scatter | solution.py:194
  1474.9 285.5 %reduce-scatter.30.cloned.1.call-done = f32[256,2048]{1,0:T(8,128)} async-done(((f32[2048,2048]{1,0:T(8,128)}), f32[256,2048]{1,0:T(8,128)}) %reduce-scatter.30.cloned.1.call-update) | async-done | bytes 2097168 | tf_op jit(solution)/shard_map/reduce_scatter | solution.py:195
  1760.5 13.9 multiply_subtract_fusion
  1790.1 256.3 %reduce-scatter.32.cloned.1.call-done = f32[256,2048]{0,1:T(8,128)} async-done(((f32[2048,2048]{0,1:T(8,128)}), f32[256,2048]{0,1:T(8,128)}) %reduce-scatter.32.cloned.1.call-update) | async-done | bytes 2097168 | tf_op jit(solution)/shard_map/reduce_scatter | solution.py:196
  2071.4 39.0 %reduce-scatter.36.cloned.1.call-done = f32[64,2]{1,0:T(8,128)} async-done(((f32[512,2]{1,0:T(8,128)}), f32[64,2]{1,0:T(8,128)}) %reduce-scatter.36.cloned.1.call-update) | async-done | bytes 528
  2111.9 208.9 %reduce-scatter.24.cloned.1.call-done = f32[256,3,512]{2,0,1:T(8,128)} async-done(((f32[2048,3,512]{2,0,1:T(8,128)}), f32[256,3,512]{2,0,1:T(8,128)}) %reduce-scatter.24.cloned.1.call-update) | async-done | bytes 1572880 | tf_op jit(solution)/shard_map/reduce_scatter | solution.py:192
  (200 shorter events, 174.9 us)
Async XLA Ops:
  7.2 105.4 %all-gather.13.cloned.1.call-start = ((), (), s32[]{:S(2)}) async-start(), calls=%async_computation.12 | async-start | bytes 7077888 | tf_op jit(solution)/shard_map/all_gather | solution.py:100
  9.8 137.7 %all-gather.11.cloned.1.call-start = ((), (), s32[]{:S(2)}) async-start(), calls=%async_computation.11 | async-start | bytes 5242880 | tf_op jit(solution)/shard_map/all_gather | solution.py:50
  38.6 246.9 %copy-start.21 = (f32[1,512]{1,0:T(1,128)}, f32[1,512]{1,0:T(1,128)S(1)}, u32[]{:S(2)}) copy-start(f32[1,512]{1,0:T(1,128)S(1)} %get-tuple-element.149) | copy-start | bytes 6148
  41.1 158.4 %all-gather.15.cloned.1.call-start = ((), (), s32[]{:S(2)}) async-start(), calls=%async_computation.13 | async-start | bytes 2359296 | tf_op jit(solution)/shard_map/all_gather | solution.py:101
  42.0 235.2 %reduce-scatter.16.cloned.1.call-start = ((), (), s32[]{:S(2)}) async-start(), calls=%async_computation.14 | async-start | bytes 10485760 | tf_op jit(solution)/shard_map/reduce_scatter | solution.py:39
  59.1 104.0 %copy-start.13 = (f32[1024]{0:T(1024)}, f32[1024]{0:T(1024)S(1)}, u32[]{:S(2)}) copy-start(f32[1024]{0:T(1024)S(1)} %fusion.36) | copy-start | bytes 12292
  59.1 104.0 %copy-start.25 = (f32[1,512]{1,0:T(1,128)}, f32[1,512]{1,0:T(1,128)S(1)}, u32[]{:S(2)}) copy-start(f32[1,512]{1,0:T(1,128)S(1)} %get-tuple-element.146) | copy-start | bytes 6148
  59.2 104.0 %copy-start.27 = (f32[1,512]{1,0:T(1,128)}, f32[1,512]{1,0:T(1,128)S(1)}, u32[]{:S(2)}) copy-start(f32[1,512]{1,0:T(1,128)S(1)} %get-tuple-element.147) | copy-start | bytes 6148
  59.2 104.0 %copy-start.29 = (f32[1,512]{1,0:T(1,128)}, f32[1,512]{1,0:T(1,128)S(1)}, u32[]{:S(2)}) copy-start(f32[1,512]{1,0:T(1,128)S(1)} %get-tuple-element.148) | copy-start | bytes 6148
  158.1 4.7 collective-permute-start
  206.8 300.9 %all-gather.19.cloned.1.call-start = ((), (), s32[]{:S(2)}) async-start(), calls=%async_computation.16 | async-start | bytes 18874368 | tf_op jit(solution)/shard_map/all_gather | solution.py:102
  212.6 329.8 %all-gather.17.cloned.1.call-start = ((), (), s32[]{:S(2)}) async-start(), calls=%async_computation.15 | async-start | bytes 5242880 | tf_op jit(solution)/shard_map/all_gather | solution.py:50
  287.3 291.2 %all-gather.23.cloned.1.call-start = ((), (), s32[]{:S(2)}) async-start(), calls=%async_computation.19 | async-start | bytes 5242880 | tf_op jit(solution)/shard_map/all_gather | solution.py:43
  288.1 418.4 %all-gather.21.cloned.1.call-start = ((), (), s32[]{:S(2)}) async-start(), calls=%async_computation.17 | async-start | bytes 9437184 | tf_op jit(solution)/shard_map/all_gather | solution.py:103
  291.3 531.7 %reduce-scatter.20.cloned.1.call-start = ((), (), s32[]{:S(2)}) async-start(), calls=%async_computation.20 | async-start | bytes 10485760 | tf_op jit(solution)/shard_map/reduce_scatter | solution.py:54
  752.9 144.3 %reduce-scatter.18.cloned.1.call-start = ((), (), s32[]{:S(2)}) async-start(), calls=%async_computation.18 | async-start | bytes 10485760 | tf_op jit(solution)/shard_map/reduce_scatter | solution.py:39
  767.6 55.4 %copy-start.3 = (f32[1024,512]{1,0:T(8,128)S(1)}, f32[1024,512]{1,0:T(8,128)}, u32[]{:S(2)}) copy-start(f32[1024,512]{1,0:T(8,128)} %copy-done.2) | copy-start | bytes 6291460
  767.6 55.4 %copy-start.18 = (f32[1024,1]{0,1:T(1,128)S(1)}, f32[1024,1]{0,1:T(1,128)}, u32[]{:S(2)}) copy-start(f32[1024,1]{0,1:T(1,128)} %copy-done.17) | copy-start | bytes 12292
  767.6 55.4 %copy-start.22 = (f32[1,512]{1,0:T(1,128)S(1)}, f32[1,512]{1,0:T(1,128)}, u32[]{:S(2)}) copy-start(f32[1,512]{1,0:T(1,128)} %copy-done.21) | copy-start | bytes 6148
  767.6 129.6 %copy-start.10 = (bf16[1024,512]{1,0:T(8,128)(2,1)S(1)}, bf16[1024,512]{1,0:T(8,128)(2,1)}, u32[]{:S(2)}) copy-start(bf16[1024,512]{1,0:T(8,128)(2,1)} %param.23) | copy-start | bytes 3145732
  767.6 129.5 %copy-start.31 = (f32[1024,1]{0,1:T(1,128)S(1)}, f32[1024,1]{0,1:T(1,128)}, u32[]{:S(2)}) copy-start(f32[1024,1]{0,1:T(1,128)} %get-tuple-element.130) | copy-start | bytes 12292
  767.7 168.2 %all-gather.25.cloned.1.call-start = ((), (), s32[]{:S(2)}) async-start(), calls=%async_computation.21 | async-start | bytes 5242880 | tf_op jit(solution)/shard_map/all_gather | solution.py:43
  901.3 130.8 %reduce-scatter.22.cloned.1.call-start = ((), (), s32[]{:S(2)}) async-start(), calls=%async_computation.22 | async-start | bytes 10485760 | tf_op jit(solution)/shard_map/reduce_scatter | solution.py:54
  944.3 5.9 collective-permute-start.1
  960.2 137.0 %reduce-scatter.34.cloned.1.call-start = ((), (), s32[]{:S(2)}) async-start(), calls=%async_computation.28 | async-start | bytes 294912
  961.1 227.0 %reduce-scatter.26.cloned.1.call-start = ((), (), s32[]{:S(2)}) async-start(), calls=%async_computation.24 | async-start | bytes 4718592 | tf_op jit(solution)/shard_map/reduce_scatter | solution.py:193
  968.1 506.9 %reduce-scatter.28.cloned.1.call-start = ((), (), s32[]{:S(2)}) async-start(), calls=%async_computation.25 | async-start | bytes 18874368 | tf_op jit(solution)/shard_map/reduce_scatter | solution.py:194
  985.1 775.4 %reduce-scatter.30.cloned.1.call-start = ((), (), s32[]{:S(2)}) async-start(), calls=%async_computation.26 | async-start | bytes 18874368 | tf_op jit(solution)/shard_map/reduce_scatter | solution.py:195
  1000.7 1045.7 %reduce-scatter.32.cloned.1.call-start = ((), (), s32[]{:S(2)}) async-start(), calls=%async_computation.27 | async-start | bytes 18874368 | tf_op jit(solution)/shard_map/reduce_scatter | solution.py:196
  1016.1 1094.3 %reduce-scatter.36.cloned.1.call-start = ((), (), s32[]{:S(2)}) async-start(), calls=%async_computation.29 | async-start | bytes 294912
  1035.4 1285.4 %reduce-scatter.24.cloned.1.call-start = ((), (), s32[]{:S(2)}) async-start(), calls=%async_computation.23 | async-start | bytes 14155776 | tf_op jit(solution)/shard_map/reduce_scatter | solution.py:192
  1053.3 44.7 %copy-start.36 = (f32[3,64]{1,0:T(4,128)S(1)}, f32[3,64]{1,0:T(4,128)}, u32[]{:S(2)}) copy-start(f32[3,64]{1,0:T(4,128)} %param.38) | copy-start | bytes 2308
  (35 other events, 544.7 us)
Sparse Core Ops, SparseCore 0:
  10.8 101.7 all-gather.12
  114.8 32.6 all-gather.10
  150.2 49.2 all-gather.14
  206.9 70.2 reduce-scatter.15
  280.0 227.5 all-gather.18
  509.7 32.6 all-gather.16
  544.1 34.4 all-gather.22
  581.5 124.9 all-gather.20
  753.0 69.9 reduce-scatter.19
  825.4 71.7 reduce-scatter.17
  901.3 34.4 all-gather.24
  960.3 71.6 reduce-scatter.21
  1035.9 61.2 reduce-scatter.33
  1101.2 86.8 reduce-scatter.25
  1192.3 282.6 reduce-scatter.27
  1478.6 281.8 reduce-scatter.29
  1764.6 281.7 reduce-scatter.31
  2050.1 60.2 reduce-scatter.35
  2114.1 206.6 reduce-scatter.23
where the time goes:
time: 2340 us; the launch traced here: 2330 us
  waiting for transfers between devices  1920 us (82%)
  matrix products  182 us (8%)
  local copies, waits for them, and re-layouts  81.6 us (3%)
  other arithmetic  64.6 us (3%)
  blocking collectives  63.1 us (3%)
    reduce_scatter x1, waiting for transfers between devices, shards(): lax.psum_scatter(feed_done[1], 'seq', scatter_dimension=0, tiled=True)  286 us
    reduce_scatter x1, waiting for transfers between devices, shards(): lax.psum_scatter(feed_done[0], 'seq', scatter_dimension=0, tiled=True)  284 us
    reduce_scatter x1, waiting for transfers between devices, shards(): lax.psum_scatter(feed_done[2], 'seq', scatter_dimension=0, tiled=True)  256 us
    all_gather x1, waiting for transfers between devices, shards(): lax.all_gather(low_weights[2], 'seq', axis=0, tiled=True)  216 us
    reduce_scatter x1, waiting for transfers between devices, shards(): lax.psum_scatter(entry_grad, 'seq', scatter_dimension=0, tiled=True)  209 us
    reduce_scatter x2, waiting for transfers between devices, reduce_branch(): return lax.psum_scatter(term, 'tp', scatter_dimension=1, tiled=True)  131 us
    all_gather x1, waiting for transfers between devices, shards(): lax.all_gather(low_weights[3], 'seq', axis=0, tiled=True)  128 us
    reduce_scatter x1, waiting for transfers between devices, shards(): lax.psum_scatter(exit_grad, 'seq', scatter_dimension=0, tiled=True)  89.5 us
  transfers between devices with their start and end apart: 21, of which 21 were waited for; matrix products, arithmetic and copies ran while one was open for 10% of the time, Pallas kernels for 0%

commit v1 on v0

v1 whole, which is shorter than its diff:
```python
import functools

import jax
import jax.numpy as jnp
from jax import lax
from jax.experimental import pallas as pl
from jax.experimental.pallas import tpu as pltpu
from jax.sharding import PartitionSpec as P

D = 2048
STEP = 10


EPSILON = 1e-05
BETA_ONE = 0.9
BETA_TWO = 0.95
ADAM_EPSILON = 1e-08
WEIGHT_DECAY = 0.1
RATE_WIDE = 0.04
RATE_CONV = 0.5
RATE_GAIN = 0.4

MESH = pl.DeviceIdType.MESH
LOW = jnp.bfloat16
VMEM_BYTES = 60 * 1024 * 1024


def ring_place(index, count):
    side = index % 2
    level = index // 2
    return level * (1 - side) + (count - 1 - level) * side


def ring_index(place, count):
    back = place // (count // 2)
    return (1 - back) * (2 * place) + back * (2 * (count - 1 - place) + 1)


def ring_ends(count):
    place = ring_place(lax.axis_index("seq"), count)
    ahead = ring_index((place + 1) % count, count)
    behind = ring_index((place + count - 1) % count, count)
    return place, ahead, behind


def greet(ahead, behind, column):
    barrier = pltpu.get_barrier_semaphore()
    for other in (ahead, behind):
        pl.semaphore_signal(barrier, inc=1, device_id=(other, column), device_id_type=MESH)
    pl.semaphore_wait(barrier, 2)


def gather_kernel(count, arrays, *refs):
    shard_refs = refs[:arrays]
    full_refs = refs[arrays : 2 * arrays]
    send_sem, recv_sem, own_sem = refs[2 * arrays :]
    column = lax.axis_index("tp")
    place, ahead, behind = ring_ends(count)
    greet(ahead, behind, column)

    def copy(array, step, way):
        owner = ring_index((place + count - step) % count if way == 0 else (place + step) % count, count)
        half = shard_refs[array].shape[0] // 2
        part = pl.ds(way * half, half)
        return pltpu.make_async_remote_copy(
            src_ref=full_refs[array].at[owner, part],
            dst_ref=full_refs[array].at[owner, part],
            send_sem=send_sem.at[array, way, step],
            recv_sem=recv_sem.at[array, way, step],
            device_id=(ahead if way == 0 else behind, column),
            device_id_type=MESH,
        )

    def first(array, way):
        half = shard_refs[array].shape[0] // 2
        part = pl.ds(way * half, half)
        return pltpu.make_async_remote_copy(
            src_ref=shard_refs[array].at[part],
            dst_ref=full_refs[array].at[lax.axis_index("seq"), part],
            send_sem=send_sem.at[array, way, 0],
            recv_sem=recv_sem.at[array, way, 0],
            device_id=(ahead if way == 0 else behind, column),
            device_id_type=MESH,
        )

    def own(array):
        return pltpu.make_async_copy(
            shard_refs[array], full_refs[array].at[lax.axis_index("seq")], own_sem.at[array]
        )

    for array in range(arrays):
        for way in range(2):
            first(array, way).start()
    for array in range(arrays):
        own(array).start()

    def hop(step, carry):
        for array in range(arrays):
            for way in range(2):
                copy(array, step - 1, way).wait_recv()
                copy(array, step, way).start()
        return carry

    lax.fori_loop(1, count - 1, hop, 0)
    for array in range(arrays):
        for way in range(2):
            copy(array, count - 2, way).wait_recv()

    def sent(step, carry):
        for array in range(arrays):
            for way in range(2):
                copy(array, step, way).wait_send()
        return carry

    lax.fori_loop(0, count - 1, sent, 0)
    for array in range(arrays):
        own(array).wait()


def ring_gather(shards, collective):
    count = lax.axis_size("seq")
    arrays = len(shards)
    moved = sum(shard.size for shard in shards) * 2 * count
    fulls = pl.pallas_call(
        functools.partial(gather_kernel, count, arrays),
        out_shape=[jax.ShapeDtypeStruct((count,) + shard.shape, shard.dtype) for shard in shards],
        in_specs=[pl.BlockSpec(memory_space=pl.ANY)] * arrays,
        out_specs=[pl.BlockSpec(memory_space=pl.ANY)] * arrays,
        scratch_shapes=[
            pltpu.SemaphoreType.DMA((arrays, 2, count - 1)),
            pltpu.SemaphoreType.DMA((arrays, 2, count - 1)),
            pltpu.SemaphoreType.DMA((arrays,)),
        ],
        compiler_params=pltpu.CompilerParams(
            collective_id=collective, has_side_effects=True, vmem_limit_bytes=VMEM_BYTES
        ),
        cost_estimate=pl.CostEstimate(flops=0, bytes_accessed=30 * moved, transcendentals=0),
        name="ring_gather",
    )(*shards)
    return [full.reshape(count * full.shape[1], full.shape[2]) for full in fulls]


def chunks_of(width):
    return 2 if width % 256 == 0 and width > 256 else 1


def scatter_kernel(count, arrays, *refs):
    left_refs = refs[:arrays]
    right_refs = refs[arrays : 2 * arrays]
    out_refs = refs[2 * arrays : 3 * arrays]
    scratch = refs[3 * arrays :]
    lefts = scratch[:arrays]
    rights = scratch[arrays : 2 * arrays]
    slots = scratch[2 * arrays : 3 * arrays]
    finals = scratch[3 * arrays : 4 * arrays]
    send_sem, recv_sem, load_sem, done_sem = scratch[4 * arrays :]
    column = lax.axis_index("tp")
    place, ahead, behind = ring_ends(count)
    loads = []
    for array in range(arrays):
        loads.append(pltpu.make_async_copy(left_refs[array], lefts[array], load_sem.at[array, 0]))
        loads.append(pltpu.make_async_copy(right_refs[array], rights[array], load_sem.at[array, 1]))
    for load in loads:
        load.start()
    greet(ahead, behind, column)

    def pieces(array):
        half = rights[array].shape[1] // 2
        parts = chunks_of(half)
        width = half // parts
        return [(way, part, way * half + part * width, part * width, width) for part in range(parts) for way in range(2)]

    def term(array, step, way, start, width):
        owner = ring_index((place + 2 * count - 1 - step) % count if way == 0 else (place + 1 + step) % count, count)
        rows = finals[array].shape[0]
        left = lefts[array][pl.ds(pl.multiple_of(owner * rows, 16), rows), :]
        return jnp.dot(left, rights[array][:, start : start + width], preferred_element_type=jnp.float32)

    def copy(array, step, way, part, inner, width):
        held = slots[array].at[way, step, :, pl.ds(inner, width)]
        return pltpu.make_async_remote_copy(
            src_ref=held,
            dst_ref=slots[array].at[way, step + 1, :, pl.ds(inner, width)],
            send_sem=send_sem.at[array, way, part, step],
            recv_sem=recv_sem.at[array, way, part, step],
            device_id=(ahead if way == 0 else behind, column),
            device_id_type=MESH,
        )

    for array in range(arrays):
        loads[2 * array].wait()
        loads[2 * array + 1].wait()
        for way, part, start, inner, width in pieces(array):
            slots[array][way, 0, :, inner : inner + width] = term(array, 0, way, start, width).astype(LOW)
            copy(array, 0, way, part, inner, width).start()

    def hop(step, carry):
        for array in range(arrays):
            for way, part, start, inner, width in pieces(array):
                mine = term(array, step, way, start, width)
                copy(array, step - 1, way, part, inner, width).wait_recv()
                held = slots[array].at[way, step, :, pl.ds(inner, width)]
                held[...] = (held[...].astype(jnp.float32) + mine).astype(LOW)
                copy(array, step, way, part, inner, width).start()
        return carry

    lax.fori_loop(1, count - 1, hop, 0)
    stores = []
    for array in range(arrays):
        for way, part, start, inner, width in pieces(array):
            mine = term(array, count - 1, way, start, width)
            copy(array, count - 2, way, part, inner, width).wait_recv()
            held = slots[array][way, count - 1, :, inner : inner + width]
            finals[array][:, start : start + width] = held.astype(jnp.float32) + mine
        store = pltpu.make_async_copy(finals[array], out_refs[array], done_sem.at[array])
        store.start()
        stores.append(store)

    def sent(step, carry):
        for array in range(arrays):
            for way, part, start, inner, width in pieces(array):
                copy(array, step, way, part, inner, width).wait_send()
        return carry

    lax.fori_loop(0, count - 1, sent, 0)
    for store in stores:
        store.wait()


def ring_scatter(pairs, collective):
    count = lax.axis_size("seq")
    arrays = len(pairs)
    lefts = [left for left, right in pairs]
    rights = [right for left, right in pairs]
    rows = [left.shape[0] // count for left in lefts]
    widths = [right.shape[1] for right in rights]
    moved = sum(left.shape[0] * width * 2 for left, width in zip(lefts, widths))
    flops = sum(2 * left.shape[0] * left.shape[1] * width for left, width in zip(lefts, widths))
    return pl.pallas_call(
        functools.partial(scatter_kernel, count, arrays),
        out_shape=[jax.ShapeDtypeStruct((row, width), jnp.float32) for row, width in zip(rows, widths)],
        in_specs=[pl.BlockSpec(memory_space=pl.ANY)] * (2 * arrays),
        out_specs=[pl.BlockSpec(memory_space=pl.ANY)] * arrays,
        scratch_shapes=[pltpu.VMEM(left.shape, left.dtype) for left in lefts]
        + [pltpu.VMEM(right.shape, right.dtype) for right in rights]
        + [pltpu.VMEM((2, count, row, width // 2), LOW) for row, width in zip(rows, widths)]
        + [pltpu.VMEM((row, width), jnp.float32) for row, width in zip(rows, widths)]
        + [
            pltpu.SemaphoreType.DMA((arrays, 2, 2, count - 1)),
            pltpu.SemaphoreType.DMA((arrays, 2, 2, count - 1)),
            pltpu.SemaphoreType.DMA((arrays, 2)),
            pltpu.SemaphoreType.DMA((arrays,)),
        ],
        compiler_params=pltpu.CompilerParams(
            collective_id=collective, has_side_effects=True, vmem_limit_bytes=VMEM_BYTES
        ),
        cost_estimate=pl.CostEstimate(flops=flops, bytes_accessed=30 * moved, transcendentals=0),
        name="ring_scatter",
    )(*lefts, *rights)


def from_behind(block, axis, distance):
    devices = range(lax.axis_size(axis))
    route = [(i - distance, i) for i in devices if i - distance in devices]
    return lax.ppermute(block, axis, route)


def contract_rows(left, right):
    return lax.dot_general(
        left, right, (((0,), (0,)), ((), ())), preferred_element_type=jnp.float32
    )


def contract_cols(left, right):
    return lax.dot_general(
        left, right, (((1,), (1,)), ((), ())), preferred_element_type=jnp.float32
    )


def gather_features(own):
    return lax.all_gather(own.T, "tp", axis=0, tiled=True)


def reduce_branch(term):
    return lax.psum_scatter(term.astype(LOW), "tp", scatter_dimension=1, tiled=True).astype(jnp.float32)


def norm_forward(values, gain_row):
    row_total = lax.psum(jnp.sum(values * values, axis=1, keepdims=True), "tp")
    row_scale = lax.rsqrt(row_total / D + EPSILON)
    own_normed = (values * row_scale * gain_row).astype(LOW)
    return gather_features(own_normed), row_scale


def norm_backward(grad_normed, kept_rows, row_scale, kept_gain):
    inner_sum = lax.psum(jnp.sum(grad_normed * kept_gain * kept_rows, axis=1, keepdims=True), "tp")
    rows_grad = row_scale * kept_gain * grad_normed - kept_rows * row_scale**3 * inner_sum / D
    return (rows_grad, jnp.sum(grad_normed * kept_rows * row_scale, axis=0))


def adam_update(weight, first, second, grad, rate, decay):
    first_next = BETA_ONE * first + (1.0 - BETA_ONE) * grad
    second_next = BETA_TWO * second + (1.0 - BETA_TWO) * grad * grad
    corrected = first_next / (1.0 - BETA_ONE**STEP)
    spread = jnp.sqrt(second_next / (1.0 - BETA_TWO**STEP)) + ADAM_EPSILON
    return (weight - rate * (corrected / spread + decay * weight), first_next, second_next)


def shards(
    tokens,
    bounds,
    cotangent,
    entry_weight,
    entry_first,
    entry_second,
    exit_weight,
    exit_first,
    exit_second,
    expand_weight,
    expand_first,
    expand_second,
    shrink_weight,
    shrink_first,
    shrink_second,
    conv_kernel,
    conv_first,
    conv_second,
    norm_gains,
    gain_first,
    gain_second,
):
    rows_dev = tokens.shape[0]
    channels = tokens.shape[1]
    hidden = shrink_weight.shape[1]
    small = jnp.concatenate([conv_kernel, norm_gains], axis=0).astype(LOW)
    small_full = lax.all_gather(small, "seq", axis=1, tiled=True).astype(jnp.float32)
    kernel = small_full[:3]
    gains_row = small_full[3:]
    entry_low = entry_weight.reshape(entry_weight.shape[0], 3 * channels).astype(LOW)
    gate_low = expand_weight[:, 0].astype(LOW)
    up_low = expand_weight[:, 1].astype(LOW)

    position = jnp.arange(rows_dev, dtype=jnp.int32)[:, None]
    boundary = bounds[0]
    see_one = (position != boundary).astype(jnp.float32)
    see_two = see_one * (position - 1 != boundary).astype(jnp.float32)
    tokens_f = tokens.astype(jnp.float32)

    normed_one, scale_one = norm_forward(tokens_f, gains_row[0])
    entry_full, exit_full = ring_gather([entry_low, exit_weight.astype(LOW)], 0)
    projected = contract_rows(normed_one, entry_full)
    input_gate = projected[:, :channels]
    output_gate = projected[:, channels : 2 * channels]
    values_rows = projected[:, 2 * channels :]
    gated_rows = (input_gate * values_rows).astype(LOW)
    previous = from_behind(gated_rows[-2:], "seq", 1)
    extended = jnp.concatenate([previous, gated_rows], axis=0).astype(jnp.float32)
    conv_out = (
        kernel[2] * extended[2:]
        + kernel[1] * extended[1:-1] * see_one
        + kernel[0] * extended[:-2] * see_two
    )
    mixer_rows = (output_gate * conv_out).astype(LOW)
    branch = reduce_branch(contract_cols(mixer_rows, exit_full))
    (gate_full,) = ring_gather([gate_low], 1)
    residual = tokens_f + branch
    normed_two, scale_two = norm_forward(residual, gains_row[1])
    (up_full,) = ring_gather([up_low], 2)
    cot_full = gather_features(cotangent)
    (shrink_full,) = ring_gather([shrink_weight.astype(LOW)], 3)
    gate_rows = contract_rows(normed_two, gate_full)
    up_rows = contract_rows(normed_two, up_full)
    sigmoid_gate = jax.nn.sigmoid(gate_rows)
    silu_gate = gate_rows * sigmoid_gate
    activation = (silu_gate * up_rows).astype(LOW)

    act_grad = contract_rows(cot_full, shrink_full)
    gate_grad = (
        act_grad * up_rows * sigmoid_gate * (1.0 + gate_rows * (1.0 - sigmoid_gate))
    ).astype(LOW)
    up_grad = (act_grad * silu_gate).astype(LOW)
    two_term = contract_cols(gate_grad, gate_full) + contract_cols(up_grad, up_full)
    grad_normed_two = reduce_branch(two_term)
    (shrink_part,) = ring_scatter([(cot_full, activation)], 4)
    mixed = (residual + reduce_branch(contract_cols(activation, shrink_full))).astype(LOW)
    residual_norm_grad, gain_two_grad = norm_backward(grad_normed_two, residual, scale_two, gains_row[1])
    residual_grad = cotangent.astype(jnp.float32) + residual_norm_grad
    branch_full = gather_features(residual_grad.astype(LOW))
    (gate_part,) = ring_scatter([(normed_two, gate_grad)], 5)
    mixer_grad = contract_rows(branch_full, exit_full)
    out_gate_grad = (mixer_grad * conv_out).astype(LOW)
    conv_grad = mixer_grad * output_gate
    lag_zero = conv_grad * kernel[2]
    lag_one = conv_grad * see_one * kernel[1]
    lag_two = conv_grad * see_two * kernel[0]
    padded_grad = (
        jnp.pad(lag_zero, ((2, 0), (0, 0)))
        + jnp.pad(lag_one, ((1, 1), (0, 0)))
        + jnp.pad(lag_two, ((0, 2), (0, 0)))
    )
    returned = from_behind(padded_grad[:2], "seq", -1)
    gated_grad = padded_grad[2:] + jnp.pad(returned, ((rows_dev - 2, 0), (0, 0)))
    kernel_grad = jnp.stack(
        [
            jnp.sum(conv_grad * see_two * extended[:-2], axis=0),
            jnp.sum(conv_grad * see_one * extended[1:-1], axis=0),
            jnp.sum(conv_grad * extended[2:], axis=0),
        ]
    )
    in_gate_grad = (gated_grad * values_rows).astype(LOW)
    values_grad = (gated_grad * input_gate).astype(LOW)
    projected_grad = jnp.concatenate([in_gate_grad, out_gate_grad, values_grad], axis=1)
    one_term = contract_cols(projected_grad, entry_full)
    grad_normed_one = reduce_branch(one_term)
    (up_part,) = ring_scatter([(normed_two, up_grad)], 6)
    tokens_norm_grad, gain_one_grad = norm_backward(grad_normed_one, tokens_f, scale_one, gains_row[0])
    tokens_grad = residual_grad + tokens_norm_grad
    small_grad = jnp.concatenate([kernel_grad, gain_one_grad[None], gain_two_grad[None]], axis=0)
    small_part = lax.psum_scatter(small_grad, "seq", scatter_dimension=1, tiled=True)
    kernel_part = small_part[:3]
    gains_part = small_part[3:]
    entry_part, exit_part = ring_scatter([(normed_one, projected_grad), (branch_full, mixer_rows)], 7)
    entry_part = entry_part.reshape(entry_weight.shape)
    expand_part = jnp.stack([gate_part, up_part], axis=1)
    entry_next, entry_first_next, entry_second_next = adam_update(
        entry_weight, entry_first, entry_second, entry_part, RATE_WIDE, WEIGHT_DECAY
    )
    exit_next, exit_first_next, exit_second_next = adam_update(
        exit_weight, exit_first, exit_second, exit_part, RATE_WIDE, WEIGHT_DECAY
    )
    expand_next, expand_first_next, expand_second_next = adam_update(
        expand_weight, expand_first, expand_second, expand_part, RATE_WIDE, WEIGHT_DECAY
    )
    shrink_next, shrink_first_next, shrink_second_next = adam_update(
        shrink_weight, shrink_first, shrink_second, shrink_part, RATE_WIDE, WEIGHT_DECAY
    )
    conv_next, conv_first_next, conv_second_next = adam_update(
        conv_kernel, conv_first, conv_second, kernel_part, RATE_CONV, 0.0
    )
    gains_next, gains_first_next, gains_second_next = adam_update(
        norm_gains, gain_first, gain_second, gains_part, RATE_GAIN, 0.0
    )
    return (
        mixed,
        tokens_grad,
        entry_next,
        entry_first_next,
        entry_second_next,
        exit_next,
        exit_first_next,
        exit_second_next,
        expand_next,
        expand_first_next,
        expand_second_next,
        shrink_next,
        shrink_first_next,
        shrink_second_next,
        conv_next,
        conv_first_next,
        conv_second_next,
        gains_next,
        gains_first_next,
        gains_second_next,
    )


def solution(mesh):
    rows = P("seq", "tp")
    stacked = P("seq", None, "tp")
    small = P(None, ("tp", "seq"))
    return jax.shard_map(
        shards,
        mesh=mesh,
        in_specs=(rows, P("seq"), rows) + (stacked,) * 3 + (rows,) * 3 + (stacked,) * 3 + (rows,) * 3 + (small,) * 6,
        out_specs=(rows, rows) + (stacked,) * 3 + (rows,) * 3 + (stacked,) * 3 + (rows,) * 3 + (small,) * 6,
        check_vma=False,
    )
```

time: 2340 us -> 1190 us (0.51)
  waiting for transfers between devices: 1920 us -> 186 us
  Pallas kernels: 0 us -> 680 us
  matrix products: 182 us -> 120 us
  local copies, waits for them, and re-layouts: 81.6 us -> 54.9 us
    reduce_scatter x9 -> x4, waiting for transfers between devices: 1320 us -> 95.6 us  [reduce_branch(): lax.psum_scatter(term.astype(LOW), 'tp', scatter_dimension=1, tiled=True)]
    pallas_call x0 -> x8, Pallas kernels: none -> 680 us  [the longest x4 345 us: ring_scatter(): pl.pallas_call(functools.partial(scatter_kernel, count, arrays), out_shap...]
    all_gather x8 -> x4, waiting for transfers between devices: 516 us -> 35.7 us  [gather_features(): return lax.all_gather(own.T, 'tp', axis=0, tiled=True)]
    dot_general x4 -> x0, matrix products: 60.2 us -> none  [the longest x1 23.7 us: shards(): jnp.dot(normed_two, expand_full.reshape(width_full, 2 * hidden), preferre...]
    all_gather x2 -> x0, local copies, waits for them, and re-layouts: 31.5 us -> none  [the longest x1 22.6 us: shards(): lax.all_gather(low_weights[2], 'seq', axis=0, tiled=True)]
    unnamed x21 -> x10, waiting for transfers between devices: 81 us -> 49.7 us
    unnamed x106 -> x95, local copies, waits for them, and re-layouts: 45.2 us -> 48 us
    dot_general x4 -> x5, matrix products: 54.3 us -> 53.6 us  [contract_cols(): lax.dot_general(left, right, (((1,), (1,)), ((), ())), preferred_element_...]
  transfers between devices with their start and end apart: 21 -> 11, of which waited for: 21 -> 6; matrix products, arithmetic and copies ran while one was open for 10% -> 11% of each run, Pallas kernels for 0% -> 58%
where the time goes in v1:
time: 1190 us; the launch traced here: 1180 us
  Pallas kernels  680 us (57%)
  waiting for transfers between devices  186 us (16%)
  matrix products  120 us (10%)
  other arithmetic  64.3 us (5%)
  local copies, waits for them, and re-layouts  54.9 us (5%)
  blocking collectives  52 us (4%)
  between operations  15.6 us (1%)
    pallas_call x4, Pallas kernels, ring_scatter(): pl.pallas_call(functools.partial(scatter_kernel, count, arrays), out_shap...  345 us
    pallas_call x4, Pallas kernels, ring_gather(): pl.pallas_call(functools.partial(gather_kernel, count, arrays), out_shape...  335 us
    reduce_scatter x4, waiting for transfers between devices, reduce_branch(): lax.psum_scatter(term.astype(LOW), 'tp', scatter_dimension=1, tiled=True)  95.6 us
    dot_general x5, matrix products, contract_rows(): lax.dot_general(left, right, (((0,), (0,)), ((), ())), preferred_element_...  66.8 us
    dot_general x5, matrix products, contract_cols(): lax.dot_general(left, right, (((1,), (1,)), ((), ())), preferred_element_...  53.6 us
    unnamed x10, waiting for transfers between devices  49.7 us
    unnamed x95, local copies, waits for them, and re-layouts  48 us
    all_gather x4, waiting for transfers between devices, gather_features(): return lax.all_gather(own.T, 'tp', axis=0, tiled=True)  35.7 us
  transfers between devices with their start and end apart: 11, of which 6 were waited for; matrix products, arithmetic and copies ran while one was open for 11% of the time, Pallas kernels for 58%

profile of v1, /device:TPU:0, one launch (start us, length us, event | category | flops | bytes accessed | tf_op | source)
XLA Modules:
  0.0 1178.4 jit_solution(7606864620832646693)
XLA Ops:
  9.0 8.3 psum.28
  18.0 26.3 %all-gather = bf16[8,64,5]{1,2,0:T(8,128)(2,1)S(1)} all-gather(bf16[1,64,5]{1,2,0:T(8,128)(2,1)S(1)} %maximum_bitcast_fusion), channel_id=1, replica_groups=mesh['seq'=8,'tp'=4] {'seq'}, dimensions={0}, use_global_device_ids=true | all-gather | bytes 5760 | tf_op jit(solution)/shard_map/all_gather | solution.py:336
  51.5 78.4 %ring_gather.4 = (bf16[8,256,1536]{2,1,0:T(8,128)(2,1)}, bf16[8,256,512]{2,1,0:T(8,128)(2,1)}) custom-call(bf16[256,1536]{1,0:T(8,128)(2,1)} %copy.124.refs_0_, bf16[256,512]{1,0:T(8,128)(2,1)} %convert_element_type.115.refs_1_), custom_call_target="tpu_custom_call" | custom-call | bytes 251658240 | tf_op jit(solution)/shard_map/ring_gather/pallas_call | solution.py:124
  129.9 10.3 fusion.36
  152.9 44.6 %reduce-scatter.8.cloned.1.call-done = bf16[1024,512]{0,1:T(8,128)(2,1)} async-done(((bf16[1024,2048]{0,1:T(8,128)(2,1)}), bf16[1024,512]{0,1:T(8,128)(2,1)}) %reduce-scatter.8.cloned.1.call-update) | async-done | bytes 1048592 | tf_op jit(solution)/shard_map/reduce_scatter | solution.py:285
  199.1 5.8 psum.29
  216.0 85.1 %ring_gather.5 = bf16[8,256,2048]{2,1,0:T(8,128)(2,1)} custom-call(bf16[256,2048]{1,0:T(8,128)(2,1)} %get-tuple-element.151.refs_0_), custom_call_target="tpu_custom_call" | custom-call | bytes 251658240 | tf_op jit(solution)/shard_map/ring_gather/pallas_call | solution.py:124
  301.1 93.7 %ring_gather.6 = bf16[8,256,2048]{2,1,0:T(8,128)(2,1)} custom-call(bf16[256,2048]{1,0:T(8,128)(2,1)} %get-tuple-element.152.refs_0_), custom_call_target="tpu_custom_call" | custom-call | bytes 251658240 | tf_op jit(solution)/shard_map/ring_gather/pallas_call | solution.py:124
  397.5 78.1 %ring_gather.7 = bf16[8,256,2048]{2,1,0:T(8,128)(2,1)} custom-call(bf16[256,2048]{1,0:T(8,128)(2,1)} %convert_element_type.126.refs_0_), custom_call_target="tpu_custom_call" | custom-call | bytes 251658240 | tf_op jit(solution)/shard_map/ring_gather/pallas_call | solution.py:124
  475.6 14.9 %fusion.37 = f32[1024,2048]{1,0:T(8,128)} fusion(bf16[2048,1024]{1,0:T(8,128)(2,1)} %all-gather.8.cloned.1.call-done.refs_0_, bf16[2048,2048]{1,0:T(8,128)(2,1)} %bitcast.73), kind=kOutput, calls=%fused_computation.102 | convolution fusion | flops 8589934592 | bytes 20971520 | tf_op jit(solution)/shard_map/dot_general | solution.py:269
  490.5 13.7 %fusion.38 = f32[1024,2048]{1,0:T(8,128)} fusion(bf16[2048,1024]{1,0:T(8,128)(2,1)S(1)} %copy-done.33, bf16[2048,2048]{1,0:T(8,128)(2,1)} %bitcast.75), kind=kOutput, calls=%fused_computation.103 | convolution fusion | flops 8589934592 | bytes 20971520 | tf_op jit(solution)/shard_map/dot_general | solution.py:269
  504.2 22.6 %multiply_convert_fusion = (bf16[1024,2048]{1,0:T(8,128)(2,1)S(1)}, bf16[1024,2048]{1,0:T(8,128)(2,1)}, bf16[1024,2048]{1,0:T(8,128)(2,1)}) fusion(f32[1024,2048]{1,0:T(8,128)} %fusion.37, f32[1024,2048]{1,0:T(8,128)} %fusion.38, bf16[2048,1024]{1,0:T(8,128)(2,1)} %all-gather.10.cloned.1.call-done.refs_0_, bf16[2048,2048]{1,0:T(8,128)(2,1)} %bitcast.71), kind=kOutput, calls=%fused_computation.1 | convolution fusion | flops 8621391872 | bytes 41943040 | tf_op jit(solution)/shard_map/dot_general | solution.py:269
  526.8 14.1 %fusion.39 = f32[1024,2048]{0,1:T(8,128)S(1)} fusion(bf16[1024,2048]{1,0:T(8,128)(2,1)} %get-tuple-element.141.refs_1_, bf16[2048,2048]{1,0:T(8,128)(2,1)} %bitcast.74), kind=kOutput, calls=%fused_computation.104 | convolution fusion | flops 8589934592 | bytes 20971520 | tf_op jit(solution)/shard_map/dot_general | solution.py:275
  540.8 12.9 %add_convert_fusion = bf16[1024,2048]{0,1:T(8,128)(2,1)} fusion(f32[1024,2048]{0,1:T(8,128)S(1)} %fusion.39, bf16[1024,2048]{1,0:T(8,128)(2,1)S(1)} %get-tuple-element.140.refs_1_, bf16[2048,2048]{1,0:T(8,128)(2,1)} %bitcast.76), kind=kOutput, calls=%fused_computation | convolution fusion | flops 8594128896 | bytes 25165824 | tf_op jit(solution)/shard_map/dot_general | solution.py:275
  553.8 51.0 %reduce-scatter.12.cloned.1.call-done = bf16[1024,512]{0,1:T(8,128)(2,1)} async-done(((bf16[1024,2048]{0,1:T(8,128)(2,1)}), bf16[1024,512]{0,1:T(8,128)(2,1)}) %reduce-scatter.12.cloned.1.call-update) | async-done | bytes 1048592 | tf_op jit(solution)/shard_map/reduce_scatter | solution.py:285
  607.3 5.8 psum.30
  617.1 35.7 %all-gather.12.cloned.1.call-done.refs_1_ = bf16[2048,1024]{1,0:T(8,128)(2,1)} async-done(((bf16[512,1024]{1,0:T(8,128)(2,1)}), bf16[2048,1024]{1,0:T(8,128)(2,1)}) %all-gather.12.cloned.1.call-update) | async-done | bytes 4194320 | tf_op jit(solution)/shard_map/all_gather | solution.py:281
  652.8 5.4 fusion.40
  669.3 8.4 convolution_convert_fusion
  677.8 13.9 %convolution_convert_fusion.1 = bf16[1024,2048]{0,1:T(8,128)(2,1)} fusion(bf16[1024,2048]{1,0:T(8,128)(2,1)} %get-tuple-element.142.refs_1_, bf16[2048,2048]{1,0:T(8,128)(2,1)} %bitcast.72), kind=kOutput, calls=%fused_computation.21 | convolution fusion | flops 8592031744 | bytes 16777216 | tf_op jit(solution)/shard_map/dot_general | solution.py:275
  697.7 87.3 %ring_scatter.5 = f32[256,2048]{1,0:T(8,128)} custom-call(bf16[2048,1024]{1,0:T(8,128)(2,1)} %all-gather.8.cloned.1.call-done.refs_0_, bf16[1024,2048]{1,0:T(8,128)(2,1)} %get-tuple-element.141.refs_1_), custom_call_target="tpu_custom_call" | custom-call | flops 8589934592 | bytes 251658240 | tf_op jit(solution)/shard_map/ring_scatter/pallas_call | solution.py:239
  785.0 85.7 %ring_scatter.6 = f32[256,2048]{1,0:T(8,128)} custom-call(bf16[2048,1024]{1,0:T(8,128)(2,1)} %all-gather.8.cloned.1.call-done.refs_0_, bf16[1024,2048]{1,0:T(8,128)(2,1)} %copy-done.34), custom_call_target="tpu_custom_call" | custom-call | flops 8589934592 | bytes 251658240 | tf_op jit(solution)/shard_map/ring_scatter/pallas_call | solution.py:239
  870.8 13.6 %multiply_subtract_fusion = (f32[256,2,2048]{2,0,1:T(8,128)S(1)}, f32[256,2,2048]{2,0,1:T(8,128)S(1)}, f32[256,2,2048]{2,0,1:T(8,128)S(1)}) fusion(f32[256,2,2048]{2,1,0:T(2,128)} %param.30, f32[256,1,2048]{2,0,1:T(8,128)} %bitcast.80, f32[256,1,2048]{2,0,1:T(8,128)S(1)} %bitcast.79, f32[256,2,2048]{2,1,0:T(2,128)} %param.31, f32[256,2,2048]{2,1,0:T(2,128)} %param.32), kind=kLoop, calls=%fused_computation.18 | loop fusion | flops 16777216 | bytes 29360128 | tf_op jit(solution)/shard_map/sub | solution.py:306
  884.4 5.2 copy.147
  894.9 5.2 copy.149
  900.1 85.3 %ring_scatter.7 = f32[256,2048]{1,0:T(8,128)} custom-call(bf16[2048,1024]{1,0:T(8,128)(2,1)} %all-gather.10.cloned.1.call-done.refs_0_, bf16[1024,2048]{1,0:T(8,128)(2,1)} %get-tuple-element.142.refs_1_), custom_call_target="tpu_custom_call" | custom-call | flops 8589934592 | bytes 251658240 | tf_op jit(solution)/shard_map/ring_scatter/pallas_call | solution.py:239
  985.5 7.0 multiply_subtract_fusion.1
  994.3 86.7 %ring_scatter.4 = (f32[256,1536]{1,0:T(8,128)}, f32[256,512]{1,0:T(8,128)}) custom-call(bf16[2048,1024]{1,0:T(8,128)(2,1)} %all-gather.6.cloned.1.call-done.refs_0_, bf16[2048,1024]{1,0:T(8,128)(2,1)} %all-gather.12.cloned.1.call-done.refs_1_, bf16[1024,1536]{1,0:T(8,128)(2,1)} %pad_maximum_fusion.1.refs_2_, bf16[1024,512]{1,0:T(8,128)(2,1)} %copy-done.19), custom_call_target="tpu_custom_call" | custom-call | flops 8589934592 | bytes 251658240 | tf_op jit(solution)/shard_map/ring_scatter/pallas_call | solution.py:239
  1084.2 5.3 multiply_subtract_fusion.2
  1103.3 5.8 psum.31
  1109.2 5.4 fusion.10
  1119.0 49.5 %reduce-scatter.16.cloned.1.call-done = f32[64,5]{1,0:T(8,128)} async-done(((f32[512,5]{1,0:T(8,128)}), f32[64,5]{1,0:T(8,128)}) %reduce-scatter.16.cloned.1.call-update) | async-done | bytes 1296
  (161 shorter events, 91.9 us)
Async XLA Ops:
  7.2 10.8 copy-start.25
  7.2 10.8 copy-start.29
  7.2 122.7 %all-gather.6.cloned.1.call-start = ((), (), s32[]{:S(2)}) async-start(), calls=%async_computation.5 | async-start | bytes 5242880 | tf_op jit(solution)/shard_map/all_gather | solution.py:281
  18.0 27.8 %copy-start.20 = (f32[1024,1]{0,1:T(1,128)}, f32[1024,1]{0,1:T(1,128)S(1)}, u32[]{:S(2)}) copy-start(f32[1024,1]{0,1:T(1,128)S(1)} %get-tuple-element.135) | copy-start | bytes 12292
  45.7 151.8 %reduce-scatter.8.cloned.1.call-start = ((), (), s32[]{:S(2)}) async-start(), calls=%async_computation.6 | async-start | bytes 5242880 | tf_op jit(solution)/shard_map/reduce_scatter | solution.py:285
  140.7 4.3 collective-permute-start
  152.9 322.7 %all-gather.8.cloned.1.call-start = ((), (), s32[]{:S(2)}) async-start(), calls=%async_computation.7 | async-start | bytes 5242880 | tf_op jit(solution)/shard_map/all_gather | solution.py:281
  207.5 296.7 %all-gather.10.cloned.1.call-start = ((), (), s32[]{:S(2)}) async-start(), calls=%async_computation.9 | async-start | bytes 5242880 | tf_op jit(solution)/shard_map/all_gather | solution.py:281
  209.9 395.0 %reduce-scatter.12.cloned.1.call-start = ((), (), s32[]{:S(2)}) async-start(), calls=%async_computation.10 | async-start | bytes 5242880 | tf_op jit(solution)/shard_map/reduce_scatter | solution.py:285
  475.6 14.9 %copy-start.33 = (bf16[2048,1024]{1,0:T(8,128)(2,1)S(1)}, bf16[2048,1024]{1,0:T(8,128)(2,1)}, u32[]{:S(2)}) copy-start(bf16[2048,1024]{1,0:T(8,128)(2,1)} %all-gather.8.cloned.1.call-done.refs_0_) | copy-start | bytes 12582916
  526.8 14.1 %copy-start.34 = (bf16[1024,2048]{1,0:T(8,128)(2,1)}, bf16[1024,2048]{1,0:T(8,128)(2,1)S(1)}, u32[]{:S(2)}) copy-start(bf16[1024,2048]{1,0:T(8,128)(2,1)S(1)} %get-tuple-element.140.refs_1_) | copy-start | bytes 12582916
  553.7 99.0 %all-gather.12.cloned.1.call-start = ((), (), s32[]{:S(2)}) async-start(), calls=%async_computation.11 | async-start | bytes 5242880 | tf_op jit(solution)/shard_map/all_gather | solution.py:281
  617.0 483.1 %reduce-scatter.14.cloned.1.call-start = ((), (), s32[]{:S(2)}) async-start(), calls=%async_computation.12 | async-start | bytes 5242880 | tf_op jit(solution)/shard_map/reduce_scatter | solution.py:285
  660.7 7.3 copy-start.9
  661.2 8.1 slice-start.2
  661.2 8.1 slice-start.3
  661.2 5.9 collective-permute-start.1
  677.7 431.5 %reduce-scatter.10.cloned.1.call-start = ((), (), s32[]{:S(2)}) async-start(), calls=%async_computation.8 | async-start | bytes 5242880 | tf_op jit(solution)/shard_map/reduce_scatter | solution.py:285
  691.7 476.8 %reduce-scatter.16.cloned.1.call-start = ((), (), s32[]{:S(2)}) async-start(), calls=%async_computation.13 | async-start | bytes 294912
  785.0 85.7 %copy-start.15 = (f32[256,2048]{1,0:T(8,128)S(1)}, f32[256,2048]{1,0:T(8,128)}, u32[]{:S(2)}) copy-start(f32[256,2048]{1,0:T(8,128)} %ring_scatter.5) | copy-start | bytes 6291460
  900.1 85.3 %copy-start.6 = (f32[256,2048]{1,0:T(8,128)S(1)}, f32[256,2048]{1,0:T(8,128)}, u32[]{:S(2)}) copy-start(f32[256,2048]{1,0:T(8,128)} %param.33) | copy-start | bytes 6291460
  985.5 7.1 copy-start.10
  985.5 7.1 copy-start.12
  1100.1 9.1 copy-start
  1100.1 9.1 copy-start.2
  1100.1 9.1 copy-start.24
  1117.6 52.6 %copy-start.30 = (f32[2,64]{1,0:T(2,128)S(1)}, f32[2,64]{1,0:T(2,128)}, u32[]{:S(2)}) copy-start(f32[2,64]{1,0:T(2,128)} %param.39) | copy-start | bytes 1540
  1117.6 52.6 %copy-start.31 = (f32[2,64]{1,0:T(2,128)S(1)}, f32[2,64]{1,0:T(2,128)}, u32[]{:S(2)}) copy-start(f32[2,64]{1,0:T(2,128)} %param.40) | copy-start | bytes 1540
  1117.6 52.6 %copy-start.32 = (f32[2,64]{1,0:T(2,128)S(1)}, f32[2,64]{1,0:T(2,128)}, u32[]{:S(2)}) copy-start(f32[2,64]{1,0:T(2,128)} %param.41) | copy-start | bytes 1540
  1117.6 53.2 %copy-start.26 = (f32[3,64]{1,0:T(4,128)S(1)}, f32[3,64]{1,0:T(4,128)}, u32[]{:S(2)}) copy-start(f32[3,64]{1,0:T(4,128)} %param.36) | copy-start | bytes 2308
  1117.6 53.2 %copy-start.27 = (f32[3,64]{1,0:T(4,128)S(1)}, f32[3,64]{1,0:T(4,128)}, u32[]{:S(2)}) copy-start(f32[3,64]{1,0:T(4,128)} %param.37) | copy-start | bytes 2308
  1117.6 53.2 %copy-start.28 = (f32[3,64]{1,0:T(4,128)S(1)}, f32[3,64]{1,0:T(4,128)}, u32[]{:S(2)}) copy-start(f32[3,64]{1,0:T(4,128)} %param.38) | copy-start | bytes 2308
  (18 other events, 58.2 us)
Sparse Core Ops, SparseCore 0:
  45.8 32.9 all-gather.5
  153.0 44.4 reduce-scatter.7
  207.6 35.5 all-gather.7
  244.7 34.4 all-gather.9
  553.9 50.9 reduce-scatter.11
  617.2 35.5 all-gather.11
  677.8 44.4 reduce-scatter.13
  725.0 44.5 reduce-scatter.9
  1109.3 59.1 reduce-scatter.15

commit v2 on v1

--- a/solution.py
+++ b/solution.py
@@ -277,19 +277,26 @@
     )
 
 
+def tie(*values):
+    return lax.optimization_barrier(values)
+
+
+def gather_rows(own):
+    return lax.all_gather(own, "tp", axis=0, tiled=True)
+
+
 def gather_features(own):
-    return lax.all_gather(own.T, "tp", axis=0, tiled=True)
+    return gather_rows(own.T)
 
 
 def reduce_branch(term):
-    return lax.psum_scatter(term.astype(LOW), "tp", scatter_dimension=1, tiled=True).astype(jnp.float32)
+    return lax.psum_scatter(term, "tp", scatter_dimension=1, tiled=True).astype(jnp.float32)
 
 
 def norm_forward(values, gain_row):
     row_total = lax.psum(jnp.sum(values * values, axis=1, keepdims=True), "tp")
     row_scale = lax.rsqrt(row_total / D + EPSILON)
-    own_normed = (values * row_scale * gain_row).astype(LOW)
-    return gather_features(own_normed), row_scale
+    return (values * row_scale * gain_row).astype(LOW), row_scale
 
 
 def norm_backward(grad_normed, kept_rows, row_scale, kept_gain):
@@ -331,11 +338,9 @@
 ):
     rows_dev = tokens.shape[0]
     channels = tokens.shape[1]
-    hidden = shrink_weight.shape[1]
-    small = jnp.concatenate([conv_kernel, norm_gains], axis=0).astype(LOW)
-    small_full = lax.all_gather(small, "seq", axis=1, tiled=True).astype(jnp.float32)
-    kernel = small_full[:3]
-    gains_row = small_full[3:]
+    count = lax.axis_size("seq")
+    small = jnp.concatenate([conv_kernel, norm_gains], axis=0)
+    small = jnp.pad(small, ((0, 32 - small.shape[0]), (0, 128 - small.shape[1]))).astype(LOW)
     entry_low = entry_weight.reshape(entry_weight.shape[0], 3 * channels).astype(LOW)
     gate_low = expand_weight[:, 0].astype(LOW)
     up_low = expand_weight[:, 1].astype(LOW)
@@ -346,8 +351,19 @@
     see_two = see_one * (position - 1 != boundary).astype(jnp.float32)
     tokens_f = tokens.astype(jnp.float32)
 
-    normed_one, scale_one = norm_forward(tokens_f, gains_row[0])
-    entry_full, exit_full = ring_gather([entry_low, exit_weight.astype(LOW)], 0)
+    tokens_full = gather_features(tokens)
+    entry_full, exit_full, small_full = ring_gather([entry_low, exit_weight.astype(LOW), small], 0)
+    tokens_full, entry_full, small_full = tie(tokens_full, entry_full, small_full)
+    small_full = small_full.reshape(count, 32, 128)[:, :5, : conv_kernel.shape[1]]
+    small_full = small_full.swapaxes(0, 1).reshape(5, channels).astype(jnp.float32)
+    kernel = small_full[:3]
+    gains_row = small_full[3:]
+    gain_one_full = lax.all_gather(gains_row[0].astype(LOW), "tp", axis=0, tiled=True).astype(jnp.float32)
+
+    tokens_full = tokens_full.astype(jnp.float32)
+    scale_row = lax.rsqrt(jnp.sum(tokens_full * tokens_full, axis=0, keepdims=True) / D + EPSILON)
+    normed_one = (tokens_full * scale_row * gain_one_full[:, None]).astype(LOW)
+    scale_one = scale_row.reshape(rows_dev, 1)
     projected = contract_rows(normed_one, entry_full)
     input_gate = projected[:, :channels]
     output_gate = projected[:, channels : 2 * channels]
@@ -361,13 +377,17 @@
         + kernel[0] * extended[:-2] * see_two
     )
     mixer_rows = (output_gate * conv_out).astype(LOW)
-    branch = reduce_branch(contract_cols(mixer_rows, exit_full))
+    branch_term, gate_low = tie(contract_cols(mixer_rows, exit_full).astype(LOW), gate_low)
     (gate_full,) = ring_gather([gate_low], 1)
+    branch, gate_full = tie(reduce_branch(branch_term), gate_full)
     residual = tokens_f + branch
-    normed_two, scale_two = norm_forward(residual, gains_row[1])
+    own_normed_two, scale_two = norm_forward(residual, gains_row[1])
+    own_normed_two, up_low = tie(own_normed_two.T, up_low)
     (up_full,) = ring_gather([up_low], 2)
-    cot_full = gather_features(cotangent)
-    (shrink_full,) = ring_gather([shrink_weight.astype(LOW)], 3)
+    normed_two, up_full = tie(gather_rows(own_normed_two), up_full)
+    cot_own, shrink_low, normed_two = tie(cotangent.T, shrink_weight.astype(LOW), normed_two)
+    (shrink_full,) = ring_gather([shrink_low], 3)
+    cot_full, shrink_full = tie(gather_rows(cot_own), shrink_full)
     gate_rows = contract_rows(normed_two, gate_full)
     up_rows = contract_rows(normed_two, up_full)
     sigmoid_gate = jax.nn.sigmoid(gate_rows)
@@ -380,13 +400,16 @@
     ).astype(LOW)
     up_grad = (act_grad * silu_gate).astype(LOW)
     two_term = contract_cols(gate_grad, gate_full) + contract_cols(up_grad, up_full)
-    grad_normed_two = reduce_branch(two_term)
+    two_term, activation = tie(two_term.astype(LOW), activation)
     (shrink_part,) = ring_scatter([(cot_full, activation)], 4)
-    mixed = (residual + reduce_branch(contract_cols(activation, shrink_full))).astype(LOW)
+    grad_normed_two, shrink_part = tie(reduce_branch(two_term), shrink_part)
     residual_norm_grad, gain_two_grad = norm_backward(grad_normed_two, residual, scale_two, gains_row[1])
     residual_grad = cotangent.astype(jnp.float32) + residual_norm_grad
-    branch_full = gather_features(residual_grad.astype(LOW))
+    mixed_term = contract_cols(activation, shrink_full).astype(LOW)
+    branch_own, mixed_term, gate_grad = tie(residual_grad.astype(LOW).T, mixed_term, gate_grad)
     (gate_part,) = ring_scatter([(normed_two, gate_grad)], 5)
+    branch_full, gate_part, mixed_branch = tie(gather_rows(branch_own), gate_part, reduce_branch(mixed_term))
+    mixed = (residual + mixed_branch).astype(LOW)
     mixer_grad = contract_rows(branch_full, exit_full)
     out_gate_grad = (mixer_grad * conv_out).astype(LOW)
     conv_grad = mixer_grad * output_gate
@@ -410,15 +433,19 @@
     in_gate_grad = (gated_grad * values_rows).astype(LOW)
     values_grad = (gated_grad * input_gate).astype(LOW)
     projected_grad = jnp.concatenate([in_gate_grad, out_gate_grad, values_grad], axis=1)
-    one_term = contract_cols(projected_grad, entry_full)
-    grad_normed_one = reduce_branch(one_term)
+    one_term, up_grad = tie(contract_cols(projected_grad, entry_full).astype(LOW), up_grad)
     (up_part,) = ring_scatter([(normed_two, up_grad)], 6)
+    grad_normed_one, up_part = tie(reduce_branch(one_term), up_part)
     tokens_norm_grad, gain_one_grad = norm_backward(grad_normed_one, tokens_f, scale_one, gains_row[0])
     tokens_grad = residual_grad + tokens_norm_grad
     small_grad = jnp.concatenate([kernel_grad, gain_one_grad[None], gain_two_grad[None]], axis=0)
-    small_part = lax.psum_scatter(small_grad, "seq", scatter_dimension=1, tiled=True)
+    small_grad = lax.psum(small_grad, "seq")
+    small_part = lax.dynamic_slice_in_dim(
+        small_grad, lax.axis_index("seq") * conv_kernel.shape[1], conv_kernel.shape[1], axis=1
+    )
     kernel_part = small_part[:3]
     gains_part = small_part[3:]
+    projected_grad, small_part = tie(projected_grad, small_part)
     entry_part, exit_part = ring_scatter([(normed_one, projected_grad), (branch_full, mixer_rows)], 7)
     entry_part = entry_part.reshape(entry_weight.shape)
     expand_part = jnp.stack([gate_part, up_part], axis=1)

time: 1190 us -> 1000 us (0.84)
  waiting for transfers between devices: 186 us -> 5.05 us
  Pallas kernels: 680 us -> 666 us
    reduce_scatter x4, waiting for transfers between devices: 95.6 us -> 0.07 us  [reduce_branch(): lax.psum_scatter(term, 'tp', scatter_dimension=1, tiled=True)]
    unnamed x10 -> x8, waiting for transfers between devices: 49.7 us -> 0.81 us
    psum x0 -> x1, blocking collectives: none -> 35.9 us  [shards(): small_grad = lax.psum(small_grad, 'seq')]
    all_gather x4, waiting for transfers between devices: 35.7 us -> 0.03 us  [gather_rows(): return lax.all_gather(own, 'tp', axis=0, tiled=True)]
    all_gather x1, blocking collectives: 26.3 us -> 5.33 us  [shards(): lax.all_gather(gains_row[0].astype(LOW), 'tp', axis=0, tiled=True)]
    pallas_call x4, Pallas kernels: 345 us -> 325 us  [ring_scatter(): pl.pallas_call(functools.partial(scatter_kernel, count, arrays), out_shap...]
    unnamed x95 -> x117, local copies, waits for them, and re-layouts: 48 us -> 51.5 us
  transfers between devices with their start and end apart: 11 -> 10, of which waited for: 6 -> 2; matrix products, arithmetic and copies ran while one was open for 11% -> 6% of each run, Pallas kernels for 58% -> 59%
where the time goes in v2:
time: 1000 us; the launch traced here: 999 us
  Pallas kernels  666 us (67%)
  matrix products  116 us (12%)
  other arithmetic  73.8 us (7%)
  blocking collectives  58.4 us (6%)
  local copies, waits for them, and re-layouts  57.9 us (6%)
  between operations  15.7 us (2%)
    pallas_call x4, Pallas kernels, ring_gather(): pl.pallas_call(functools.partial(gather_kernel, count, arrays), out_shape...  341 us
    pallas_call x4, Pallas kernels, ring_scatter(): pl.pallas_call(functools.partial(scatter_kernel, count, arrays), out_shap...  325 us
    dot_general x5, matrix products, contract_rows(): lax.dot_general(left, right, (((0,), (0,)), ((), ())), preferred_element_...  63.7 us
    dot_general x5, matrix products, contract_cols(): lax.dot_general(left, right, (((1,), (1,)), ((), ())), preferred_element_...  52.2 us
    unnamed x117, local copies, waits for them, and re-layouts  51.5 us
    psum x1, blocking collectives, shards(): small_grad = lax.psum(small_grad, 'seq')  35.9 us
    sub x6, other arithmetic, adam_update(): weight - rate * (corrected / spread + decay * weight)  30 us
  transfers between devices with their start and end apart: 10, of which 2 were waited for; matrix products, arithmetic and copies ran while one was open for 6% of the time, Pallas kernels for 59%

profile of v2, /device:TPU:0, one launch (start us, length us, event | category | flops | bytes accessed | tf_op | source)
XLA Modules:
  0.0 999.1 jit_solution(5979098918766237337)
XLA Ops:
  13.0 4.4 copy.135
  18.1 85.4 %ring_gather.4 = (bf16[8,256,1536]{2,1,0:T(8,128)(2,1)}, bf16[8,256,512]{2,1,0:T(8,128)(2,1)}, bf16[8,32,128]{2,1,0:T(8,128)(2,1)}) custom-call(bf16[256,1536]{1,0:T(8,128)(2,1)} %copy.96.refs_0_, bf16[256,512]{1,0:T(8,128)(2,1)} %convert_element_type.130.refs_1_, bf16[32,128]{1,0:T(8,128)(2,1)} %fusion.22.refs_2_), custom_call_target="tpu_custom_call" | custom-call | bytes 253624320 | tf_op jit(solution)/shard_map/ring_gather/pallas_call | solution.py:124
  106.0 5.3 all-gather
  118.6 6.7 fusion.34
  137.9 4.4 convolution_convert_fusion.2
  142.7 84.9 %ring_gather.5 = bf16[8,256,2048]{2,1,0:T(8,128)(2,1)} custom-call(bf16[256,2048]{1,0:T(8,128)(2,1)} %get-tuple-element.63.refs_0_), custom_call_target="tpu_custom_call" | custom-call | bytes 251658240 | tf_op jit(solution)/shard_map/ring_gather/pallas_call | solution.py:124
  230.9 5.6 psum.28
  243.5 83.9 %ring_gather.6 = bf16[8,256,2048]{2,1,0:T(8,128)(2,1)} custom-call(bf16[256,2048]{1,0:T(8,128)(2,1)} %get-tuple-element.66.refs_0_), custom_call_target="tpu_custom_call" | custom-call | bytes 251658240 | tf_op jit(solution)/shard_map/ring_gather/pallas_call | solution.py:124
  327.5 87.0 %ring_gather.7 = bf16[8,256,2048]{2,1,0:T(8,128)(2,1)} custom-call(bf16[256,2048]{1,0:T(8,128)(2,1)} %convert_element_type.145.refs_0_), custom_call_target="tpu_custom_call" | custom-call | bytes 251658240 | tf_op jit(solution)/shard_map/ring_gather/pallas_call | solution.py:124
  414.5 14.7 %fusion.36 = f32[1024,2048]{1,0:T(8,128)} fusion(bf16[2048,1024]{1,0:T(8,128)(2,1)} %all-gather.8.cloned.1.call-done.refs_0_, bf16[2048,2048]{1,0:T(8,128)(2,1)} %bitcast.58), kind=kOutput, calls=%fused_computation.106 | convolution fusion | flops 8589934592 | bytes 20971520 | tf_op jit(solution)/shard_map/dot_general | solution.py:269
  429.2 14.9 %fusion.35 = f32[1024,2048]{1,0:T(8,128)} fusion(bf16[2048,1024]{1,0:T(8,128)(2,1)} %all-gather.10.cloned.1.call-done.refs_0_, bf16[2048,2048]{1,0:T(8,128)(2,1)} %bitcast.62), kind=kOutput, calls=%fused_computation.105 | convolution fusion | flops 8589934592 | bytes 20971520 | tf_op jit(solution)/shard_map/dot_general | solution.py:269
  444.1 22.1 %multiply_convert_fusion = (bf16[1024,2048]{1,0:T(8,128)(2,1)}, bf16[1024,2048]{1,0:T(8,128)(2,1)}, bf16[1024,2048]{1,0:T(8,128)(2,1)}) fusion(f32[1024,2048]{1,0:T(8,128)} %fusion.36, f32[1024,2048]{1,0:T(8,128)} %fusion.35, bf16[2048,1024]{1,0:T(8,128)(2,1)S(1)} %copy-done.45, bf16[2048,2048]{1,0:T(8,128)(2,1)} %bitcast.60), kind=kOutput, calls=%fused_computation.5 | convolution fusion | flops 8621391872 | bytes 41943040 | tf_op jit(solution)/shard_map/dot_general | solution.py:269
  466.2 12.7 %fusion.37 = f32[1024,2048]{0,1:T(8,128)S(1)} fusion(bf16[1024,2048]{1,0:T(8,128)(2,1)} %get-tuple-element.79.refs_1_, bf16[2048,2048]{1,0:T(8,128)(2,1)} %bitcast.59), kind=kOutput, calls=%fused_computation.107 | convolution fusion | flops 8589934592 | bytes 20971520 | tf_op jit(solution)/shard_map/dot_general | solution.py:275
  478.9 13.0 %add_convert_fusion = bf16[1024,2048]{0,1:T(8,128)(2,1)} fusion(f32[1024,2048]{0,1:T(8,128)S(1)} %fusion.37, bf16[1024,2048]{1,0:T(8,128)(2,1)S(1)} %copy-done.46, bf16[2048,2048]{1,0:T(8,128)(2,1)} %bitcast.61), kind=kOutput, calls=%fused_computation.6 | convolution fusion | flops 8594128896 | bytes 25165824 | tf_op jit(solution)/shard_map/dot_general | solution.py:275
  491.9 78.3 %ring_scatter.4 = f32[256,2048]{1,0:T(8,128)} custom-call(bf16[2048,1024]{1,0:T(8,128)(2,1)} %all-gather.10.cloned.1.call-done.refs_0_, bf16[1024,2048]{1,0:T(8,128)(2,1)} %get-tuple-element.76.refs_1_), custom_call_target="tpu_custom_call" | custom-call | flops 8589934592 | bytes 251658240 | tf_op jit(solution)/shard_map/ring_scatter/pallas_call | solution.py:239
  570.2 13.9 %convolution_convert_fusion.1 = bf16[1024,2048]{0,1:T(8,128)(2,1)} fusion(bf16[1024,2048]{1,0:T(8,128)(2,1)} %get-tuple-element.76.refs_1_, bf16[2048,2048]{1,0:T(8,128)(2,1)} %bitcast.63), kind=kOutput, calls=%fused_computation.20 | convolution fusion | flops 8592031744 | bytes 16777216 | tf_op jit(solution)/shard_map/dot_general | solution.py:275
  587.4 5.8 psum.29
  593.2 3.8 convert_bitcast_fusion
  597.9 86.7 %ring_scatter.5 = f32[256,2048]{1,0:T(8,128)} custom-call(bf16[2048,1024]{1,0:T(8,128)(2,1)} %all-gather.8.cloned.1.call-done.refs_0_, bf16[1024,2048]{1,0:T(8,128)(2,1)} %get-tuple-element.79.refs_1_), custom_call_target="tpu_custom_call" | custom-call | flops 8589934592 | bytes 251658240 | tf_op jit(solution)/shard_map/ring_scatter/pallas_call | solution.py:239
  687.4 5.4 fusion.38
  703.9 8.2 convolution_convert_fusion
  718.4 8.2 multiply_subtract_fusion.1
  728.3 85.4 %ring_scatter.6 = f32[256,2048]{1,0:T(8,128)} custom-call(bf16[2048,1024]{1,0:T(8,128)(2,1)} %all-gather.8.cloned.1.call-done.refs_0_, bf16[1024,2048]{1,0:T(8,128)(2,1)} %get-tuple-element.84.refs_1_), custom_call_target="tpu_custom_call" | custom-call | flops 8589934592 | bytes 251658240 | tf_op jit(solution)/shard_map/ring_scatter/pallas_call | solution.py:239
  815.6 13.9 %multiply_subtract_fusion = (f32[256,2,2048]{2,0,1:T(8,128)S(1)}, f32[256,2,2048]{2,0,1:T(8,128)S(1)}, f32[256,2,2048]{2,0,1:T(8,128)S(1)}) fusion(f32[256,2,2048]{2,1,0:T(2,128)} %param.30, f32[256,1,2048]{2,0,1:T(8,128)} %bitcast.67, f32[256,1,2048]{2,0,1:T(8,128)S(1)} %bitcast.66, f32[256,2,2048]{2,1,0:T(2,128)} %param.31, f32[256,2,2048]{2,1,0:T(2,128)} %param.32), kind=kLoop, calls=%fused_computation.17 | loop fusion | flops 16777216 | bytes 29360128 | tf_op jit(solution)/shard_map/sub | solution.py:313
  829.5 5.2 copy.119
  834.8 5.2 copy.120
  840.0 5.2 copy.121
  846.1 35.9 %psum.31 = f32[5,512]{1,0:T(8,128)S(1)} all-reduce(f32[5,512]{1,0:T(8,128)S(1)} %concatenate.16), channel_id=1, replica_groups=mesh['seq'=8,'tp'=4] {'seq'}, use_global_device_ids=true, to_apply=%region_16.17 | all-reduce | flops 2560 | bytes 20480 | tf_op jit(solution)/shard_map/psum | solution.py:442
  882.2 74.9 %ring_scatter.7 = (f32[256,1536]{1,0:T(8,128)}, f32[256,512]{1,0:T(8,128)}) custom-call(bf16[2048,1024]{1,0:T(8,128)(2,1)} %copy-done.14, bf16[2048,1024]{1,0:T(8,128)(2,1)} %all-gather.12.cloned.1.call-done.refs_1_, bf16[1024,1536]{1,0:T(8,128)(2,1)} %pad_maximum_fusion.1.refs_2_, bf16[1024,512]{1,0:T(8,128)(2,1)} %copy-done.26), custom_call_target="tpu_custom_call" | custom-call | flops 8589934592 | bytes 251658240 | tf_op jit(solution)/shard_map/ring_scatter/pallas_call | solution.py:239
  960.2 5.3 multiply_subtract_fusion.2
  973.4 5.6 psum.30
  979.1 6.0 fusion.10
  (190 shorter events, 85.4 us)
Async XLA Ops:
  7.2 97.9 %all-gather.6.cloned.1.call-start = ((), (), s32[]{:S(2)}) async-start(), calls=%async_computation.4 | async-start | bytes 5242880 | tf_op jit(solution)/shard_map/all_gather | solution.py:285
  9.6 217.9 %reduce-scatter.5.cloned.1.call-start = ((), (), s32[]{:S(2)}) async-start(), calls=%async_computation.5 | async-start | bytes 5242880 | tf_op jit(solution)/shard_map/reduce_scatter | solution.py:293
  105.9 8.6 copy-start.33
  111.3 4.5 copy-start.7
  118.6 6.8 copy-start.14
  128.4 4.7 collective-permute-start
  133.4 4.5 copy-start.23
  142.3 185.1 %all-gather.8.cloned.1.call-start = ((), (), s32[]{:S(2)}) async-start(), calls=%async_computation.6 | async-start | bytes 5242880 | tf_op jit(solution)/shard_map/all_gather | solution.py:285
  239.4 189.8 %all-gather.10.cloned.1.call-start = ((), (), s32[]{:S(2)}) async-start(), calls=%async_computation.7 | async-start | bytes 5242880 | tf_op jit(solution)/shard_map/all_gather | solution.py:285
  327.5 256.7 %reduce-scatter.7.cloned.1.call-start = ((), (), s32[]{:S(2)}) async-start(), calls=%async_computation.8 | async-start | bytes 5242880 | tf_op jit(solution)/shard_map/reduce_scatter | solution.py:293
  429.2 14.9 %copy-start.45 = (bf16[2048,1024]{1,0:T(8,128)(2,1)S(1)}, bf16[2048,1024]{1,0:T(8,128)(2,1)}, u32[]{:S(2)}) copy-start(bf16[2048,1024]{1,0:T(8,128)(2,1)} %all-gather.8.cloned.1.call-done.refs_0_) | copy-start | bytes 12582916
  466.2 12.7 %copy-start.46 = (bf16[1024,2048]{1,0:T(8,128)(2,1)S(1)}, bf16[1024,2048]{1,0:T(8,128)(2,1)}, u32[]{:S(2)}) copy-start(bf16[1024,2048]{1,0:T(8,128)(2,1)} %get-tuple-element.84.refs_1_) | copy-start | bytes 12582916
  491.9 192.7 %reduce-scatter.9.cloned.1.call-start = ((), (), s32[]{:S(2)}) async-start(), calls=%async_computation.10 | async-start | bytes 5242880 | tf_op jit(solution)/shard_map/reduce_scatter | solution.py:293
  586.0 7.2 copy-start.8
  597.1 90.3 %all-gather.12.cloned.1.call-start = ((), (), s32[]{:S(2)}) async-start(), calls=%async_computation.9 | async-start | bytes 5242880 | tf_op jit(solution)/shard_map/all_gather | solution.py:285
  597.8 215.9 %reduce-scatter.11.cloned.1.call-start = ((), (), s32[]{:S(2)}) async-start(), calls=%async_computation.11 | async-start | bytes 5242880 | tf_op jit(solution)/shard_map/reduce_scatter | solution.py:293
  687.4 5.4 copy-start.11
  695.8 6.0 slice-start
  695.8 8.1 slice-start.2
  695.8 5.9 slice-start.1
  695.8 8.1 slice-start.3
  695.9 5.9 collective-permute-start.1
  718.4 8.2 copy-start.17
  718.4 8.2 copy-start.19
  815.3 29.9 %copy-start.6 = (f32[1024,512]{0,1:T(8,128)}, f32[1024,512]{0,1:T(8,128)S(1)}, u32[]{:S(2)}) copy-start(f32[1024,512]{0,1:T(8,128)S(1)} %convert_element_type.161) | copy-start | bytes 6291460
  840.0 5.3 copy-start.4
  840.0 5.3 copy-start.32
  840.0 5.3 copy-start.34
  970.3 8.8 copy-start.1
  970.3 8.8 copy-start.35
  985.0 4.4 copy-start.37
  985.0 4.4 copy-start.38
  (29 other events, 64.1 us)
Sparse Core Ops, SparseCore 0:
  10.2 37.1 all-gather.5
  142.5 45.4 reduce-scatter.4
  239.6 34.0 all-gather.7
  327.6 33.4 all-gather.9
  492.0 43.7 reduce-scatter.6
  597.2 43.4 reduce-scatter.8
  642.8 34.4 all-gather.11
  712.3 43.8 reduce-scatter.10

commit v3 on v0

v3 whole, which is shorter than its diff:
```python
import functools

import jax
import jax.numpy as jnp
from jax import lax
from jax.experimental import pallas as pl
from jax.experimental.layout import Layout, with_layout_constraint
from jax.experimental.pallas import tpu as pltpu
from jax.sharding import PartitionSpec as P

D = 2048
STEP = 10


EPSILON = 1e-05
BETA_ONE = 0.9
BETA_TWO = 0.95
ADAM_EPSILON = 1e-08
WEIGHT_DECAY = 0.1
RATE_WIDE = 0.04
RATE_CONV = 0.5
RATE_GAIN = 0.4

MESH = pl.DeviceIdType.MESH
LOW = jnp.bfloat16
VMEM_BYTES = 60 * 1024 * 1024


def ring_place(index, count):
    side = index % 2
    level = index // 2
    return level * (1 - side) + (count - 1 - level) * side


def ring_index(place, count):
    back = place // (count // 2)
    return (1 - back) * (2 * place) + back * (2 * (count - 1 - place) + 1)


def ring_ends(count):
    place = ring_place(lax.axis_index("seq"), count)
    ahead = ring_index((place + 1) % count, count)
    behind = ring_index((place + count - 1) % count, count)
    return place, ahead, behind


def greet(peers):
    barrier = pltpu.get_barrier_semaphore()
    for peer in peers:
        pl.semaphore_signal(barrier, inc=1, device_id=peer, device_id_type=MESH)
    pl.semaphore_wait(barrier, len(peers))


def split(items, sizes):
    parts, start = [], 0
    for size in sizes:
        parts.append(items[start : start + size])
        start += size
    return parts


class GatherRing:
    name = "ring_gather"

    def __init__(self, shards):
        self.count = lax.axis_size("seq")
        self.inputs = list(shards)
        self.arrays = len(shards)
        self.rows = [shard.shape[0] for shard in shards]
        self.parts = 2 if min(self.rows) % 64 == 0 else 1
        self.ticks = (self.count - 2) * self.parts
        self.out_shapes = [jax.ShapeDtypeStruct((self.count,) + shard.shape, shard.dtype) for shard in shards]
        sems = pltpu.SemaphoreType.DMA((self.arrays, 2, self.parts, self.count - 1))
        self.scratch = [sems, sems, pltpu.SemaphoreType.DMA((self.arrays,))]
        self.flops = 0
        self.bytes = 20 * sum(shard.size for shard in shards) * 2 * self.count

    def bind(self, ins, outs, scratch):
        self.shard_refs, self.full_refs = ins, outs
        self.send_sem, self.recv_sem, self.own_sem = scratch
        self.column = lax.axis_index("tp")
        self.place, self.ahead, self.behind = ring_ends(self.count)

    def pieces(self):
        return [(array, way) for array in range(self.arrays) for way in range(2)]

    def copy(self, array, way, part, step, first=False):
        move = (self.place + self.count - step) if way == 0 else (self.place + step)
        owner = ring_index(move % self.count, self.count)
        size = self.rows[array] // 2 // self.parts
        rows = pl.ds(pl.multiple_of(way * (self.rows[array] // 2) + part * size, 16), size)
        there = self.full_refs[array].at[owner, rows]
        return pltpu.make_async_remote_copy(
            src_ref=self.shard_refs[array].at[rows] if first else there,
            dst_ref=there,
            send_sem=self.send_sem.at[array, way, part, step],
            recv_sem=self.recv_sem.at[array, way, part, step],
            device_id=(self.ahead if way == 0 else self.behind, self.column),
            device_id_type=MESH,
        )

    def own(self, array):
        there = self.full_refs[array].at[lax.axis_index("seq")]
        return pltpu.make_async_copy(self.shard_refs[array], there, self.own_sem.at[array])

    def peers(self):
        return [(self.ahead, self.column), (self.behind, self.column)]

    def prepare(self):
        pass

    def start(self):
        for part in range(self.parts):
            for array, way in self.pieces():
                self.copy(array, way, part, 0, True).start()
        for array in range(self.arrays):
            self.own(array).start()

    def tick(self, index):
        step, part = 1 + index // self.parts, index % self.parts
        for array, way in self.pieces():
            self.copy(array, way, part, step - 1).wait_recv()
            self.copy(array, way, part, step).start()

    def finish(self):
        for part in range(self.parts):
            for array, way in self.pieces():
                self.copy(array, way, part, self.count - 2).wait_recv()

        def sent(step, carry):
            for part in range(self.parts):
                for array, way in self.pieces():
                    self.copy(array, way, part, step).wait_send()
            return carry

        lax.fori_loop(0, self.count - 1, sent, 0)
        for array in range(self.arrays):
            self.own(array).wait()


class ScatterRing:
    name = "ring_scatter"

    def __init__(self, pairs):
        self.count = count = lax.axis_size("seq")
        lefts = [left for left, right in pairs]
        rights = [right for left, right in pairs]
        self.inputs = lefts + rights
        self.arrays = len(pairs)
        self.rows = [left.shape[0] // count for left in lefts]
        self.columns = [right.shape[1] for right in rights]
        self.parts = 2 if min(self.columns) % 512 == 0 else 1
        self.ticks = (count - 2) * self.parts
        self.out_shapes = [
            jax.ShapeDtypeStruct((row, width), jnp.float32) for row, width in zip(self.rows, self.columns)
        ]
        sems = pltpu.SemaphoreType.DMA((self.arrays, 2, self.parts, count - 1))
        self.scratch = (
            [pltpu.VMEM(left.shape, left.dtype) for left in lefts]
            + [pltpu.VMEM(right.shape, right.dtype) for right in rights]
            + [pltpu.VMEM((2, count, row, width // 2), LOW) for row, width in zip(self.rows, self.columns)]
            + [pltpu.VMEM((row, width), jnp.float32) for row, width in zip(self.rows, self.columns)]
            + [sems, sems, pltpu.SemaphoreType.DMA((self.arrays, 2)), pltpu.SemaphoreType.DMA((self.arrays,))]
        )
        self.flops = sum(2 * left.size * width for left, width in zip(lefts, self.columns))
        self.bytes = 20 * sum(left.shape[0] * width * 2 for left, width in zip(lefts, self.columns))

    def bind(self, ins, outs, scratch):
        arrays = self.arrays
        self.in_refs, self.out_refs = ins, outs
        self.lefts, self.rights, self.slots, self.finals = split(scratch, [arrays] * 4)
        self.send_sem, self.recv_sem, self.load_sem, self.done_sem = scratch[4 * arrays :]
        self.column = lax.axis_index("tp")
        self.place, self.ahead, self.behind = ring_ends(self.count)

    def pieces(self):
        return [(array, way) for array in range(self.arrays) for way in range(2)]

    def span(self, array, way, part):
        half = self.columns[array] // 2
        width = half // self.parts
        inner = part * width
        return way * half + inner, inner, width

    def term(self, array, way, part, step):
        move = (self.place + 2 * self.count - 1 - step) if way == 0 else (self.place + 1 + step)
        owner = ring_index(move % self.count, self.count)
        rows = self.rows[array]
        start, _, width = self.span(array, way, part)
        left = self.lefts[array][pl.ds(pl.multiple_of(owner * rows, 16), rows), :]
        right = self.rights[array][:, pl.ds(pl.multiple_of(start, 128), width)]
        return jnp.dot(left, right, preferred_element_type=jnp.float32)

    def held(self, array, way, part, step):
        _, inner, width = self.span(array, way, part)
        return self.slots[array].at[way, step, :, pl.ds(pl.multiple_of(inner, 128), width)]

    def copy(self, array, way, part, step):
        return pltpu.make_async_remote_copy(
            src_ref=self.held(array, way, part, step),
            dst_ref=self.held(array, way, part, step + 1),
            send_sem=self.send_sem.at[array, way, part, step],
            recv_sem=self.recv_sem.at[array, way, part, step],
            device_id=(self.ahead if way == 0 else self.behind, self.column),
            device_id_type=MESH,
        )

    def loads(self):
        return [
            pltpu.make_async_copy(
                self.in_refs[array + side * self.arrays],
                (self.rights if side else self.lefts)[array],
                self.load_sem.at[array, side],
            )
            for array in range(self.arrays)
            for side in range(2)
        ]

    def peers(self):
        return [(self.ahead, self.column), (self.behind, self.column)]

    def prepare(self):
        for load in self.loads():
            load.start()

    def start(self):
        for load in self.loads():
            load.wait()
        for part in range(self.parts):
            for array, way in self.pieces():
                self.held(array, way, part, 0)[...] = self.term(array, way, part, 0).astype(LOW)
                self.copy(array, way, part, 0).start()

    def tick(self, index):
        step, part = 1 + index // self.parts, index % self.parts
        for array, way in self.pieces():
            mine = self.term(array, way, part, step)
            self.copy(array, way, part, step - 1).wait_recv()
            held = self.held(array, way, part, step)
            held[...] = (held[...].astype(jnp.float32) + mine).astype(LOW)
            self.copy(array, way, part, step).start()

    def finish(self):
        last = self.count - 1
        for part in range(self.parts):
            for array, way in self.pieces():
                start, _, width = self.span(array, way, part)
                mine = self.term(array, way, part, last)
                self.copy(array, way, part, last - 1).wait_recv()
                self.finals[array][:, start : start + width] = (
                    self.held(array, way, part, last)[...].astype(jnp.float32) + mine
                )
        stores = [
            pltpu.make_async_copy(self.finals[array], self.out_refs[array], self.done_sem.at[array])
            for array in range(self.arrays)
        ]
        for store in stores:
            store.start()

        def sent(step, carry):
            for part in range(self.parts):
                for array, way in self.pieces():
                    self.copy(array, way, part, step).wait_send()
            return carry

        lax.fori_loop(0, last, sent, 0)
        for store in stores:
            store.wait()


class NoJob:
    inputs, out_shapes, scratch, tiles, flops = [], [], [], 0, 0

    def bind(self, ins, outs, scratch):
        pass

    def peers(self):
        return []

    def start(self):
        pass

    def finish(self):
        pass


class Job:
    wide = 256

    def __init__(self, whole, tiled, outs, tiles, flops):
        self.whole, self.tiled = whole, tiled
        self.inputs = list(whole) + [array for array, axis in tiled]
        self.axes = [axis for array, axis in tiled]
        self.out_shapes = [jax.ShapeDtypeStruct(shape, dtype) for shape, dtype in outs]
        self.tiles = tiles
        self.flops = flops
        self.scratch = (
            [pltpu.VMEM(array.shape, array.dtype) for array in self.inputs]
            + [pltpu.VMEM(shape, dtype) for shape, dtype in outs]
            + [
                pltpu.SemaphoreType.DMA((len(whole),)),
                pltpu.SemaphoreType.DMA((len(tiled), tiles)),
                pltpu.SemaphoreType.DMA((len(outs), tiles)),
            ]
        )

    def bind(self, ins, outs, scratch):
        self.in_refs, self.out_refs = ins, outs
        sizes = [len(self.whole), len(self.tiled), len(outs)]
        self.whole_v, self.tiled_v, self.outs_v = split(scratch, sizes)
        self.whole_sem, self.tiled_sem, self.out_sem = scratch[sum(sizes) :]

    def peers(self):
        return []

    def window(self, axis, index):
        span = pl.ds(pl.multiple_of(index * self.wide, 128), self.wide)
        return (span,) if axis == 0 else (slice(None), span)

    def whole_load(self, which):
        return pltpu.make_async_copy(self.in_refs[which], self.whole_v[which], self.whole_sem.at[which])

    def tiled_load(self, which, index):
        window = self.window(self.axes[which], index)
        there = self.in_refs[len(self.whole) + which].at[window]
        return pltpu.make_async_copy(there, self.tiled_v[which].at[window], self.tiled_sem.at[which, index])

    def out_window(self, index):
        return self.window(1, index)

    def store(self, which, index):
        window = self.out_window(index)
        return pltpu.make_async_copy(
            self.outs_v[which].at[window], self.out_refs[which].at[window], self.out_sem.at[which, index]
        )

    def start(self):
        for which in range(len(self.whole)):
            self.whole_load(which).start()

        def begin(index, carry):
            for which in range(len(self.tiled)):
                self.tiled_load(which, index).start()
            return carry

        lax.fori_loop(0, self.tiles, begin, 0)

    def tile(self, index):
        @pl.when(index == 0)
        def _():
            for which in range(len(self.whole)):
                self.whole_load(which).wait()

        for which in range(len(self.tiled)):
            self.tiled_load(which, index).wait()
        tiles = [ref[self.window(axis, index)] for ref, axis in zip(self.tiled_v, self.axes)]
        for which, value in enumerate(self.compute(self.whole_v, tiles)):
            self.outs_v[which][self.out_window(index)] = value
            self.store(which, index).start()

    def finish(self):
        def end(index, carry):
            for which in range(len(self.outs_v)):
                self.store(which, index).wait()
            return carry

        lax.fori_loop(0, self.tiles, end, 0)


def blocks_dot(blocks, weight):
    parts, _, depth = blocks.shape
    total = None
    for part in range(parts):
        term = jnp.dot(blocks[part], weight[part * depth : (part + 1) * depth], preferred_element_type=jnp.float32)
        total = term if total is None else total + term
    return total


class ExpandJob(Job):
    def __init__(self, normed, gate_full, up_full):
        rows, width = normed.shape[1], gate_full.shape[1]
        outs = [((rows, width), jnp.float32), ((rows, width), jnp.float32), ((rows, width), LOW)]
        super().__init__(
            [normed], [(gate_full, 1), (up_full, 1)], outs, width // self.wide, 4 * rows * gate_full.size
        )

    def compute(self, whole, tiles):
        gate_rows = blocks_dot(whole[0], tiles[0])
        up_rows = blocks_dot(whole[0], tiles[1])
        return gate_rows, up_rows, (gate_rows * jax.nn.sigmoid(gate_rows) * up_rows).astype(LOW)


class HiddenGradJob(Job):
    def __init__(self, cot, shrink_full, gate_rows, up_rows):
        rows, width = gate_rows.shape
        outs = [((rows, width), LOW), ((rows, width), LOW)]
        tiled = [(shrink_full, 1), (gate_rows, 1), (up_rows, 1)]
        super().__init__([cot], tiled, outs, width // self.wide, 2 * rows * shrink_full.size)

    def compute(self, whole, tiles):
        _, gate_rows, up_rows = tiles
        act_grad = blocks_dot(whole[0], tiles[0])
        sigmoid_gate = jax.nn.sigmoid(gate_rows)
        gate_grad = act_grad * up_rows * sigmoid_gate * (1.0 + gate_rows * (1.0 - sigmoid_gate))
        return gate_grad.astype(LOW), (act_grad * (gate_rows * sigmoid_gate)).astype(LOW)


class WidthJob(Job):
    def __init__(self, lefts, weights):
        rows, width = lefts[0].shape[0], weights[0].shape[0]
        flops = 2 * rows * sum(weight.size for weight in weights)
        self.own = width // lax.axis_size("tp")
        self.height = rows
        out = ((rows * lax.axis_size("tp"), self.own), LOW)
        super().__init__(lefts, [(weight, 0) for weight in weights], [out], width // self.wide, flops)

    def out_window(self, index):
        return owner_window(index, self.wide, self.own, self.height)

    def compute(self, whole, tiles):
        total = None
        for left, weight in zip(whole, tiles):
            term = contract_cols(left[...], weight)
            total = term if total is None else total + term
        return (total.astype(LOW),)


def owner_window(index, wide, own, height):
    each = own // wide
    rows = pl.ds(pl.multiple_of(index // each * height, 16), height)
    return rows, pl.ds(pl.multiple_of(index % each * wide, 128), wide)


class MixerJob:
    def __init__(self, inputs, outs, extra, phases, flops):
        self.inputs = list(inputs)
        self.out_shapes = [jax.ShapeDtypeStruct(shape, dtype) for shape, dtype in outs]
        self.phases = phases
        self.tiles = sum(phases)
        self.flops = flops
        self.scratch = (
            [pltpu.VMEM(array.shape, array.dtype) for array in self.inputs]
            + [pltpu.VMEM(shape, dtype) for shape, dtype in outs]
            + extra
            + [
                pltpu.SemaphoreType.DMA((len(self.inputs),)),
                pltpu.SemaphoreType.DMA((len(outs),)),
                pltpu.SemaphoreType.DMA((2,)),
            ]
        )

    def bind(self, ins, outs, scratch):
        self.in_refs, self.out_refs = ins, outs
        extra = len(scratch) - len(ins) - len(outs) - 3
        self.ins_v, self.outs_v, self.extra_v = split(scratch, [len(ins), len(outs), extra])
        self.in_sem, self.out_sem, self.pass_sem = scratch[-3:]
        self.count = lax.axis_size("seq")
        self.seq = lax.axis_index("seq")
        self.column = lax.axis_index("tp")

    def peers(self):
        after = (self.seq + 1) % self.count
        before = (self.seq + self.count - 1) % self.count
        return [(after, self.column), (before, self.column)]

    def load(self, which):
        return pltpu.make_async_copy(self.in_refs[which], self.ins_v[which], self.in_sem.at[which])

    def store(self, which):
        return pltpu.make_async_copy(self.outs_v[which], self.out_refs[which], self.out_sem.at[which])

    def passing(self, source, target, forward):
        step = 1 if forward else self.count - 1
        return pltpu.make_async_remote_copy(
            src_ref=source,
            dst_ref=target,
            send_sem=self.pass_sem.at[0],
            recv_sem=self.pass_sem.at[1],
            device_id=((self.seq + step) % self.count, self.column),
            device_id_type=MESH,
        )

    def start(self):
        for which in range(len(self.inputs)):
            self.load(which).start()

    def tile(self, index):
        begin = 0
        for phase, tiles in enumerate(self.phases):
            here = index - begin

            @pl.when((here >= 0) & (here < tiles))
            def _(phase=phase, here=here, tiles=tiles):
                @pl.when(here == 0)
                def _():
                    self.before(phase)

                self.work(phase, here)

                @pl.when(here == tiles - 1)
                def _():
                    self.after(phase)

            begin += tiles

    def finish(self):
        for which in range(len(self.out_shapes)):
            self.store(which).wait()


def visible(bound_row, shape):
    position = lax.broadcasted_iota(jnp.int32, shape, 0)
    see_one = position != bound_row
    return position, see_one, see_one & (position - 1 != bound_row)


def lagged(rows, halo, position):
    last, second = halo[15:16].astype(jnp.float32), halo[14:15].astype(jnp.float32)
    one = jnp.where(position == 0, last, pltpu.roll(rows, 1, 0))
    two = jnp.where(position == 0, second, jnp.where(position == 1, last, pltpu.roll(rows, 2, 0)))
    return one, two


class EntryJob(MixerJob):
    def __init__(self, tokens, gains, entry_full, exit_full, taps, bound):
        parts, rows, own = tokens.shape
        width, columns = exit_full.shape
        self.rows, self.columns, self.own = rows, columns, own
        self.width = width
        outs = [
            ((rows, 3 * columns), jnp.float32),
            ((rows, columns), jnp.float32),
            ((rows, columns), LOW),
            ((16, columns), LOW),
            ((rows, columns), LOW),
            ((parts * rows, own), LOW),
            ((rows, 128), jnp.float32),
            ((width, rows), LOW),
        ]
        phases = [rows // 256, 3 * columns // 256, 1, columns // 128, width // 256]
        flops = 2 * rows * (entry_full.size + exit_full.size)
        super().__init__([tokens, gains, entry_full, exit_full, taps, bound], outs, [], phases, flops)

    def halo(self):
        return self.passing(self.outs_v[2].at[pl.ds(self.rows - 16, 16)], self.outs_v[3], True)

    def before(self, phase):
        if phase == 0:
            for which in (0, 1):
                self.load(which).wait()
        if phase == 1:
            self.store(6).start()
            self.store(7).start()
            self.load(2).wait()
        if phase == 3:
            for which in (4, 5):
                self.load(which).wait()
            self.halo().wait_recv()
            self.store(3).start()
        if phase == 4:
            self.load(3).wait()

    def after(self, phase):
        if phase == 1:
            self.store(0).start()
        if phase == 2:
            self.halo().start()
            self.store(2).start()
        if phase == 3:
            self.store(1).start()
            self.store(4).start()
        if phase == 4:
            self.store(5).start()

    def finish(self):
        self.halo().wait_send()
        super().finish()

    def work(self, phase, index):
        tokens, gains, entry, exits, taps, bound = self.ins_v
        projected, conv, gated, halo, mixer, term, scales, turned_rows = self.outs_v
        columns = self.columns
        if phase == 0:
            rows = pl.ds(pl.multiple_of(index * 256, 256), 256)
            values = [tokens[part, rows, :].astype(jnp.float32) for part in range(tokens.shape[0])]
            total = sum(jnp.sum(value * value, axis=1, keepdims=True) for value in values)
            scale = lax.rsqrt(total / D + EPSILON)
            scales[rows, :] = jnp.broadcast_to(scale, (256, 128))
            for part, value in enumerate(values):
                normed = (value * scale * gains[part, 0:1, :]).astype(LOW)
                tokens[part, rows, :] = normed
                turned_rows[part * self.own : (part + 1) * self.own, rows] = normed.T
        if phase == 1:
            span = pl.ds(pl.multiple_of(index * 256, 256), 256)
            projected[:, span] = blocks_dot(tokens, entry[:, span])
        if phase == 2:
            gated[...] = (projected[:, :columns] * projected[:, 2 * columns :]).astype(LOW)
        if phase == 3:
            span = pl.ds(pl.multiple_of(index * 128, 128), 128)
            middle = pl.ds(pl.multiple_of(columns + index * 128, 128), 128)
            rows = gated[:, span].astype(jnp.float32)
            position, see_one, see_two = visible(bound[0:1, :], rows.shape)
            before = halo[:, span].astype(jnp.float32) * jnp.where(self.seq > 0, 1.0, 0.0)
            one, two = lagged(rows, before, position)
            total = (
                taps[2:3, span] * rows
                + taps[1:2, span] * jnp.where(see_one, one, 0.0)
                + taps[0:1, span] * jnp.where(see_two, two, 0.0)
            )
            conv[:, span] = total
            mixer[:, span] = (projected[:, middle] * total).astype(LOW)
        if phase == 4:
            features = pl.ds(pl.multiple_of(index * 256, 256), 256)
            window = owner_window(index, 256, self.own, self.rows)
            term[window] = contract_cols(mixer[...], exits[features, :]).astype(LOW)


class MixerGradJob(MixerJob):
    def __init__(self, branch, exit_full, entry_full, projected, conv, gated, halo, taps, bound):
        parts, rows, own = branch.shape
        width, columns = exit_full.shape
        self.rows, self.columns, self.own = rows, columns, own
        outs = [((rows, 3 * columns), LOW), ((parts * rows, own), LOW), ((8, columns), jnp.float32)]
        extra = [
            pltpu.VMEM((rows, columns), jnp.float32),
            pltpu.VMEM((8, columns), jnp.float32),
            pltpu.VMEM((8, columns), jnp.float32),
        ]
        phases = [columns // 256, 1, columns // 128, width // 256]
        flops = 2 * rows * (entry_full.size + exit_full.size)
        inputs = [branch, exit_full, entry_full, projected, conv, gated, halo, taps, bound]
        super().__init__(inputs, outs, extra, phases, flops)

    def back(self):
        return self.passing(self.extra_v[1], self.extra_v[2], False)

    def before(self, phase):
        if phase == 0:
            for which in (0, 1, 3, 4):
                self.load(which).wait()
        if phase == 1:
            for which in (7, 8):
                self.load(which).wait()
        if phase == 2:
            for which in (5, 6):
                self.load(which).wait()
            self.back().wait_recv()
        if phase == 3:
            self.load(2).wait()

    def after(self, phase):
        if phase == 1:
            self.back().start()
        if phase == 2:
            self.store(0).start()
            self.store(2).start()
        if phase == 3:
            self.store(1).start()

    def finish(self):
        self.back().wait_send()
        super().finish()

    def work(self, phase, index):
        branch, exits, entry, projected, conv, gated, halo, taps, bound = self.ins_v
        grads, term, taps_grad = self.outs_v
        conv_grad, sent, returned = self.extra_v
        columns, height = self.columns, self.rows
        if phase == 0:
            span = pl.ds(pl.multiple_of(index * 256, 256), 256)
            middle = pl.ds(pl.multiple_of(columns + index * 256, 256), 256)
            mixer_grad = blocks_dot(branch, exits[:, span])
            grads[:, middle] = (mixer_grad * conv[:, span]).astype(LOW)
            conv_grad[:, span] = mixer_grad * projected[:, middle]
        if phase == 1:
            for start in range(0, columns, 128):
                span = slice(start, start + 128)
                rows = conv_grad[0:8, span]
                position, see_one, see_two = visible(bound[0:1, :], rows.shape)
                one = pltpu.roll(jnp.where(see_one, rows, 0.0) * taps[1:2, span], 1, 0)
                two = jnp.where(see_two, rows, 0.0) * taps[0:1, span]
                sent[:, span] = two + jnp.where(position == 0, 0.0, one)
            taps_grad[...] = jnp.zeros_like(taps_grad)
        if phase == 2:
            span = pl.ds(pl.multiple_of(index * 128, 128), 128)
            last = pl.ds(pl.multiple_of(2 * columns + index * 128, 128), 128)
            rows = conv_grad[:, span]
            position, see_one, see_two = visible(bound[0:1, :], rows.shape)
            seen_one, seen_two = jnp.where(see_one, rows, 0.0), jnp.where(see_two, rows, 0.0)
            one = pltpu.roll(seen_one * taps[1:2, span], height - 1, 0)
            two = pltpu.roll(seen_two * taps[0:1, span], height - 2, 0)
            after = returned[:, span] * jnp.where(self.seq < self.count - 1, 1.0, 0.0)
            gated_grad = (
                rows * taps[2:3, span]
                + jnp.where(position == height - 1, after[1:2], one)
                + jnp.where(position < height - 2, two, jnp.where(position == height - 2, after[0:1], 0.0))
            )
            grads[:, span] = (gated_grad * projected[:, last]).astype(LOW)
            grads[:, last] = (gated_grad * projected[:, span]).astype(LOW)
            own_rows = gated[:, span].astype(jnp.float32)
            before = halo[:, span].astype(jnp.float32) * jnp.where(self.seq > 0, 1.0, 0.0)
            lag_one, lag_two = lagged(own_rows, before, position)
            taps_grad[0:1, span] = jnp.sum(seen_two * lag_two, axis=0, keepdims=True)
            taps_grad[1:2, span] = jnp.sum(seen_one * lag_one, axis=0, keepdims=True)
            taps_grad[2:3, span] = jnp.sum(rows * own_rows, axis=0, keepdims=True)
        if phase == 3:
            features = pl.ds(pl.multiple_of(index * 256, 256), 256)
            window = owner_window(index, 256, self.own, height)
            term[window] = contract_cols(grads[...], entry[features, :]).astype(LOW)


class SmallSumJob:
    tiles, flops = 0, 0

    def __init__(self, blocks):
        count = lax.axis_size("seq")
        self.inputs = [blocks]
        self.out_shapes = [jax.ShapeDtypeStruct(blocks.shape[1:], blocks.dtype)]
        self.scratch = [
            pltpu.VMEM(blocks.shape, blocks.dtype),
            pltpu.VMEM(blocks.shape, blocks.dtype),
            pltpu.VMEM(blocks.shape[1:], blocks.dtype),
            pltpu.SemaphoreType.DMA((2,)),
            pltpu.SemaphoreType.DMA((count,)),
            pltpu.SemaphoreType.DMA((count,)),
        ]

    def bind(self, ins, outs, scratch):
        self.source, self.target = ins[0], outs[0]
        self.own, self.slots, self.total, self.local_sem, self.send_sem, self.recv_sem = scratch
        self.count = lax.axis_size("seq")
        self.seq = lax.axis_index("seq")
        self.column = lax.axis_index("tp")

    def peers(self):
        return [((self.seq + far) % self.count, self.column) for far in range(1, self.count)]

    def copy(self, far):
        other = (self.seq + far) % self.count
        return pltpu.make_async_remote_copy(
            src_ref=self.own.at[other],
            dst_ref=self.slots.at[far],
            send_sem=self.send_sem.at[far],
            recv_sem=self.recv_sem.at[far],
            device_id=(other, self.column),
            device_id_type=MESH,
        )

    def start(self):
        load = pltpu.make_async_copy(self.source, self.own, self.local_sem.at[0])
        load.start()
        load.wait()

        def begin(far, carry):
            self.copy(far).start()
            return carry

        lax.fori_loop(1, self.count, begin, 0)

    def finish(self):
        self.total[...] = self.own[self.seq]

        def add(far, carry):
            self.copy(far).wait_recv()
            self.total[...] += self.slots[far]
            return carry

        lax.fori_loop(1, self.count, add, 0)
        store = pltpu.make_async_copy(self.total, self.target, self.local_sem.at[1])
        store.start()

        def sent(far, carry):
            self.copy(far).wait_send()
            return carry

        lax.fori_loop(1, self.count, sent, 0)
        store.wait()


def ring_kernel(ring, job, *refs):
    sizes = [len(group) for group in (ring.inputs, job.inputs, ring.out_shapes, job.out_shapes, ring.scratch, job.scratch)]
    ring_in, job_in, ring_out, job_out, ring_scratch, job_scratch = split(refs, sizes)
    ring.bind(ring_in, ring_out, ring_scratch)
    job.bind(job_in, job_out, job_scratch)
    ring.prepare()
    greet(ring.peers() + job.peers())
    ring.start()
    job.start()
    each = -(-job.tiles // ring.ticks)

    def step(index, carry):
        for inner in range(each):
            tile = index * each + inner

            @pl.when(tile < job.tiles)
            def _(tile=tile):
                job.tile(tile)

        ring.tick(index)
        return carry

    lax.fori_loop(0, ring.ticks, step, 0)
    ring.finish()
    job.finish()


def run_ring(ring, job, collective):
    inputs = ring.inputs + job.inputs
    outs = ring.out_shapes + job.out_shapes
    return pl.pallas_call(
        functools.partial(ring_kernel, ring, job),
        out_shape=outs,
        in_specs=[pl.BlockSpec(memory_space=pl.ANY)] * len(inputs),
        out_specs=[pl.BlockSpec(memory_space=pl.ANY)] * len(outs),
        scratch_shapes=ring.scratch + job.scratch,
        compiler_params=pltpu.CompilerParams(
            collective_id=collective, has_side_effects=True, vmem_limit_bytes=VMEM_BYTES
        ),
        cost_estimate=pl.CostEstimate(flops=ring.flops + job.flops, bytes_accessed=ring.bytes, transcendentals=0),
        name=ring.name,
    )(*inputs)


def flat(full):
    return full.reshape(full.shape[0] * full.shape[1], full.shape[2])


def contract_rows(left, right):
    return lax.dot_general(
        left, right, (((0,), (0,)), ((), ())), preferred_element_type=jnp.float32
    )


def contract_cols(left, right):
    return lax.dot_general(
        left, right, (((1,), (1,)), ((), ())), preferred_element_type=jnp.float32
    )


def tie(*values):
    return lax.optimization_barrier(values)


def gather_rows(own):
    return lax.all_gather(own, "tp", axis=0, tiled=True)


def turned(own):
    return with_layout_constraint(own.T, Layout(major_to_minor=(0, 1)))


def gather_blocks(own):
    return gather_rows(own).reshape(-1, *own.shape)


def reduce_branch(term):
    return lax.psum_scatter(term, "tp", scatter_dimension=0, tiled=True).astype(jnp.float32)


def share_small(own):
    count = lax.axis_size("tp")
    pieces = [own] + [
        lax.ppermute(own, "tp", [(i, (i + far) % count) for i in range(count)]) for far in range(1, count)
    ]
    place = lax.axis_index("tp")
    return jnp.stack([lax.dynamic_index_in_dim(jnp.stack(pieces), (place - part) % count, 0, False) for part in range(count)])


def norm_forward(values, gain_row):
    row_total = lax.psum(jnp.sum(values * values, axis=1, keepdims=True), "tp")
    row_scale = lax.rsqrt(row_total / D + EPSILON)
    return (values * row_scale * gain_row).astype(LOW), row_scale


def norm_backward(grad_normed, kept_rows, row_scale, kept_gain):
    inner_sum = lax.psum(jnp.sum(grad_normed * kept_gain * kept_rows, axis=1, keepdims=True), "tp")
    rows_grad = row_scale * kept_gain * grad_normed - kept_rows * row_scale**3 * inner_sum / D
    return (rows_grad, jnp.sum(grad_normed * kept_rows * row_scale, axis=0))


def adam_update(weight, first, second, grad, rate, decay):
    first_next = BETA_ONE * first + (1.0 - BETA_ONE) * grad
    second_next = BETA_TWO * second + (1.0 - BETA_TWO) * grad * grad
    corrected = first_next / (1.0 - BETA_ONE**STEP)
    spread = jnp.sqrt(second_next / (1.0 - BETA_TWO**STEP)) + ADAM_EPSILON
    return (weight - rate * (corrected / spread + decay * weight), first_next, second_next)


def adam_kernel(pieces, *refs):
    weight, first, second = refs[:3]
    grads, outs = refs[3 : 3 + pieces], refs[3 + pieces :]
    start = 0
    for grad in grads:
        span = slice(start, start + grad.shape[1])
        start += grad.shape[1]
        results = adam_update(weight[:, span], first[:, span], second[:, span], grad[...], RATE_WIDE, WEIGHT_DECAY)
        for out, result in zip(outs, results):
            out[:, span] = result


def adam_rows(weight, first, second, grads, planes=1):
    rows, columns = weight.shape[0] // planes, weight.shape[1]
    block = max(rows // 8, 8) if columns > 1024 else max(rows // 2, 8)
    steps = rows // block
    state = pl.BlockSpec((block, columns), lambda plane, step: (plane * steps + step, 0))
    grad_specs = [
        pl.BlockSpec((block, grad.shape[1] // planes), lambda plane, step: (step, plane)) for grad in grads
    ]
    return pl.pallas_call(
        functools.partial(adam_kernel, len(grads)),
        out_shape=[jax.ShapeDtypeStruct(weight.shape, weight.dtype)] * 3,
        grid=(planes, steps),
        in_specs=[state] * 3 + grad_specs,
        out_specs=[state] * 3,
        cost_estimate=pl.CostEstimate(flops=20 * weight.size, bytes_accessed=28 * weight.size, transcendentals=0),
        name="adam_rows",
    )(weight, first, second, *grads)


def adam_pairs_kernel(lanes, *refs):
    weight, first, second = refs[:3]
    grads, outs, mixed = refs[3:7], refs[7:10], refs[10]
    rows = grads[0].shape[0]
    tiles = grads[0].shape[1] // lanes
    for which, grad in enumerate(grads):
        half, side = which // 2, which % 2
        for tile in range(tiles):
            place = (half * tiles + tile) * 2 + side
            mixed[pl.ds(place, rows, stride=4 * tiles), :] = grad[:, tile * lanes : (tile + 1) * lanes]
    results = adam_update(weight[...], first[...], second[...], mixed[...], RATE_WIDE, WEIGHT_DECAY)
    for out, result in zip(outs, results):
        out[...] = result


def adam_pairs(weight, first, second, grads):
    rows, _, columns = weight.shape
    lanes = 128
    deep = columns // lanes

    def seen(array):
        return array.reshape(rows, 2, deep, lanes).transpose(0, 2, 1, 3).reshape(rows * deep * 2, lanes)

    block = max(rows // 8, 8)
    state = pl.BlockSpec((block * deep * 2, lanes), lambda step: (step, 0))
    results = pl.pallas_call(
        functools.partial(adam_pairs_kernel, lanes),
        out_shape=[jax.ShapeDtypeStruct((rows * deep * 2, lanes), weight.dtype)] * 3,
        grid=(rows // block,),
        in_specs=[state] * 3 + [pl.BlockSpec((block, columns // 2), lambda step: (step, 0))] * 4,
        out_specs=[state] * 3,
        scratch_shapes=[pltpu.VMEM((block * deep * 2, lanes), jnp.float32)],
        cost_estimate=pl.CostEstimate(flops=20 * weight.size, bytes_accessed=28 * weight.size, transcendentals=0),
        name="adam_pairs",
    )(seen(weight), seen(first), seen(second), *grads)
    return [
        result.reshape(rows, deep, 2, lanes).transpose(0, 2, 1, 3).reshape(rows, 2, columns) for result in results
    ]


def adam_planes(weight, first, second, grad):
    rows, planes, columns = weight.shape

    def seen(array):
        return array.transpose(1, 0, 2).reshape(planes * rows, columns)

    results = adam_rows(seen(weight), seen(first), seen(second), [grad], planes)
    return [result.reshape(planes, rows, columns).transpose(1, 0, 2) for result in results]


def shards(
    tokens,
    bounds,
    cotangent,
    entry_weight,
    entry_first,
    entry_second,
    exit_weight,
    exit_first,
    exit_second,
    expand_weight,
    expand_first,
    expand_second,
    shrink_weight,
    shrink_first,
    shrink_second,
    conv_kernel,
    conv_first,
    conv_second,
    norm_gains,
    gain_first,
    gain_second,
):
    rows_dev = tokens.shape[0]
    channels = tokens.shape[1]
    count = lax.axis_size("seq")
    small = jnp.concatenate([conv_kernel, norm_gains], axis=0)
    small = jnp.pad(small, ((0, 64 - small.shape[0]), (0, 128 - small.shape[1]))).astype(LOW)
    entry_low = entry_weight.reshape(entry_weight.shape[0], 3 * channels).astype(LOW)
    hidden_half = shrink_weight.shape[1] // 2
    halves = (slice(0, hidden_half), slice(hidden_half, 2 * hidden_half))
    gate_low = [expand_weight[:, 0, half].astype(LOW) for half in halves]
    up_low = [expand_weight[:, 1, half].astype(LOW) for half in halves]
    shrink_low = [shrink_weight[:, half].astype(LOW) for half in halves]
    gate_full, up_full, shrink_full = [None] * 2, [None] * 2, [None] * 2
    gate_rows, up_rows, activation = [None] * 2, [None] * 2, [None] * 2
    gate_grad, up_grad = [None] * 2, [None] * 2
    shrink_part, gate_part, up_part = [None] * 2, [None] * 2, [None] * 2
    idle = NoJob()

    tokens_f = tokens.astype(jnp.float32)
    bound = jnp.broadcast_to(bounds[0], (8, 128))

    tokens_blocks = gather_blocks(tokens)
    exit_full, small_full = run_ring(GatherRing([exit_weight.astype(LOW), small]), idle, 0)
    small_full = small_full.reshape(count, 64, 128)[:, :8, : conv_kernel.shape[1]]
    small_full = small_full.swapaxes(0, 1).reshape(8, channels).astype(jnp.float32)
    taps = small_full
    gains_row = small_full[3:5]
    gain_blocks = share_small(jnp.broadcast_to(gains_row[0:1], (8, channels)))
    entry_low, small_full = tie(entry_low, small_full)
    (entry_full,) = run_ring(GatherRing([entry_low]), idle, 14)
    entry_full, exit_full = flat(entry_full), flat(exit_full)
    tokens_blocks, entry_full, gain_blocks = tie(tokens_blocks, entry_full, gain_blocks)
    cot_own, cotangent_rows, gate_low[0], entry_full = tie(turned(cotangent), cotangent, gate_low[0], entry_full)
    full, projected, conv_out, gated_rows, halo, mixer_rows, branch_term, scales, normed_one = run_ring(
        GatherRing([gate_low[0]]), EntryJob(tokens_blocks, gain_blocks, entry_full, exit_full, taps, bound), 1
    )
    scale_one = scales[:, :1]
    gate_full[0] = flat(full)
    branch_term, up_low[0] = tie(branch_term, up_low[0])
    (full,) = run_ring(GatherRing([up_low[0]]), idle, 2)
    branch, up_full[0] = tie(reduce_branch(branch_term), flat(full))
    residual = tokens_f + branch
    own_normed_two, scale_two = norm_forward(residual, gains_row[1])
    own_normed_two = with_layout_constraint(own_normed_two, Layout(major_to_minor=(0, 1)))
    own_normed_two, gate_low[1] = tie(own_normed_two, gate_low[1])
    (full,) = run_ring(GatherRing([gate_low[1]]), idle, 3)
    normed_blocks, gate_full[1] = tie(gather_blocks(own_normed_two), flat(full))
    own_normed_two, up_low[1] = tie(turned(own_normed_two), up_low[1])
    full, gate_rows[0], up_rows[0], activation[0] = run_ring(
        GatherRing([up_low[1]]), ExpandJob(normed_blocks, gate_full[0], up_full[0]), 4
    )
    normed_two, up_full[1] = tie(gather_rows(own_normed_two), flat(full))
    cotangent_rows, shrink_low[0], normed_two = tie(cotangent_rows, shrink_low[0], normed_two)
    full, gate_rows[1], up_rows[1], activation[1] = run_ring(
        GatherRing([shrink_low[0]]), ExpandJob(normed_blocks, gate_full[1], up_full[1]), 5
    )
    cot_blocks, shrink_full[0] = tie(gather_blocks(cotangent_rows), flat(full))
    cot_own, shrink_low[1], cot_blocks = tie(cot_own, shrink_low[1], cot_blocks)
    full, gate_grad[0], up_grad[0] = run_ring(
        GatherRing([shrink_low[1]]), HiddenGradJob(cot_blocks, shrink_full[0], gate_rows[0], up_rows[0]), 6
    )
    cot_full, shrink_full[1] = tie(gather_rows(cot_own), flat(full))
    shrink_part[0], gate_grad[1], up_grad[1] = run_ring(
        ScatterRing([(cot_full, activation[0])]),
        HiddenGradJob(cot_blocks, shrink_full[1], gate_rows[1], up_rows[1]),
        7,
    )
    shrink_part[1], two_term = run_ring(
        ScatterRing([(cot_full, activation[1])]), WidthJob(gate_grad + up_grad, gate_full + up_full), 8
    )
    two_term, gate_grad[0] = tie(two_term, gate_grad[0])
    gate_part[0], mixed_term = run_ring(
        ScatterRing([(normed_two, gate_grad[0])]), WidthJob(activation, shrink_full), 9
    )
    grad_normed_two, gate_part[0], mixed_term = tie(reduce_branch(two_term), gate_part[0], mixed_term)
    residual_norm_grad, gain_two_grad = norm_backward(grad_normed_two, residual, scale_two, gains_row[1])
    residual_grad = cotangent.astype(jnp.float32) + residual_norm_grad
    branch_own = with_layout_constraint(residual_grad.astype(LOW), Layout(major_to_minor=(0, 1)))
    branch_own, up_grad[0] = tie(branch_own, up_grad[0])
    (up_part[0],) = run_ring(ScatterRing([(normed_two, up_grad[0])]), idle, 10)
    branch_blocks, up_part[0] = tie(gather_blocks(branch_own), up_part[0])
    branch_own, mixed_term, gate_grad[1], branch_blocks = tie(
        turned(branch_own), mixed_term, gate_grad[1], branch_blocks
    )
    gate_part[1], projected_grad, one_term, taps_grad = run_ring(
        ScatterRing([(normed_two, gate_grad[1])]),
        MixerGradJob(branch_blocks, exit_full, entry_full, projected, conv_out, gated_rows, halo, taps, bound),
        11,
    )
    mixed_branch, gate_part[1], branch_full = tie(reduce_branch(mixed_term), gate_part[1], gather_rows(branch_own))
    mixed = (residual + mixed_branch).astype(LOW)
    one_term, up_grad[1], mixed_branch = tie(one_term, up_grad[1], mixed_branch)
    (up_part[1],) = run_ring(ScatterRing([(normed_two, up_grad[1])]), idle, 12)
    grad_normed_one, up_part[1] = tie(reduce_branch(one_term), up_part[1])
    tokens_norm_grad, gain_one_grad = norm_backward(grad_normed_one, tokens_f, scale_one, gains_row[0])
    tokens_grad = residual_grad + tokens_norm_grad
    small_grad = jnp.concatenate([taps_grad[:3], gain_one_grad[None], gain_two_grad[None]], axis=0)
    small_blocks = small_grad.reshape(5, count, conv_kernel.shape[1]).swapaxes(0, 1)
    small_blocks = jnp.pad(small_blocks, ((0, 0), (0, 3), (0, 128 - conv_kernel.shape[1])))
    entry_part, exit_part, small_part = run_ring(
        ScatterRing([(normed_one, projected_grad), (branch_full, mixer_rows)]), SmallSumJob(small_blocks), 13
    )
    kernel_part = small_part[:3, : conv_kernel.shape[1]]
    gains_part = small_part[3:5, : conv_kernel.shape[1]]
    entry_next, entry_first_next, entry_second_next = adam_planes(
        entry_weight, entry_first, entry_second, entry_part
    )
    exit_next, exit_first_next, exit_second_next = adam_rows(exit_weight, exit_first, exit_second, [exit_part])
    expand_next, expand_first_next, expand_second_next = adam_pairs(
        expand_weight, expand_first, expand_second, [gate_part[0], up_part[0], gate_part[1], up_part[1]]
    )
    shrink_next, shrink_first_next, shrink_second_next = adam_rows(
        shrink_weight, shrink_first, shrink_second, shrink_part
    )
    conv_next, conv_first_next, conv_second_next = adam_update(
        conv_kernel, conv_first, conv_second, kernel_part, RATE_CONV, 0.0
    )
    gains_next, gains_first_next, gains_second_next = adam_update(
        norm_gains, gain_first, gain_second, gains_part, RATE_GAIN, 0.0
    )
    return (
        mixed,
        tokens_grad,
        entry_next,
        entry_first_next,
        entry_second_next,
        exit_next,
        exit_first_next,
        exit_second_next,
        expand_next,
        expand_first_next,
        expand_second_next,
        shrink_next,
        shrink_first_next,
        shrink_second_next,
        conv_next,
        conv_first_next,
        conv_second_next,
        gains_next,
        gains_first_next,
        gains_second_next,
    )


def solution(mesh):
    rows = P("seq", "tp")
    stacked = P("seq", None, "tp")
    small = P(None, ("tp", "seq"))
    return jax.shard_map(
        shards,
        mesh=mesh,
        in_specs=(rows, P("seq"), rows) + (stacked,) * 3 + (rows,) * 3 + (stacked,) * 3 + (rows,) * 3 + (small,) * 6,
        out_specs=(rows, rows) + (stacked,) * 3 + (rows,) * 3 + (stacked,) * 3 + (rows,) * 3 + (small,) * 6,
        check_vma=False,
    )
```

time: 2340 us -> 894 us (0.38)
  waiting for transfers between devices: 1920 us -> 22.1 us
  Pallas kernels: 0 us -> 776 us
  matrix products: 182 us -> 0 us
  local copies, waits for them, and re-layouts: 81.6 us -> 16.8 us
  blocking collectives: 63.1 us -> 17.4 us
  other arithmetic: 64.6 us -> 34.5 us
    reduce_scatter x9 -> x4, waiting for transfers between devices: 1320 us -> 1.44 us  [reduce_branch(): lax.psum_scatter(term, 'tp', scatter_dimension=0, tiled=True)]
    pallas_call x0 -> x19, Pallas kernels: none -> 776 us  [the longest x15 743 us: run_ring(): pl.pallas_call(functools.partial(ring_kernel, ring, job), out_shape=outs,...]
    all_gather x8 -> x7, waiting for transfers between devices: 516 us -> 19.3 us  [gather_rows(): return lax.all_gather(own, 'tp', axis=0, tiled=True)]
    dot_general x13 -> x0, matrix products: 182 us -> none  [the longest x5 67.1 us: contract_rows(): lax.dot_general(left, right, (((0,), (0,)), ((), ())), preferred_element_...]
    unnamed x21 -> x11, waiting for transfers between devices: 81 us -> 1.36 us
    unnamed x106 -> x23, local copies, waits for them, and re-layouts: 45.2 us -> 6.37 us
    all_gather x2 -> x0, blocking collectives: 38.7 us -> none  [the longest x1 22.3 us: shards(): lax.all_gather(low_weights[5], 'seq', axis=1, tiled=True)]
    all_gather x2 -> x0, local copies, waits for them, and re-layouts: 31.5 us -> none  [the longest x1 22.6 us: shards(): lax.all_gather(low_weights[2], 'seq', axis=0, tiled=True)]
  transfers between devices with their start and end apart: 21 -> 14, of which waited for: 21 -> 2; matrix products, arithmetic and copies ran while one was open for 10% -> 3% of each run, Pallas kernels for 0% -> 58%
where the time goes in v3:
time: 894 us; the launch traced here: 885 us
  Pallas kernels  776 us (87%)
  other arithmetic  34.5 us (4%)
  waiting for transfers between devices  22.1 us (2%)
  blocking collectives  17.4 us (2%)
  local copies, waits for them, and re-layouts  16.8 us (2%)
  between operations  15.5 us (2%)
    pallas_call x15, Pallas kernels, run_ring(): pl.pallas_call(functools.partial(ring_kernel, ring, job), out_shape=outs,...  743 us
    all_gather x7, waiting for transfers between devices, gather_rows(): return lax.all_gather(own, 'tp', axis=0, tiled=True)  19.3 us
    pallas_call x3, Pallas kernels, adam_rows(): pl.pallas_call(functools.partial(adam_kernel, len(grads)), out_shape=[jax...  18.2 us
  transfers between devices with their start and end apart: 14, of which 2 were waited for; matrix products, arithmetic and copies ran while one was open for 3% of the time, Pallas kernels for 58%

profile of v3, /device:TPU:0, one launch (start us, length us, event | category | flops | bytes accessed | tf_op | source)
XLA Modules:
  0.0 885.2 jit_solution(14688647236218782707)
XLA Ops:
  11.7 34.3 %ring_gather.8 = (bf16[8,256,512]{2,1,0:T(8,128)(2,1)}, bf16[8,64,128]{2,1,0:T(8,128)(2,1)}) custom-call(bf16[256,512]{1,0:T(8,128)(2,1)} %convert_element_type.70.refs_0_, bf16[64,128]{1,0:T(8,128)(2,1)} %fusion.13.refs_1_), custom_call_target="tpu_custom_call" | custom-call | bytes 44564480 | tf_op jit(solution)/shard_map/ring_gather/pallas_call | solution.py:810
  48.6 4.4 copy.68
  58.9 63.0 %ring_gather.9 = bf16[8,256,1536]{2,1,0:T(8,128)(2,1)} custom-call(bf16[256,1536]{1,0:T(8,128)(2,1)} %copy.57.refs_0_), custom_call_target="tpu_custom_call" | custom-call | bytes 125829120 | tf_op jit(solution)/shard_map/ring_gather/pallas_call | solution.py:810
  123.2 47.7 %ring_gather.10 = (bf16[8,256,1024]{2,1,0:T(8,128)(2,1)}, f32[1024,1536]{1,0:T(8,128)}, f32[1024,512]{1,0:T(8,128)}, bf16[1024,512]{1,0:T(8,128)(2,1)}, bf16[16,...) custom-call(bf16[256,1024]{1,0:T(8,128)(2,1)} %get-tuple-element.121, ...), custom_call_target="tpu_custom_call" | custom-call | flops 8589934592 | bytes 83886080 | tf_op jit(solution)/shard_map/ring_gather/pallas_call | solution.py:810
  171.1 41.7 %ring_gather.11 = bf16[8,256,1024]{2,1,0:T(8,128)(2,1)} custom-call(bf16[256,1024]{1,0:T(8,128)(2,1)} %get-tuple-element.128.refs_0_), custom_call_target="tpu_custom_call" | custom-call | bytes 83886080 | tf_op jit(solution)/shard_map/ring_gather/pallas_call | solution.py:810
  216.1 5.8 psum.21
  223.2 2.3 copy.58
  228.8 44.0 %ring_gather.12 = bf16[8,256,1024]{2,1,0:T(8,128)(2,1)} custom-call(bf16[256,1024]{1,0:T(8,128)(2,1)} %get-tuple-element.135.refs_0_), custom_call_target="tpu_custom_call" | custom-call | bytes 83886080 | tf_op jit(solution)/shard_map/ring_gather/pallas_call | solution.py:810
  272.9 42.7 %ring_gather.13 = (bf16[8,256,1024]{2,1,0:T(8,128)(2,1)}, f32[1024,1024]{1,0:T(8,128)}, f32[1024,1024]{1,0:T(8,128)}, bf16[1024,1024]{1,0:T(8,128)(2,1)}) custom-call(bf16[256,1024]{1,0:T(8,128)(2,1)} %get-tuple-element.134.refs_0_, bf16[4,1024,512]{2,1,0:T(8,128)(2,1)} %bitcast.113, bf16[2048,1024]{1,0:T(8,128)(2,1)} %bitcast.126, bf16[2048,1024]{1,0:T(8,128)(2,1)} %bitcast.88), custom_call_target="tpu_custom_call" | custom-call | flops 8589934592 | bytes 83886080 | tf_op jit(solution)/shard_map/ring_gather/pallas_call | solution.py:810
  315.7 42.4 %ring_gather.14 = (bf16[8,256,1024]{2,1,0:T(8,128)(2,1)}, f32[1024,1024]{1,0:T(8,128)}, f32[1024,1024]{1,0:T(8,128)}, bf16[1024,1024]{1,0:T(8,128)(2,1)}) custom-call(bf16[256,1024]{1,0:T(8,128)(2,1)} %get-tuple-element.142.refs_0_, bf16[4,1024,512]{2,1,0:T(8,128)(2,1)} %bitcast.114, bf16[2048,1024]{1,0:T(8,128)(2,1)} %bitcast.90, bf16[2048,1024]{1,0:T(8,128)(2,1)} %bitcast.128), custom_call_target="tpu_custom_call" | custom-call | flops 8589934592 | bytes 83886080 | tf_op jit(solution)/shard_map/ring_gather/pallas_call | solution.py:810
  358.2 41.8 %ring_gather.15 = (bf16[8,256,1024]{2,1,0:T(8,128)(2,1)}, bf16[1024,1024]{1,0:T(8,128)(2,1)}, bf16[1024,1024]{1,0:T(8,128)(2,1)}) custom-call(bf16[256,1024]{1,0:T(8,128)(2,1)} %get-tuple-element.148.refs_0_, bf16[4,1024,512]{2,1,0:T(8,128)(2,1)} %bitcast.99, bf16[2048,1024]{1,0:T(8,128)(2,1)} %bitcast.97, f32[1024,1024]{1,0:T(8,128)} %get-tuple-element.151.refs_3_, ...), custom_call_target="tpu_custom_call" | custom-call | flops 4294967296 | bytes 83886080 | tf_op jit(solution)/shard_map/ring_gather/pallas_call | solution.py:810
  400.0 46.5 %ring_scatter.7 = (f32[256,1024]{1,0:T(8,128)}, bf16[1024,1024]{1,0:T(8,128)(2,1)}, bf16[1024,1024]{1,0:T(8,128)(2,1)}) custom-call(bf16[2048,1024]{1,0:T(8,128)(2,1)} %all-gather.16.cloned.1.call-done.refs_0_, bf16[1024,1024]{1,0:T(8,128)(2,1)} %get-tuple-element.157.refs_1_.refs_2_, bf16[4,1024,512]{2,1,0:T(8,128)(2,1)} %bitcast.100, ...), custom_call_target="tpu_custom_call" | custom-call | flops 8589934592 | bytes 83886080 | tf_op jit(solution)/shard_map/ring_scatter/pallas_call | solution.py:810
  446.5 51.7 %ring_scatter.8 = (f32[256,1024]{1,0:T(8,128)}, bf16[4096,512]{1,0:T(8,128)(2,1)}) custom-call(bf16[2048,1024]{1,0:T(8,128)(2,1)} %all-gather.16.cloned.1.call-done.refs_0_, bf16[1024,1024]{1,0:T(8,128)(2,1)} %get-tuple-element.155.refs_1_.refs_3_, bf16[1024,1024]{1,0:T(8,128)(2,1)} %get-tuple-element.167.refs_2_.refs_1_, ...), custom_call_target="tpu_custom_call" | custom-call | flops 21474836480 | bytes 83886080 | tf_op jit(solution)/shard_map/ring_scatter/pallas_call | solution.py:810
  498.5 46.1 %ring_scatter.9 = (f32[256,1024]{1,0:T(8,128)}, bf16[4096,512]{1,0:T(8,128)(2,1)}) custom-call(bf16[2048,1024]{1,0:T(8,128)(2,1)} %all-gather.10.cloned.1.call-done.refs_0_, bf16[1024,1024]{1,0:T(8,128)(2,1)} %get-tuple-element.167.refs_2_.refs_1_, bf16[1024,1024]{1,0:T(8,128)(2,1)} %get-tuple-element.157.refs_1_.refs_2_, ...), custom_call_target="tpu_custom_call" | custom-call | flops 12884901888 | bytes 83886080 | tf_op jit(solution)/shard_map/ring_scatter/pallas_call | solution.py:810
  544.6 2.8 convert_element_type.80
  547.4 2.2 multiply_reduce_fusion
  549.6 5.7 psum.22
  555.3 3.4 fusion.18
  558.8 2.3 copy.59
  561.1 46.4 %ring_scatter.10.refs_4_ = f32[256,1024]{1,0:T(8,128)} custom-call(bf16[2048,1024]{1,0:T(8,128)(2,1)} %all-gather.10.cloned.1.call-done.refs_0_, bf16[1024,1024]{1,0:T(8,128)(2,1)} %get-tuple-element.173.refs_4_.refs_1_), custom_call_target="tpu_custom_call" | custom-call | flops 4294967296 | bytes 83886080 | tf_op jit(solution)/shard_map/ring_scatter/pallas_call | solution.py:810
  608.3 57.1 %ring_scatter.11 = (f32[256,1024]{1,0:T(8,128)}, bf16[1024,1536]{1,0:T(8,128)(2,1)}, bf16[4096,512]{1,0:T(8,128)(2,1)}, f32[8,512]{1,0:T(8,128)}) custom-call(bf16[2048,1024]{1,0:T(8,128)(2,1)} %all-gather.10.cloned.1.call-done.refs_0_, bf16[1024,1024]{1,0:T(8,128)(2,1)} %get-tuple-element.176.refs_3_.refs_1_, bf16[4,1024,512]{2,1,0:T(8,128)(2,1)} %bitcast.118, ...), custom_call_target="tpu_custom_call" | custom-call | flops 12884901888 | bytes 83886080 | tf_op jit(solution)/shard_map/ring_scatter/pallas_call | solution.py:810
  665.5 2.8 convert_element_type.82
  668.3 19.2 %all-gather.20.cloned.1.call-done.refs_1_ = bf16[2048,1024]{1,0:T(8,128)(2,1)} async-done(((bf16[512,1024]{1,0:T(8,128)(2,1)}), bf16[2048,1024]{1,0:T(8,128)(2,1)}) %all-gather.20.cloned.1.call-update) | async-done | bytes 4194320 | tf_op jit(solution)/shard_map/all_gather | solution.py:845
  688.9 9.0 %adam_rows.5 = (f32[256,2048]{1,0:T(8,128)}, f32[256,2048]{1,0:T(8,128)}, f32[256,2048]{1,0:T(8,128)}) custom-call(f32[256,2048]{1,0:T(8,128)} %refs_0_.3, f32[256,2048]{1,0:T(8,128)} %refs_1_.3, f32[256,2048]{1,0:T(8,128)} %refs_2_.3, f32[256,1024]{1,0:T(8,128)} %get-tuple-element.210.refs_3_, f32[256,1024]{1,0:T(8,128)} %get-tuple-element.211.refs_4_), custom_call_target="tpu_custom_call" | custom-call | flops 10485760 | bytes 14680064 | tf_op jit(solution)/shard_map/adam_rows/pallas_call | solution.py:909
  698.1 3.4 add_convert_fusion
  701.5 47.3 %ring_scatter.12.refs_6_ = f32[256,1024]{1,0:T(8,128)} custom-call(bf16[2048,1024]{1,0:T(8,128)(2,1)} %all-gather.10.cloned.1.call-done.refs_0_, bf16[1024,1024]{1,0:T(8,128)(2,1)} %get-tuple-element.188.refs_5_.refs_1_), custom_call_target="tpu_custom_call" | custom-call | flops 4294967296 | bytes 83886080 | tf_op jit(solution)/shard_map/ring_scatter/pallas_call | solution.py:810
  751.3 6.0 psum.23
  757.9 89.9 %ring_scatter.13 = (f32[256,1536]{1,0:T(8,128)}, f32[256,512]{1,0:T(8,128)}, f32[8,128]{1,0:T(8,128)}) custom-call(bf16[2048,1024]{1,0:T(8,128)(2,1)} %get-tuple-element.190.refs_0_, bf16[2048,1024]{1,0:T(8,128)(2,1)} %all-gather.20.cloned.1.call-done.refs_1_, bf16[1024,1536]{1,0:T(8,128)(2,1)} %get-tuple-element.192.refs_2_, ...), custom_call_target="tpu_custom_call" | custom-call | flops 8589934592 | bytes 167772160 | tf_op jit(solution)/shard_map/ring_scatter/pallas_call | solution.py:810
  850.5 3.5 fusion.3
  854.0 2.6 adam_rows.4
  856.6 6.6 adam_rows.3
  863.2 15.0 %adam_pairs.1 = (f32[8192,128]{1,0:T(8,128)}, f32[8192,128]{1,0:T(8,128)}, f32[8192,128]{1,0:T(8,128)}) custom-call(f32[8192,128]{1,0:T(8,128)} %bitcast.84, f32[8192,128]{1,0:T(8,128)} %bitcast.95, f32[8192,128]{1,0:T(8,128)} %bitcast.96, f32[256,1024]{1,0:T(8,128)} %get-tuple-element.203.refs_3_, f32[256,1024]{1,0:T(8,128)} %ring_scatter.10.refs_4_, ...), custom_call_target="tpu_custom_call" | custom-call | flops 20971520 | bytes 29360128 | tf_op jit(solution)/shard_map/adam_pairs/pallas_call | solution.py:945
  (96 shorter events, 30.1 us)
Async XLA Ops:
  7.2 115.4 %all-gather.8.cloned.1.call-start = ((), (), s32[]{:S(2)}) async-start(), calls=%async_computation.4 | async-start | bytes 5242880 | tf_op jit(solution)/shard_map/all_gather | solution.py:845
  7.9 206.3 %reduce-scatter.5.cloned.1.call-start = ((), (), s32[]{:S(2)}) async-start(), calls=%async_computation.5 | async-start | bytes 5242880 | tf_op jit(solution)/shard_map/reduce_scatter | solution.py:857
  46.9 75.0 %collective-permute-start.2 = (f32[8,512]{1,0:T(8,128)S(1)}, f32[8,512]{1,0:T(8,128)S(1)}, u32[]{:S(2)}, u32[]{:S(2)}) collective-permute-start(f32[8,512]{1,0:T(8,128)S(1)} %broadcast_in_dim.19), channel_id=1, source_target_pairs={{0,3},{1,0},{2,1},{3,2},{4,7},{5,4},{6,5},{7,6},{8,11},{9,8},{10,9... | collective-permute-start | bytes 49160 | tf_op jit(solution)/shard_map/ppermute | solution.py:863
  46.9 75.0 %collective-permute-start.1 = (f32[8,512]{1,0:T(8,128)S(1)}, f32[8,512]{1,0:T(8,128)S(1)}, u32[]{:S(2)}, u32[]{:S(2)}) collective-permute-start(f32[8,512]{1,0:T(8,128)S(1)} %broadcast_in_dim.19), channel_id=1, source_target_pairs={{0,2},{1,3},{2,0},{3,1},{4,6},{5,7},{6,4},{7,5},{8,10},{9,11},{10,... | collective-permute-start | bytes 49160 | tf_op jit(solution)/shard_map/ppermute | solution.py:863
  48.5 73.5 %collective-permute-start = (f32[8,512]{1,0:T(8,128)S(1)}, f32[8,512]{1,0:T(8,128)S(1)}, u32[]{:S(2)}, u32[]{:S(2)}) collective-permute-start(f32[8,512]{1,0:T(8,128)S(1)} %broadcast_in_dim.19), channel_id=1, source_target_pairs={{0,1},{1,2},{2,3},{3,0},{4,5},{5,6},{6,7},{7,4},{8,9},{9,10},{10,1... | collective-permute-start | bytes 49160 | tf_op jit(solution)/shard_map/ppermute | solution.py:863
  53.1 2.2 copy-start.2
  54.4 1.4 copy-start.1
  171.0 101.9 %all-gather.12.cloned.1.call-start = ((), (), s32[]{:S(2)}) async-start(), calls=%async_computation.7 | async-start | bytes 5242880 | tf_op jit(solution)/shard_map/all_gather | solution.py:845
  212.8 2.9 copy-start
  223.1 92.5 %all-gather.10.cloned.1.call-start = ((), (), s32[]{:S(2)}) async-start(), calls=%async_computation.6 | async-start | bytes 5242880 | tf_op jit(solution)/shard_map/all_gather | solution.py:845
  225.5 132.6 %all-gather.14.cloned.1.call-start = ((), (), s32[]{:S(2)}) async-start(), calls=%async_computation.8 | async-start | bytes 5242880 | tf_op jit(solution)/shard_map/all_gather | solution.py:845
  315.7 84.3 %all-gather.16.cloned.1.call-start = ((), (), s32[]{:S(2)}) async-start(), calls=%async_computation.9 | async-start | bytes 5242880 | tf_op jit(solution)/shard_map/all_gather | solution.py:845
  358.1 186.5 %reduce-scatter.7.cloned.1.call-start = ((), (), s32[]{:S(2)}) async-start(), calls=%async_computation.10 | async-start | bytes 5242880 | tf_op jit(solution)/shard_map/reduce_scatter | solution.py:857
  498.2 109.2 %all-gather.18.cloned.1.call-start = ((), (), s32[]{:S(2)}) async-start(), calls=%async_computation.11 | async-start | bytes 5242880 | tf_op jit(solution)/shard_map/all_gather | solution.py:845
  558.7 106.8 %reduce-scatter.9.cloned.1.call-start = ((), (), s32[]{:S(2)}) async-start(), calls=%async_computation.12 | async-start | bytes 5242880 | tf_op jit(solution)/shard_map/reduce_scatter | solution.py:857
  607.5 80.0 %all-gather.20.cloned.1.call-start = ((), (), s32[]{:S(2)}) async-start(), calls=%async_computation.13 | async-start | bytes 5242880 | tf_op jit(solution)/shard_map/all_gather | solution.py:845
  608.1 140.7 %reduce-scatter.11.cloned.1.call-start = ((), (), s32[]{:S(2)}) async-start(), calls=%async_computation.14 | async-start | bytes 5242880 | tf_op jit(solution)/shard_map/reduce_scatter | solution.py:857
  688.9 9.1 %copy-start.4 = (f32[8,512]{1,0:T(8,128)S(1)}, f32[8,512]{1,0:T(8,128)}, u32[]{:S(2)}) copy-start(f32[8,512]{1,0:T(8,128)} %get-tuple-element.194) | copy-start | bytes 49156
  757.9 90.0 %copy-start.7 = (f32[2,64]{1,0:T(2,128)S(1)}, f32[2,64]{1,0:T(2,128)}, u32[]{:S(2)}) copy-start(f32[2,64]{1,0:T(2,128)} %param.39) | copy-start | bytes 1540
  757.9 90.0 %copy-start.8 = (f32[2,64]{1,0:T(2,128)S(1)}, f32[2,64]{1,0:T(2,128)}, u32[]{:S(2)}) copy-start(f32[2,64]{1,0:T(2,128)} %param.40) | copy-start | bytes 1540
  757.9 90.0 %copy-start.9 = (f32[2,64]{1,0:T(2,128)S(1)}, f32[2,64]{1,0:T(2,128)}, u32[]{:S(2)}) copy-start(f32[2,64]{1,0:T(2,128)} %param.41) | copy-start | bytes 1540
  757.9 91.3 %copy-start.3 = (f32[3,64]{1,0:T(4,128)S(1)}, f32[3,64]{1,0:T(4,128)}, u32[]{:S(2)}) copy-start(f32[3,64]{1,0:T(4,128)} %param.36) | copy-start | bytes 2308
  757.9 91.3 %copy-start.5 = (f32[3,64]{1,0:T(4,128)S(1)}, f32[3,64]{1,0:T(4,128)}, u32[]{:S(2)}) copy-start(f32[3,64]{1,0:T(4,128)} %param.37) | copy-start | bytes 2308
  757.9 91.3 %copy-start.6 = (f32[3,64]{1,0:T(4,128)S(1)}, f32[3,64]{1,0:T(4,128)}, u32[]{:S(2)}) copy-start(f32[3,64]{1,0:T(4,128)} %param.38) | copy-start | bytes 2308
Sparse Core Ops, SparseCore 0:
  9.6 37.1 all-gather.7
  171.1 43.0 reduce-scatter.4
  223.2 35.5 all-gather.11
  260.9 34.4 all-gather.9
  315.8 35.0 all-gather.13
  358.2 35.9 all-gather.15
  498.4 43.7 reduce-scatter.6
  558.9 33.7 all-gather.17
  607.6 43.2 reduce-scatter.8
  653.0 34.4 all-gather.19
  690.2 44.5 reduce-scatter.10

commit v4 on v3

--- a/solution.py
+++ b/solution.py
@@ -4,7 +4,6 @@
 import jax.numpy as jnp
 from jax import lax
 from jax.experimental import pallas as pl
-from jax.experimental.layout import Layout, with_layout_constraint
 from jax.experimental.pallas import tpu as pltpu
 from jax.sharding import PartitionSpec as P
 
@@ -23,6 +22,7 @@
 
 MESH = pl.DeviceIdType.MESH
 LOW = jnp.bfloat16
+LANES = 128
 VMEM_BYTES = 60 * 1024 * 1024
 
 
@@ -160,7 +160,7 @@
             + [pltpu.VMEM(right.shape, right.dtype) for right in rights]
             + [pltpu.VMEM((2, count, row, width // 2), LOW) for row, width in zip(self.rows, self.columns)]
             + [pltpu.VMEM((row, width), jnp.float32) for row, width in zip(self.rows, self.columns)]
-            + [sems, sems, pltpu.SemaphoreType.DMA((self.arrays, 2)), pltpu.SemaphoreType.DMA((self.arrays,))]
+            + [sems, sems, pltpu.SemaphoreType.DMA((self.arrays, count + 1)), pltpu.SemaphoreType.DMA((self.arrays,))]
         )
         self.flops = sum(2 * left.size * width for left, width in zip(lefts, self.columns))
         self.bytes = 20 * sum(left.shape[0] * width * 2 for left, width in zip(lefts, self.columns))
@@ -205,31 +205,43 @@
             device_id_type=MESH,
         )
 
-    def loads(self):
-        return [
-            pltpu.make_async_copy(
-                self.in_refs[array + side * self.arrays],
-                (self.rights if side else self.lefts)[array],
-                self.load_sem.at[array, side],
-            )
-            for array in range(self.arrays)
-            for side in range(2)
-        ]
+    def right_load(self, array):
+        return pltpu.make_async_copy(
+            self.in_refs[array + self.arrays], self.rights[array], self.load_sem.at[array, self.count]
+        )
+
+    def left_load(self, array, step):
+        owner = ring_index((self.place + 2 * self.count - 1 - step) % self.count, self.count)
+        rows = pl.ds(pl.multiple_of(owner * self.rows[array], 16), self.rows[array])
+        return pltpu.make_async_copy(
+            self.in_refs[array].at[rows], self.lefts[array].at[rows], self.load_sem.at[array, step]
+        )
 
     def peers(self):
         return [(self.ahead, self.column), (self.behind, self.column)]
 
     def prepare(self):
-        for load in self.loads():
-            load.start()
+        for array in range(self.arrays):
+            self.right_load(array).start()
+            for step in (0, self.count - 2):
+                self.left_load(array, step).start()
 
     def start(self):
-        for load in self.loads():
-            load.wait()
-        for part in range(self.parts):
-            for array, way in self.pieces():
-                self.held(array, way, part, 0)[...] = self.term(array, way, part, 0).astype(LOW)
-                self.copy(array, way, part, 0).start()
+        later = list(range(1, self.count - 2)) + [self.count - 1]
+        for array in range(self.arrays):
+            for step in later:
+                self.left_load(array, step).start()
+        for array in range(self.arrays):
+            self.right_load(array).wait()
+            for step in (0, self.count - 2):
+                self.left_load(array, step).wait()
+            for part in range(self.parts):
+                for way in range(2):
+                    self.held(array, way, part, 0)[...] = self.term(array, way, part, 0).astype(LOW)
+                    self.copy(array, way, part, 0).start()
+        for array in range(self.arrays):
+            for step in later:
+                self.left_load(array, step).wait()
 
     def tick(self, index):
         step, part = 1 + index // self.parts, index % self.parts
@@ -406,11 +418,12 @@
 
 
 class WidthJob(Job):
-    def __init__(self, lefts, weights):
+    def __init__(self, lefts, weights, before=None):
         rows, width = lefts[0].shape[0], weights[0].shape[0]
         flops = 2 * rows * sum(weight.size for weight in weights)
         self.own = width // lax.axis_size("tp")
         self.height = rows
+        self.before = before
         out = ((rows * lax.axis_size("tp"), self.own), LOW)
         super().__init__(lefts, [(weight, 0) for weight in weights], [out], width // self.wide, flops)
 
@@ -419,7 +432,8 @@
 
     def compute(self, whole, tiles):
         total = None
-        for left, weight in zip(whole, tiles):
+        lefts = list(whole) + (list(self.before.outs_v) if self.before else [])
+        for left, weight in zip(lefts, tiles):
             term = contract_cols(left[...], weight)
             total = term if total is None else total + term
         return (total.astype(LOW),)
@@ -709,25 +723,320 @@
             term[window] = contract_cols(grads[...], entry[features, :]).astype(LOW)
 
 
+class Jobs:
+    def __init__(self, *jobs):
+        self.jobs = jobs
+        self.inputs = [item for job in jobs for item in job.inputs]
+        self.out_shapes = [item for job in jobs for item in job.out_shapes]
+        self.scratch = [item for job in jobs for item in job.scratch]
+        self.tiles = sum(job.tiles for job in jobs)
+        self.flops = sum(job.flops for job in jobs)
+
+    def bind(self, ins, outs, scratch):
+        groups = zip(
+            self.jobs,
+            split(ins, [len(job.inputs) for job in self.jobs]),
+            split(outs, [len(job.out_shapes) for job in self.jobs]),
+            split(scratch, [len(job.scratch) for job in self.jobs]),
+        )
+        for job, own_ins, own_outs, own_scratch in groups:
+            job.bind(own_ins, own_outs, own_scratch)
+
+    def peers(self):
+        return [peer for job in self.jobs for peer in job.peers()]
+
+    def start(self):
+        for job in self.jobs:
+            job.start()
+
+    def tile(self, index):
+        begin = 0
+        for job in self.jobs:
+            here = index - begin
+
+            @pl.when((here >= 0) & (here < job.tiles))
+            def _(job=job, here=here):
+                job.tile(here)
+
+            begin += job.tiles
+
+    def finish(self):
+        for job in self.jobs:
+            job.finish()
+
+
+class TurnJob(MixerJob):
+    def __init__(self, blocks):
+        parts, rows, own = blocks.shape
+        super().__init__([blocks], [((parts * own, rows), blocks.dtype)], [], [rows // 128], 0)
+
+    def peers(self):
+        return []
+
+    def before(self, phase):
+        self.load(0).wait()
+
+    def after(self, phase):
+        self.store(0).start()
+
+    def work(self, phase, index):
+        (blocks,), (target,) = self.ins_v, self.outs_v
+        parts, _, own = blocks.shape
+        rows = pl.ds(pl.multiple_of(index * 128, 128), 128)
+        for part in range(parts):
+            target[part * own : (part + 1) * own, rows] = blocks[part, rows, :].T
+
+
+class CastJob(MixerJob):
+    def __init__(self, pairs, plain):
+        rows, columns = plain.shape
+        lanes = pairs.shape[1]
+        self.rows, self.half, self.lanes = rows, columns // 2, lanes
+        self.block = max(rows // 8, 16)
+        outs = [((rows, columns // 2), LOW)] * 6
+        super().__init__([pairs, plain], outs, [], [rows // self.block], 0)
+
+    def peers(self):
+        return []
+
+    def before(self, phase):
+        for which in range(2):
+            self.load(which).wait()
+
+    def after(self, phase):
+        for which in range(6):
+            self.store(which).start()
+
+    def work(self, phase, index):
+        pairs, plain = self.ins_v
+        block, half, lanes = self.block, self.half, self.lanes
+        tiles = half // lanes
+        rows = pl.ds(pl.multiple_of(index * block, 16), block)
+        start = index * (block * 4 * tiles)
+        for which in range(4):
+            side, plane = which // 2, which % 2
+            for tile in range(tiles):
+                place = (side * tiles + tile) * 2 + plane
+                picked = pairs[pl.ds(start + place, block, stride=4 * tiles), :]
+                self.outs_v[which][rows, tile * lanes : (tile + 1) * lanes] = picked.astype(LOW)
+        for side in range(2):
+            self.outs_v[4 + side][rows, :] = plain[rows, side * half : (side + 1) * half].astype(LOW)
+
+
+class SmallGatherJob:
+    tiles, flops = 1, 0
+
+    def __init__(self, own):
+        self.inputs = [own]
+        devices, columns = lax.axis_size("seq"), lax.axis_size("tp")
+        whole = (devices, columns) + own.shape
+        self.out_shapes = [jax.ShapeDtypeStruct(whole, own.dtype)]
+        self.scratch = [
+            pltpu.VMEM(whole, own.dtype),
+            pltpu.SemaphoreType.DMA((2,)),
+            pltpu.SemaphoreType.DMA((columns,)),
+            pltpu.SemaphoreType.DMA((columns,)),
+            pltpu.SemaphoreType.DMA((devices,)),
+            pltpu.SemaphoreType.DMA((devices,)),
+        ]
+
+    def bind(self, ins, outs, scratch):
+        self.source, self.target = ins[0], outs[0]
+        self.whole, self.local_sem, self.near_send, self.near_recv, self.far_send, self.far_recv = scratch
+        self.devices, self.columns = lax.axis_size("seq"), lax.axis_size("tp")
+        self.seq, self.column = lax.axis_index("seq"), lax.axis_index("tp")
+
+    def peers(self):
+        near = [(self.seq, (self.column + step) % self.columns) for step in range(1, self.columns)]
+        far = [((self.seq + step) % self.devices, self.column) for step in range(1, self.devices)]
+        return near + far
+
+    def near(self, step):
+        piece = self.whole.at[self.seq, self.column]
+        return pltpu.make_async_remote_copy(
+            src_ref=piece,
+            dst_ref=piece,
+            send_sem=self.near_send.at[step],
+            recv_sem=self.near_recv.at[step],
+            device_id=(self.seq, (self.column + step) % self.columns),
+            device_id_type=MESH,
+        )
+
+    def far(self, step):
+        piece = self.whole.at[self.seq]
+        return pltpu.make_async_remote_copy(
+            src_ref=piece,
+            dst_ref=piece,
+            send_sem=self.far_send.at[step],
+            recv_sem=self.far_recv.at[step],
+            device_id=((self.seq + step) % self.devices, self.column),
+            device_id_type=MESH,
+        )
+
+    def start(self):
+        load = pltpu.make_async_copy(self.source, self.whole.at[self.seq, self.column], self.local_sem.at[0])
+        load.start()
+        load.wait()
+        for step in range(1, self.columns):
+            self.near(step).start()
+
+    def tile(self, index):
+        for step in range(1, self.columns):
+            self.near(step).wait()
+
+        def begin(step, carry):
+            self.far(step).start()
+            return carry
+
+        lax.fori_loop(1, self.devices, begin, 0)
+
+    def finish(self):
+        def end(step, carry):
+            self.far(step).wait()
+            return carry
+
+        lax.fori_loop(1, self.devices, end, 0)
+        store = pltpu.make_async_copy(self.whole, self.target, self.local_sem.at[1])
+        store.start()
+        store.wait()
+
+
+class RowSumJob(MixerJob):
+    block = 128
+
+    def __init__(self, inputs, outs, extra, rows, flops):
+        self.columns = lax.axis_size("tp")
+        blocks = rows // self.block
+        exchange = [
+            pltpu.VMEM((self.columns, blocks, self.block), jnp.float32),
+            pltpu.VMEM((blocks, self.block), jnp.float32),
+            pltpu.SemaphoreType.DMA((self.columns,)),
+            pltpu.SemaphoreType.DMA((self.columns,)),
+        ]
+        super().__init__(inputs, outs, exchange + extra, [blocks, 1, blocks], flops)
+
+    def peers(self):
+        return [(self.seq, (self.column + step) % self.columns) for step in range(1, self.columns)]
+
+    def share(self, step):
+        return pltpu.make_async_remote_copy(
+            src_ref=self.extra_v[0].at[0],
+            dst_ref=self.extra_v[0].at[step],
+            send_sem=self.extra_v[2].at[step],
+            recv_sem=self.extra_v[3].at[step],
+            device_id=(self.seq, (self.column + step) % self.columns),
+            device_id_type=MESH,
+        )
+
+    def before(self, phase):
+        if phase == 0:
+            for which in range(len(self.inputs)):
+                self.load(which).wait()
+
+    def after(self, phase):
+        if phase == 0:
+            for step in range(1, self.columns):
+                self.share(step).start()
+        if phase == 2:
+            for which in range(len(self.out_shapes)):
+                self.store(which).start()
+
+    def finish(self):
+        for step in range(1, self.columns):
+            self.share(step).wait_send()
+        super().finish()
+
+    def work(self, phase, index):
+        block = self.block
+        slots, totals = self.extra_v[:2]
+        rows = pl.ds(pl.multiple_of(index * block, block), block)
+        if phase == 0:
+            part = jnp.sum(self.values(rows), axis=1, keepdims=True)
+            slots[0, pl.ds(index, 1), :] = jnp.broadcast_to(part, (block, block)).T[0:1, :]
+        if phase == 1:
+            for step in range(1, self.columns):
+                self.share(step).wait_recv()
+            totals[...] = sum(slots[step] for step in range(self.columns))
+        if phase == 2:
+            self.use(rows, jnp.broadcast_to(totals[pl.ds(index, 1), :], (block, block)).T)
+
+
+class NormJob(RowSumJob):
+    def __init__(self, rows_in, branch, gain):
+        rows, own = rows_in.shape
+        outs = [((rows, own), jnp.float32), ((rows, own), LOW), ((rows, 128), jnp.float32)]
+        super().__init__([rows_in, branch, gain], outs, [], rows, 0)
+
+    def values(self, rows):
+        residual = self.ins_v[0][rows, :].astype(jnp.float32) + self.ins_v[1][rows, :].astype(jnp.float32)
+        self.outs_v[0][rows, :] = residual
+        return residual * residual
+
+    def use(self, rows, total):
+        residual, normed, scales = self.outs_v
+        scale = lax.rsqrt(total / D + EPSILON)
+        scales[rows, :] = scale
+        normed[rows, :] = (residual[rows, :] * scale[:, 0:1] * self.ins_v[2][0:1, :]).astype(LOW)
+
+
+class NormBackJob(RowSumJob):
+    def __init__(self, grad, kept, scales, gain, base, rounded):
+        rows, own = grad.shape
+        outs = [((rows, own), jnp.float32), ((8, own), jnp.float32)]
+        outs = outs + [((rows, own), LOW)] if rounded else outs
+        super().__init__([grad, kept, scales, gain, base], outs, [], rows, 0)
+
+    def parts(self, rows):
+        grad, kept, scales, gain, base = self.ins_v
+        return (
+            grad[rows, :].astype(jnp.float32),
+            kept[rows, :].astype(jnp.float32),
+            scales[rows, 0:1],
+            gain[0:1, :],
+        )
+
+    def before(self, phase):
+        super().before(phase)
+        if phase == 0:
+            self.outs_v[1][...] = jnp.zeros_like(self.outs_v[1])
+
+    def values(self, rows):
+        grad, kept, scale, gain = self.parts(rows)
+        product = grad * kept
+        self.outs_v[1][0:1, :] += jnp.sum(product * scale, axis=0, keepdims=True)
+        return product * gain
+
+    def use(self, rows, total):
+        grad, kept, scale, gain = self.parts(rows)
+        rows_grad = scale * gain * grad - kept * (scale * scale * scale * total[:, 0:1] / D)
+        result = self.ins_v[4][rows, :].astype(jnp.float32) + rows_grad
+        self.outs_v[0][rows, :] = result
+        if len(self.outs_v) > 2:
+            self.outs_v[2][rows, :] = result.astype(LOW)
+
+
 class SmallSumJob:
-    tiles, flops = 0, 0
-
-    def __init__(self, blocks):
+    tiles, flops = 1, 0
+
+    def __init__(self, taps_grad, gain_grad, before):
         count = lax.axis_size("seq")
-        self.inputs = [blocks]
-        self.out_shapes = [jax.ShapeDtypeStruct(blocks.shape[1:], blocks.dtype)]
+        self.inputs = [taps_grad, gain_grad]
+        shape = taps_grad.shape
+        self.before = before
+        self.out_shapes = [jax.ShapeDtypeStruct(shape, jnp.float32)]
         self.scratch = [
-            pltpu.VMEM(blocks.shape, blocks.dtype),
-            pltpu.VMEM(blocks.shape, blocks.dtype),
-            pltpu.VMEM(blocks.shape[1:], blocks.dtype),
-            pltpu.SemaphoreType.DMA((2,)),
+            pltpu.VMEM(shape, jnp.float32),
+            pltpu.VMEM(shape, jnp.float32),
+            pltpu.VMEM((count,) + shape, jnp.float32),
+            pltpu.VMEM(shape, jnp.float32),
+            pltpu.SemaphoreType.DMA((3,)),
             pltpu.SemaphoreType.DMA((count,)),
             pltpu.SemaphoreType.DMA((count,)),
         ]
 
     def bind(self, ins, outs, scratch):
-        self.source, self.target = ins[0], outs[0]
-        self.own, self.slots, self.total, self.local_sem, self.send_sem, self.recv_sem = scratch
+        self.sources, self.target = ins, outs[0]
+        self.taps, self.gain, self.slots, self.total, self.local_sem, self.send_sem, self.recv_sem = scratch
         self.count = lax.axis_size("seq")
         self.seq = lax.axis_index("seq")
         self.column = lax.axis_index("tp")
@@ -736,20 +1045,32 @@
         return [((self.seq + far) % self.count, self.column) for far in range(1, self.count)]
 
     def copy(self, far):
-        other = (self.seq + far) % self.count
         return pltpu.make_async_remote_copy(
-            src_ref=self.own.at[other],
+            src_ref=self.slots.at[0],
             dst_ref=self.slots.at[far],
             send_sem=self.send_sem.at[far],
             recv_sem=self.recv_sem.at[far],
-            device_id=(other, self.column),
+            device_id=((self.seq + far) % self.count, self.column),
             device_id_type=MESH,
         )
 
+    def loads(self):
+        return [
+            pltpu.make_async_copy(self.sources[which], (self.taps, self.gain)[which], self.local_sem.at[which])
+            for which in range(2)
+        ]
+
     def start(self):
-        load = pltpu.make_async_copy(self.source, self.own, self.local_sem.at[0])
-        load.start()
-        load.wait()
+        for load in self.loads():
+            load.start()
+
+    def tile(self, index):
+        for load in self.loads():
+            load.wait()
+        self.slots[0, 0:3, :] = self.taps[0:3, :]
+        self.slots[0, 3:4, :] = self.before.outs_v[1][0:1, :]
+        self.slots[0, 4:5, :] = self.gain[0:1, :]
+        self.slots[0, 5:8, :] = jnp.zeros_like(self.slots[0, 5:8, :])
 
         def begin(far, carry):
             self.copy(far).start()
@@ -758,7 +1079,7 @@
         lax.fori_loop(1, self.count, begin, 0)
 
     def finish(self):
-        self.total[...] = self.own[self.seq]
+        self.total[...] = self.slots[0]
 
         def add(far, carry):
             self.copy(far).wait_recv()
@@ -766,7 +1087,7 @@
             return carry
 
         lax.fori_loop(1, self.count, add, 0)
-        store = pltpu.make_async_copy(self.total, self.target, self.local_sem.at[1])
+        store = pltpu.make_async_copy(self.total, self.target, self.local_sem.at[2])
         store.start()
 
         def sent(far, carry):
@@ -786,13 +1107,17 @@
     greet(ring.peers() + job.peers())
     ring.start()
     job.start()
-    each = -(-job.tiles // ring.ticks)
+    rest = max(ring.ticks // 6, 1)
+    active = ring.ticks - rest
+    each = -(-job.tiles // active)
 
     def step(index, carry):
+        late = index - rest
+        first, after = late * job.tiles // active, (late + 1) * job.tiles // active
         for inner in range(each):
-            tile = index * each + inner
-
-            @pl.when(tile < job.tiles)
+            tile = first + inner
+
+            @pl.when((late >= 0) & (tile < after))
             def _(tile=tile):
                 job.tile(tile)
 
@@ -845,37 +1170,12 @@
     return lax.all_gather(own, "tp", axis=0, tiled=True)
 
 
-def turned(own):
-    return with_layout_constraint(own.T, Layout(major_to_minor=(0, 1)))
-
-
 def gather_blocks(own):
     return gather_rows(own).reshape(-1, *own.shape)
 
 
 def reduce_branch(term):
-    return lax.psum_scatter(term, "tp", scatter_dimension=0, tiled=True).astype(jnp.float32)
-
-
-def share_small(own):
-    count = lax.axis_size("tp")
-    pieces = [own] + [
-        lax.ppermute(own, "tp", [(i, (i + far) % count) for i in range(count)]) for far in range(1, count)
-    ]
-    place = lax.axis_index("tp")
-    return jnp.stack([lax.dynamic_index_in_dim(jnp.stack(pieces), (place - part) % count, 0, False) for part in range(count)])
-
-
-def norm_forward(values, gain_row):
-    row_total = lax.psum(jnp.sum(values * values, axis=1, keepdims=True), "tp")
-    row_scale = lax.rsqrt(row_total / D + EPSILON)
-    return (values * row_scale * gain_row).astype(LOW), row_scale
-
-
-def norm_backward(grad_normed, kept_rows, row_scale, kept_gain):
-    inner_sum = lax.psum(jnp.sum(grad_normed * kept_gain * kept_rows, axis=1, keepdims=True), "tp")
-    rows_grad = row_scale * kept_gain * grad_normed - kept_rows * row_scale**3 * inner_sum / D
-    return (rows_grad, jnp.sum(grad_normed * kept_rows * row_scale, axis=0))
+    return lax.psum_scatter(term, "tp", scatter_dimension=0, tiled=True)
 
 
 def adam_update(weight, first, second, grad, rate, decay):
@@ -932,28 +1232,28 @@
         out[...] = result
 
 
+def paired(array):
+    rows, _, columns = array.shape
+    return array.reshape(rows, 2, columns // LANES, LANES).transpose(0, 2, 1, 3).reshape(-1, LANES)
+
+
 def adam_pairs(weight, first, second, grads):
     rows, _, columns = weight.shape
-    lanes = 128
-    deep = columns // lanes
-
-    def seen(array):
-        return array.reshape(rows, 2, deep, lanes).transpose(0, 2, 1, 3).reshape(rows * deep * 2, lanes)
-
+    deep = columns // LANES
     block = max(rows // 8, 8)
-    state = pl.BlockSpec((block * deep * 2, lanes), lambda step: (step, 0))
+    state = pl.BlockSpec((block * deep * 2, LANES), lambda step: (step, 0))
     results = pl.pallas_call(
-        functools.partial(adam_pairs_kernel, lanes),
-        out_shape=[jax.ShapeDtypeStruct((rows * deep * 2, lanes), weight.dtype)] * 3,
+        functools.partial(adam_pairs_kernel, LANES),
+        out_shape=[jax.ShapeDtypeStruct((rows * deep * 2, LANES), weight.dtype)] * 3,
         grid=(rows // block,),
         in_specs=[state] * 3 + [pl.BlockSpec((block, columns // 2), lambda step: (step, 0))] * 4,
         out_specs=[state] * 3,
-        scratch_shapes=[pltpu.VMEM((block * deep * 2, lanes), jnp.float32)],
+        scratch_shapes=[pltpu.VMEM((block * deep * 2, LANES), jnp.float32)],
         cost_estimate=pl.CostEstimate(flops=20 * weight.size, bytes_accessed=28 * weight.size, transcendentals=0),
         name="adam_pairs",
-    )(seen(weight), seen(first), seen(second), *grads)
+    )(paired(weight), paired(first), paired(second), *grads)
     return [
-        result.reshape(rows, deep, 2, lanes).transpose(0, 2, 1, 3).reshape(rows, 2, columns) for result in results
+        result.reshape(rows, deep, 2, LANES).transpose(0, 2, 1, 3).reshape(rows, 2, columns) for result in results
     ]
 
 
@@ -990,109 +1290,94 @@
     gain_first,
     gain_second,
 ):
-    rows_dev = tokens.shape[0]
     channels = tokens.shape[1]
     count = lax.axis_size("seq")
+    idle = NoJob()
+    seen = conv_kernel.shape[1]
     small = jnp.concatenate([conv_kernel, norm_gains], axis=0)
-    small = jnp.pad(small, ((0, 64 - small.shape[0]), (0, 128 - small.shape[1]))).astype(LOW)
+    small = jnp.pad(small, ((0, 16 - small.shape[0]), (0, 128 - seen))).astype(LOW)
     entry_low = entry_weight.reshape(entry_weight.shape[0], 3 * channels).astype(LOW)
-    hidden_half = shrink_weight.shape[1] // 2
-    halves = (slice(0, hidden_half), slice(hidden_half, 2 * hidden_half))
-    gate_low = [expand_weight[:, 0, half].astype(LOW) for half in halves]
-    up_low = [expand_weight[:, 1, half].astype(LOW) for half in halves]
-    shrink_low = [shrink_weight[:, half].astype(LOW) for half in halves]
+    bound = jnp.broadcast_to(bounds[0], (8, 128))
+
+    tokens_blocks = gather_blocks(tokens)
+    cast = CastJob(paired(expand_weight), shrink_weight)
+    entry_full, exit_full, small_full, *low = run_ring(
+        GatherRing([entry_low, exit_weight.astype(LOW)]), Jobs(SmallGatherJob(small), cast), 0
+    )
+    entry_full, exit_full = flat(entry_full), flat(exit_full)
+    gate_low, up_low, shrink_low = low[0:4:2], low[1:4:2], low[4:6]
+    small_wide = small_full[:, :, :8, :seen].transpose(1, 2, 0, 3).reshape(-1, 8, channels).astype(jnp.float32)
+    taps = lax.dynamic_index_in_dim(small_wide, lax.axis_index("tp"), 0, False)
+    gain_blocks = small_wide[:, 3:4] + jnp.zeros((1, 8, 1), jnp.float32)
+    gain_one = jnp.broadcast_to(taps[3:4], taps.shape)
+    gain_two = jnp.broadcast_to(taps[4:5], taps.shape)
     gate_full, up_full, shrink_full = [None] * 2, [None] * 2, [None] * 2
-    gate_rows, up_rows, activation = [None] * 2, [None] * 2, [None] * 2
-    gate_grad, up_grad = [None] * 2, [None] * 2
     shrink_part, gate_part, up_part = [None] * 2, [None] * 2, [None] * 2
-    idle = NoJob()
-
-    tokens_f = tokens.astype(jnp.float32)
-    bound = jnp.broadcast_to(bounds[0], (8, 128))
-
-    tokens_blocks = gather_blocks(tokens)
-    exit_full, small_full = run_ring(GatherRing([exit_weight.astype(LOW), small]), idle, 0)
-    small_full = small_full.reshape(count, 64, 128)[:, :8, : conv_kernel.shape[1]]
-    small_full = small_full.swapaxes(0, 1).reshape(8, channels).astype(jnp.float32)
-    taps = small_full
-    gains_row = small_full[3:5]
-    gain_blocks = share_small(jnp.broadcast_to(gains_row[0:1], (8, channels)))
-    entry_low, small_full = tie(entry_low, small_full)
-    (entry_full,) = run_ring(GatherRing([entry_low]), idle, 14)
-    entry_full, exit_full = flat(entry_full), flat(exit_full)
-    tokens_blocks, entry_full, gain_blocks = tie(tokens_blocks, entry_full, gain_blocks)
-    cot_own, cotangent_rows, gate_low[0], entry_full = tie(turned(cotangent), cotangent, gate_low[0], entry_full)
-    full, projected, conv_out, gated_rows, halo, mixer_rows, branch_term, scales, normed_one = run_ring(
+
+    tokens_blocks, cotangent_rows, entry_full = tie(tokens_blocks, cotangent, entry_full)
+    cot_blocks = gather_blocks(cotangent_rows)
+    full, projected, conv_out, gated_rows, halo, mixer_rows, branch_term, scale_one, normed_one = run_ring(
         GatherRing([gate_low[0]]), EntryJob(tokens_blocks, gain_blocks, entry_full, exit_full, taps, bound), 1
     )
-    scale_one = scales[:, :1]
     gate_full[0] = flat(full)
-    branch_term, up_low[0] = tie(branch_term, up_low[0])
-    (full,) = run_ring(GatherRing([up_low[0]]), idle, 2)
+    cot_blocks, branch_term, up_low[0] = tie(cot_blocks, branch_term, up_low[0])
+    full, cot_full = run_ring(GatherRing([up_low[0]]), TurnJob(cot_blocks), 2)
     branch, up_full[0] = tie(reduce_branch(branch_term), flat(full))
-    residual = tokens_f + branch
-    own_normed_two, scale_two = norm_forward(residual, gains_row[1])
-    own_normed_two = with_layout_constraint(own_normed_two, Layout(major_to_minor=(0, 1)))
-    own_normed_two, gate_low[1] = tie(own_normed_two, gate_low[1])
-    (full,) = run_ring(GatherRing([gate_low[1]]), idle, 3)
-    normed_blocks, gate_full[1] = tie(gather_blocks(own_normed_two), flat(full))
-    own_normed_two, up_low[1] = tie(turned(own_normed_two), up_low[1])
-    full, gate_rows[0], up_rows[0], activation[0] = run_ring(
-        GatherRing([up_low[1]]), ExpandJob(normed_blocks, gate_full[0], up_full[0]), 4
-    )
-    normed_two, up_full[1] = tie(gather_rows(own_normed_two), flat(full))
-    cotangent_rows, shrink_low[0], normed_two = tie(cotangent_rows, shrink_low[0], normed_two)
-    full, gate_rows[1], up_rows[1], activation[1] = run_ring(
-        GatherRing([shrink_low[0]]), ExpandJob(normed_blocks, gate_full[1], up_full[1]), 5
-    )
-    cot_blocks, shrink_full[0] = tie(gather_blocks(cotangent_rows), flat(full))
-    cot_own, shrink_low[1], cot_blocks = tie(cot_own, shrink_low[1], cot_blocks)
-    full, gate_grad[0], up_grad[0] = run_ring(
-        GatherRing([shrink_low[1]]), HiddenGradJob(cot_blocks, shrink_full[0], gate_rows[0], up_rows[0]), 6
-    )
-    cot_full, shrink_full[1] = tie(gather_rows(cot_own), flat(full))
-    shrink_part[0], gate_grad[1], up_grad[1] = run_ring(
-        ScatterRing([(cot_full, activation[0])]),
-        HiddenGradJob(cot_blocks, shrink_full[1], gate_rows[1], up_rows[1]),
-        7,
-    )
-    shrink_part[1], two_term = run_ring(
-        ScatterRing([(cot_full, activation[1])]), WidthJob(gate_grad + up_grad, gate_full + up_full), 8
-    )
-    two_term, gate_grad[0] = tie(two_term, gate_grad[0])
-    gate_part[0], mixed_term = run_ring(
-        ScatterRing([(normed_two, gate_grad[0])]), WidthJob(activation, shrink_full), 9
-    )
-    grad_normed_two, gate_part[0], mixed_term = tie(reduce_branch(two_term), gate_part[0], mixed_term)
-    residual_norm_grad, gain_two_grad = norm_backward(grad_normed_two, residual, scale_two, gains_row[1])
-    residual_grad = cotangent.astype(jnp.float32) + residual_norm_grad
-    branch_own = with_layout_constraint(residual_grad.astype(LOW), Layout(major_to_minor=(0, 1)))
-    branch_own, up_grad[0] = tie(branch_own, up_grad[0])
+    full, residual, own_normed_two, scale_two = run_ring(
+        GatherRing([gate_low[1]]), NormJob(tokens, branch, gain_two), 3
+    )
+    own_normed_two, gate_full[1], up_low[1] = tie(own_normed_two, flat(full), up_low[1])
+    (full,) = run_ring(GatherRing([up_low[1]]), idle, 4)
+    normed_blocks, up_full[1] = tie(gather_blocks(own_normed_two), flat(full))
+    full, *expanded = run_ring(
+        GatherRing([shrink_low[0]]),
+        Jobs(*[ExpandJob(normed_blocks, gate_full[half], up_full[half]) for half in range(2)]),
+        5,
+    )
+    gate_rows, up_rows, activation = expanded[0::3], expanded[1::3], expanded[2::3]
+    shrink_full[0] = flat(full)
+    full, gate_grad_one, up_grad_one, normed_two = run_ring(
+        GatherRing([shrink_low[1]]),
+        Jobs(HiddenGradJob(cot_blocks, shrink_full[0], gate_rows[0], up_rows[0]), TurnJob(normed_blocks)),
+        6,
+    )
+    shrink_full[1] = flat(full)
+    hidden = HiddenGradJob(cot_blocks, shrink_full[1], gate_rows[1], up_rows[1])
+    width = WidthJob([gate_grad_one, up_grad_one], [gate_full[0], up_full[0], gate_full[1], up_full[1]], hidden)
+    shrink_part[0], gate_grad_two, up_grad_two, two_term = run_ring(
+        ScatterRing([(cot_full, activation[0])]), Jobs(hidden, width), 7
+    )
+    gate_grad, up_grad = [gate_grad_one, gate_grad_two], [up_grad_one, up_grad_two]
+    shrink_part[1], mixed_term = run_ring(
+        ScatterRing([(cot_full, activation[1])]), WidthJob(activation, shrink_full), 8
+    )
+    grad_normed_two, shrink_part[1], mixed_term = tie(reduce_branch(two_term), shrink_part[1], mixed_term)
+    gate_part[0], residual_grad, gain_two_grad, branch_own = run_ring(
+        ScatterRing([(normed_two, gate_grad[0])]),
+        NormBackJob(grad_normed_two, residual, scale_two, gain_two, cotangent, True),
+        9,
+    )
+    mixed_branch, branch_own, up_grad[0] = tie(reduce_branch(mixed_term), branch_own, up_grad[0])
     (up_part[0],) = run_ring(ScatterRing([(normed_two, up_grad[0])]), idle, 10)
     branch_blocks, up_part[0] = tie(gather_blocks(branch_own), up_part[0])
-    branch_own, mixed_term, gate_grad[1], branch_blocks = tie(
-        turned(branch_own), mixed_term, gate_grad[1], branch_blocks
-    )
     gate_part[1], projected_grad, one_term, taps_grad = run_ring(
         ScatterRing([(normed_two, gate_grad[1])]),
         MixerGradJob(branch_blocks, exit_full, entry_full, projected, conv_out, gated_rows, halo, taps, bound),
         11,
     )
-    mixed_branch, gate_part[1], branch_full = tie(reduce_branch(mixed_term), gate_part[1], gather_rows(branch_own))
-    mixed = (residual + mixed_branch).astype(LOW)
-    one_term, up_grad[1], mixed_branch = tie(one_term, up_grad[1], mixed_branch)
-    (up_part[1],) = run_ring(ScatterRing([(normed_two, up_grad[1])]), idle, 12)
+    one_term, up_grad[1], gate_part[1] = tie(one_term, up_grad[1], gate_part[1])
+    up_part[1], branch_full = run_ring(ScatterRing([(normed_two, up_grad[1])]), TurnJob(branch_blocks), 12)
     grad_normed_one, up_part[1] = tie(reduce_branch(one_term), up_part[1])
-    tokens_norm_grad, gain_one_grad = norm_backward(grad_normed_one, tokens_f, scale_one, gains_row[0])
-    tokens_grad = residual_grad + tokens_norm_grad
-    small_grad = jnp.concatenate([taps_grad[:3], gain_one_grad[None], gain_two_grad[None]], axis=0)
-    small_blocks = small_grad.reshape(5, count, conv_kernel.shape[1]).swapaxes(0, 1)
-    small_blocks = jnp.pad(small_blocks, ((0, 0), (0, 3), (0, 128 - conv_kernel.shape[1])))
-    entry_part, exit_part, small_part = run_ring(
-        ScatterRing([(normed_one, projected_grad), (branch_full, mixer_rows)]), SmallSumJob(small_blocks), 13
-    )
-    kernel_part = small_part[:3, : conv_kernel.shape[1]]
-    gains_part = small_part[3:5, : conv_kernel.shape[1]]
+    back = NormBackJob(grad_normed_one, tokens, scale_one, gain_one, residual_grad, False)
+    entry_part, exit_part, tokens_grad, _, small_part = run_ring(
+        ScatterRing([(normed_one, projected_grad), (branch_full, mixer_rows)]),
+        Jobs(back, SmallSumJob(taps_grad, gain_two_grad, back)),
+        13,
+    )
+    mixed = (residual + mixed_branch.astype(jnp.float32)).astype(LOW)
+    small_part = lax.dynamic_slice_in_dim(small_part, lax.axis_index("seq") * seen, seen, axis=1)
+    kernel_part = small_part[:3]
+    gains_part = small_part[3:5]
     entry_next, entry_first_next, entry_second_next = adam_planes(
         entry_weight, entry_first, entry_second, entry_part
     )

time: 894 us -> 796 us (0.89)
  other arithmetic: 34.5 us -> 4.71 us
  Pallas kernels: 776 us -> 752 us
  blocking collectives: 17.4 us -> 0 us
  waiting for transfers between devices: 22.1 us -> 6.86 us
    pallas_call x15 -> x14, Pallas kernels: 743 us -> 718 us  [run_ring(): pl.pallas_call(functools.partial(ring_kernel, ring, job), out_shape=outs,...]
    all_gather x7 -> x4, waiting for transfers between devices: 19.3 us -> 0.08 us  [gather_rows(): return lax.all_gather(own, 'tp', axis=0, tiled=True)]
    psum x3 -> x0, blocking collectives: 17.4 us -> none  [the longest x2 11.6 us: norm_backward(): lax.psum(jnp.sum(grad_normed * kept_gain * kept_rows, axis=1, keepdims=Tr...]
    convert_element_type x8 -> x2, other arithmetic: 17.5 us -> 2.17 us  [the longest x1 1.32 us: shards(): mixed = (residual + mixed_branch.astype(jnp.float32)).astype(LOW)]
  transfers between devices with their start and end apart: 14 -> 8, of which waited for: 2 -> 3; matrix products, arithmetic and copies ran while one was open for 3% -> 1% of each run, Pallas kernels for 58% -> 52%
where the time goes in v4:
time: 796 us; the launch traced here: 788 us
  Pallas kernels  752 us (94%)
  between operations  15.3 us (2%)
  local copies, waits for them, and re-layouts  8.21 us (1%)
    pallas_call x14, Pallas kernels, run_ring(): pl.pallas_call(functools.partial(ring_kernel, ring, job), out_shape=outs,...  718 us
    pallas_call x3, Pallas kernels, adam_rows(): pl.pallas_call(functools.partial(adam_kernel, len(grads)), out_shape=[jax...  18.4 us
  transfers between devices with their start and end apart: 8, of which 3 were waited for; matrix products, arithmetic and copies ran while one was open for 1% of the time, Pallas kernels for 52%

profile of v4, /device:TPU:0, one launch (start us, length us, event | category | flops | bytes accessed | tf_op | source)
XLA Modules:
  0.0 787.8 jit_solution(4253950346178174604)
XLA Ops:
  7.3 0.7 all-gather.5.cloned.1.call-update
  8.0 1.7 copy.48
  9.7 1.2 copy.50.refs_0_
  10.8 0.7 convert_element_type.28.refs_1_
  12.2 90.2 %ring_gather.7 = (bf16[8,256,1536]{2,1,0:T(8,128)(2,1)}, bf16[8,256,512]{2,1,0:T(8,128)(2,1)}, bf16[8,4,16,128]{3,2,1,0:T(8,128)(2,1)}, bf16[256,1024]{1,0:T(8,1...) custom-call(bf16[256,1536]{1,0:T(8,128)(2,1)} %copy.50.refs_0_, ...), custom_call_target="tpu_custom_call" | custom-call | bytes 167772160 | tf_op jit(solution)/shard_map/ring_gather/pallas_call | solution.py:1135
  102.5 0.9 convert_bitcast_fusion
  104.2 0.6 dynamic-slice_bitcast_fusion.refs_5_.refs_9_
  104.8 0.6 add.58.refs_2_
  106.1 46.2 %ring_gather.8 = (bf16[8,256,1024]{2,1,0:T(8,128)(2,1)}, f32[1024,1536]{1,0:T(8,128)}, f32[1024,512]{1,0:T(8,128)}, bf16[1024,512]{1,0:T(8,128)(2,1)}, bf16[16,5...) custom-call(bf16[256,1024]{1,0:T(8,128)(2,1)} %get-tuple-element.116, ...), custom_call_target="tpu_custom_call" | custom-call | flops 8589934592 | bytes 83886080 | tf_op jit(solution)/shard_map/ring_gather/pallas_call | solution.py:1135
  152.3 41.5 %ring_gather.9 = (bf16[8,256,1024]{2,1,0:T(8,128)(2,1)}, bf16[2048,1024]{1,0:T(8,128)(2,1)}) custom-call(bf16[256,1024]{1,0:T(8,128)(2,1)} %get-tuple-element.124.refs_0_, bf16[4,1024,512]{2,1,0:T(8,128)(2,1)} %bitcast.76), custom_call_target="tpu_custom_call" | custom-call | bytes 83886080 | tf_op jit(solution)/shard_map/ring_gather/pallas_call | solution.py:1135
  193.9 3.1 reduce-scatter.5.cloned.1.call-done.refs_2_
  197.6 44.9 %ring_gather.10 = (bf16[8,256,1024]{2,1,0:T(8,128)(2,1)}, f32[1024,512]{1,0:T(8,128)}, bf16[1024,512]{1,0:T(8,128)(2,1)}, f32[1024,128]{1,0:T(8,128)}) custom-call(bf16[256,1024]{1,0:T(8,128)(2,1)} %get-tuple-element.113.refs_0_, bf16[1024,512]{1,0:T(8,128)(2,1)} %refs_5_.1, bf16[1024,512]{1,0:T(8,128)(2,1)} %reduce-scatter.5.cloned.1.call-done.refs_2_, ...), custom_call_target="tpu_custom_call" | custom-call | bytes 83886080 | tf_op jit(solution)/shard_map/ring_gather/pallas_call | solution.py:1135
  243.0 43.6 %ring_gather.11 = bf16[8,256,1024]{2,1,0:T(8,128)(2,1)} custom-call(bf16[256,1024]{1,0:T(8,128)(2,1)} %get-tuple-element.135.refs_0_), custom_call_target="tpu_custom_call" | custom-call | bytes 83886080 | tf_op jit(solution)/shard_map/ring_gather/pallas_call | solution.py:1135
  286.7 44.2 %ring_gather.12 = (bf16[8,256,1024]{2,1,0:T(8,128)(2,1)}, f32[1024,1024]{1,0:T(8,128)}, f32[1024,1024]{1,0:T(8,128)}, bf16[1024,1024]{1,0:T(8,128)(2,1)}, f32[10...) custom-call(bf16[256,1024]{1,0:T(8,128)(2,1)} %get-tuple-element.130.refs_0_, ...), custom_call_target="tpu_custom_call" | custom-call | flops 17179869184 | bytes 83886080 | tf_op jit(solution)/shard_map/ring_gather/pallas_call | solution.py:1135
  330.8 43.2 %ring_gather.13 = (bf16[8,256,1024]{2,1,0:T(8,128)(2,1)}, bf16[1024,1024]{1,0:T(8,128)(2,1)}, bf16[1024,1024]{1,0:T(8,128)(2,1)}, bf16[2048,1024]{1,0:T(8,128)(2,1)}) custom-call(bf16[256,1024]{1,0:T(8,128)(2,1)} %get-tuple-element.142.refs_0_, bf16[4,1024,512]{2,1,0:T(8,128)(2,1)} %bitcast.77, bf16[2048,1024]{1,0:T(8,128)(2,1)} %bitcast.84, ...), custom_call_target="tpu_custom_call" | custom-call | flops 4294967296 | bytes 83886080 | tf_op jit(solution)/shard_map/ring_gather/pallas_call | solution.py:1135
  374.0 52.2 %ring_scatter.7 = (f32[256,1024]{1,0:T(8,128)}, bf16[1024,1024]{1,0:T(8,128)(2,1)}, bf16[1024,1024]{1,0:T(8,128)(2,1)}, bf16[4096,512]{1,0:T(8,128)(2,1)}) custom-call(bf16[2048,1024]{1,0:T(8,128)(2,1)} %get-tuple-element.129.refs_0_, bf16[1024,1024]{1,0:T(8,128)(2,1)} %get-tuple-element.141.refs_1_.refs_2_, bf16[4,1024,512]{2,1,0:T(8,128)(2,1)} %bitcast.78, ...), custom_call_target="tpu_custom_call" | custom-call | flops 25769803776 | bytes 83886080 | tf_op jit(solution)/shard_map/ring_scatter/pallas_call | solution.py:1135
  426.3 40.7 %ring_scatter.8 = (f32[256,1024]{1,0:T(8,128)}, bf16[4096,512]{1,0:T(8,128)(2,1)}) custom-call(bf16[2048,1024]{1,0:T(8,128)(2,1)} %get-tuple-element.129.refs_0_, bf16[1024,1024]{1,0:T(8,128)(2,1)} %get-tuple-element.152.refs_1_.refs_3_, bf16[1024,1024]{1,0:T(8,128)(2,1)} %get-tuple-element.141.refs_1_.refs_2_, ...), custom_call_target="tpu_custom_call" | custom-call | flops 12884901888 | bytes 83886080 | tf_op jit(solution)/shard_map/ring_scatter/pallas_call | solution.py:1135
  467.0 2.1 reduce-scatter.7.cloned.1.call-done.refs_2_
  469.2 46.2 %ring_scatter.9 = (f32[256,1024]{1,0:T(8,128)}, f32[1024,512]{1,0:T(8,128)}, f32[8,512]{1,0:T(8,128)}, bf16[1024,512]{1,0:T(8,128)(2,1)}) custom-call(bf16[2048,1024]{1,0:T(8,128)(2,1)} %get-tuple-element.156.refs_0_, bf16[1024,1024]{1,0:T(8,128)(2,1)} %get-tuple-element.149.refs_6_.refs_1_, bf16[1024,512]{1,0:T(8,128)(2,1)} %reduce-scatter.7.cloned.1.call-done.refs_2_, ...), custom_call_target="tpu_custom_call" | custom-call | flops 4294967296 | bytes 83886080 | tf_op jit(solution)/shard_map/ring_scatter/pallas_call | solution.py:1135
  515.4 0.7 reduce-scatter.9.cloned.1.call-done
  516.2 46.0 %ring_scatter.10.refs_4_ = f32[256,1024]{1,0:T(8,128)} custom-call(bf16[2048,1024]{1,0:T(8,128)(2,1)} %get-tuple-element.156.refs_0_, bf16[1024,1024]{1,0:T(8,128)(2,1)} %get-tuple-element.164.refs_7_.refs_1_), custom_call_target="tpu_custom_call" | custom-call | flops 4294967296 | bytes 83886080 | tf_op jit(solution)/shard_map/ring_scatter/pallas_call | solution.py:1135
  562.2 47.7 %ring_scatter.11 = (f32[256,1024]{1,0:T(8,128)}, bf16[1024,1536]{1,0:T(8,128)(2,1)}, bf16[4096,512]{1,0:T(8,128)(2,1)}, f32[8,512]{1,0:T(8,128)}) custom-call(bf16[2048,1024]{1,0:T(8,128)(2,1)} %get-tuple-element.156.refs_0_, bf16[1024,1024]{1,0:T(8,128)(2,1)} %get-tuple-element.162.refs_1_, bf16[4,1024,512]{2,1,0:T(8,128)(2,1)} %bitcast.98, ...), custom_call_target="tpu_custom_call" | custom-call | flops 12884901888 | bytes 83886080 | tf_op jit(solution)/shard_map/ring_scatter/pallas_call | solution.py:1135
  610.0 9.2 %adam_rows.5 = (f32[256,2048]{1,0:T(8,128)}, f32[256,2048]{1,0:T(8,128)}, f32[256,2048]{1,0:T(8,128)}) custom-call(f32[256,2048]{1,0:T(8,128)} %refs_0_.3, f32[256,2048]{1,0:T(8,128)} %refs_1_.5, f32[256,2048]{1,0:T(8,128)} %refs_2_.3, f32[256,1024]{1,0:T(8,128)} %get-tuple-element.200.refs_3_, f32[256,1024]{1,0:T(8,128)} %get-tuple-element.201.refs_4_), custom_call_target="tpu_custom_call" | custom-call | flops 10485760 | bytes 14680064 | tf_op jit(solution)/shard_map/adam_rows/pallas_call | solution.py:1209
  619.2 1.3 add_convert_fusion
  620.5 44.8 %ring_scatter.12 = (f32[256,1024]{1,0:T(8,128)}, bf16[2048,1024]{1,0:T(8,128)(2,1)}) custom-call(bf16[2048,1024]{1,0:T(8,128)(2,1)} %get-tuple-element.156.refs_0_, bf16[1024,1024]{1,0:T(8,128)(2,1)} %get-tuple-element.173.refs_1_, bf16[4,1024,512]{2,1,0:T(8,128)(2,1)} %bitcast.99), custom_call_target="tpu_custom_call" | custom-call | flops 4294967296 | bytes 83886080 | tf_op jit(solution)/shard_map/ring_scatter/pallas_call | solution.py:1135
  665.3 0.6 broadcast_in_dim.21.refs_7_
  666.0 87.2 %ring_scatter.13 = (f32[256,1536]{1,0:T(8,128)}, f32[256,512]{1,0:T(8,128)}, f32[1024,512]{1,0:T(8,128)}, f32[8,512]{1,0:T(8,128)}, f32[8,512]{1,0:T(8,128)}) custom-call(bf16[2048,1024]{1,0:T(8,128)(2,1)} %get-tuple-element.161.refs_0_, bf16[2048,1024]{1,0:T(8,128)(2,1)} %get-tuple-element.174.refs_1_, bf16[1024,1536]{1,0:T(8,128)(2,1)} %get-tuple-element.175.refs_2_, ...), custom_call_target="tpu_custom_call" | custom-call | flops 8589934592 | bytes 167772160 | tf_op jit(solution)/shard_map/ring_scatter/pallas_call | solution.py:1135
  753.2 0.8 constant_dynamic-slice_fusion.2
  755.1 2.6 adam_rows.4
  757.7 6.6 adam_rows.3
  764.3 15.2 %adam_pairs.1 = (f32[8192,128]{1,0:T(8,128)}, f32[8192,128]{1,0:T(8,128)}, f32[8192,128]{1,0:T(8,128)}) custom-call(f32[8192,128]{1,0:T(8,128)} %bitcast.75, f32[8192,128]{1,0:T(8,128)} %bitcast.82, f32[8192,128]{1,0:T(8,128)} %bitcast.83, f32[256,1024]{1,0:T(8,128)} %get-tuple-element.193.refs_3_, f32[256,1024]{1,0:T(8,128)} %ring_scatter.10.refs_4_, ...), custom_call_target="tpu_custom_call" | custom-call | flops 20971520 | bytes 29360128 | tf_op jit(solution)/shard_map/adam_pairs/pallas_call | solution.py:1245
  779.5 1.3 copy.62
  (52 shorter events, 4.2 us)
Async XLA Ops:
  7.2 3.7 copy-start.2
  7.2 4.4 copy-start.7
  7.2 4.4 copy-start.4
  7.2 95.2 %all-gather.5.cloned.1.call-start = ((), (), s32[]{:S(2)}) async-start(), calls=%async_computation.4 | async-start | bytes 5242880 | tf_op jit(solution)/shard_map/all_gather | solution.py:1170
  8.0 144.3 %all-gather.7.cloned.1.call-start = ((), (), s32[]{:S(2)}) async-start(), calls=%async_computation.5 | async-start | bytes 5242880 | tf_op jit(solution)/shard_map/all_gather | solution.py:1170
  102.5 94.5 %reduce-scatter.5.cloned.1.call-start = ((), (), s32[]{:S(2)}) async-start(), calls=%async_computation.6 | async-start | bytes 5242880 | tf_op jit(solution)/shard_map/reduce_scatter | solution.py:1178
  152.3 134.4 %all-gather.9.cloned.1.call-start = ((), (), s32[]{:S(2)}) async-start(), calls=%async_computation.7 | async-start | bytes 5242880 | tf_op jit(solution)/shard_map/all_gather | solution.py:1170
  242.5 226.7 %reduce-scatter.7.cloned.1.call-start = ((), (), s32[]{:S(2)}) async-start(), calls=%async_computation.8 | async-start | bytes 5242880 | tf_op jit(solution)/shard_map/reduce_scatter | solution.py:1178
  426.3 89.9 %reduce-scatter.9.cloned.1.call-start = ((), (), s32[]{:S(2)}) async-start(), calls=%async_computation.9 | async-start | bytes 5242880 | tf_op jit(solution)/shard_map/reduce_scatter | solution.py:1178
  469.1 93.1 %all-gather.11.cloned.1.call-start = ((), (), s32[]{:S(2)}) async-start(), calls=%async_computation.10 | async-start | bytes 5242880 | tf_op jit(solution)/shard_map/all_gather | solution.py:1170
  516.2 149.1 %reduce-scatter.11.cloned.1.call-start = ((), (), s32[]{:S(2)}) async-start(), calls=%async_computation.11 | async-start | bytes 5242880 | tf_op jit(solution)/shard_map/reduce_scatter | solution.py:1178
  609.9 9.3 %copy-start = (f32[1024,512]{1,0:T(8,128)S(1)}, f32[1024,512]{1,0:T(8,128)}, u32[]{:S(2)}) copy-start(f32[1024,512]{1,0:T(8,128)} %get-tuple-element.128.refs_3_) | copy-start | bytes 6291460
  610.0 9.3 %copy-start.3 = (bf16[1024,512]{1,0:T(8,128)(2,1)S(1)}, bf16[1024,512]{1,0:T(8,128)(2,1)}, u32[]{:S(2)}) copy-start(bf16[1024,512]{1,0:T(8,128)(2,1)} %reduce-scatter.9.cloned.1.call-done) | copy-start | bytes 3145732
  665.9 88.0 %copy-start.5 = (f32[3,64]{1,0:T(4,128)S(1)}, f32[3,64]{1,0:T(4,128)}, u32[]{:S(2)}) copy-start(f32[3,64]{1,0:T(4,128)} %param.37) | copy-start | bytes 2308
  665.9 88.0 %copy-start.6 = (f32[3,64]{1,0:T(4,128)S(1)}, f32[3,64]{1,0:T(4,128)}, u32[]{:S(2)}) copy-start(f32[3,64]{1,0:T(4,128)} %param.38) | copy-start | bytes 2308
  665.9 88.6 %copy-start.8 = (f32[2,64]{1,0:T(2,128)S(1)}, f32[2,64]{1,0:T(2,128)}, u32[]{:S(2)}) copy-start(f32[2,64]{1,0:T(2,128)} %param.40) | copy-start | bytes 1540
  665.9 88.6 %copy-start.9 = (f32[2,64]{1,0:T(2,128)S(1)}, f32[2,64]{1,0:T(2,128)}, u32[]{:S(2)}) copy-start(f32[2,64]{1,0:T(2,128)} %param.41) | copy-start | bytes 1540
  764.3 15.2 %copy-start.1 = (f32[1024,512]{1,0:T(8,128)S(1)}, f32[1024,512]{1,0:T(8,128)}, u32[]{:S(2)}) copy-start(f32[1024,512]{1,0:T(8,128)} %get-tuple-element.235) | copy-start | bytes 6291460
Sparse Core Ops, SparseCore 0:
  9.6 37.1 all-gather.4
  102.6 33.3 all-gather.6
  152.4 44.5 reduce-scatter.4
  242.6 32.9 all-gather.8
  426.4 42.6 reduce-scatter.6
  471.5 44.6 reduce-scatter.8
  517.8 34.4 all-gather.10
  610.1 42.9 reduce-scatter.10

commit v5 on v4

--- a/solution.py
+++ b/solution.py
@@ -60,82 +60,123 @@
 
 
 class GatherRing:
-    name = "ring_gather"
-
-    def __init__(self, shards):
+    def __init__(self, groups, shapes):
         self.count = lax.axis_size("seq")
-        self.inputs = list(shards)
-        self.arrays = len(shards)
-        self.rows = [shard.shape[0] for shard in shards]
-        self.parts = 2 if min(self.rows) % 64 == 0 else 1
+        self.groups = groups
+        self.rows = {full: shapes[shard].shape[0] for group in groups for shard, full in group}
+        self.order = {full: place for place, full in enumerate(self.rows)}
+        self.parts = 2 if min(self.rows.values()) % 64 == 0 else 1
         self.ticks = (self.count - 2) * self.parts
-        self.out_shapes = [jax.ShapeDtypeStruct((self.count,) + shard.shape, shard.dtype) for shard in shards]
-        sems = pltpu.SemaphoreType.DMA((self.arrays, 2, self.parts, self.count - 1))
-        self.scratch = [sems, sems, pltpu.SemaphoreType.DMA((self.arrays,))]
-        self.flops = 0
-        self.bytes = 20 * sum(shard.size for shard in shards) * 2 * self.count
-
-    def bind(self, ins, outs, scratch):
-        self.shard_refs, self.full_refs = ins, outs
+        arrays = len(self.rows)
+        sems = pltpu.SemaphoreType.DMA((arrays, 2, self.parts, self.count - 1))
+        self.scratch = [sems, sems, pltpu.SemaphoreType.DMA((arrays,))]
+
+    def bind(self, refs, scratch):
+        self.refs = refs
         self.send_sem, self.recv_sem, self.own_sem = scratch
         self.column = lax.axis_index("tp")
         self.place, self.ahead, self.behind = ring_ends(self.count)
 
-    def pieces(self):
-        return [(array, way) for array in range(self.arrays) for way in range(2)]
-
-    def copy(self, array, way, part, step, first=False):
+    def copy(self, shard, full, way, part, step, first=False):
         move = (self.place + self.count - step) if way == 0 else (self.place + step)
         owner = ring_index(move % self.count, self.count)
-        size = self.rows[array] // 2 // self.parts
-        rows = pl.ds(pl.multiple_of(way * (self.rows[array] // 2) + part * size, 16), size)
-        there = self.full_refs[array].at[owner, rows]
+        half = self.rows[full] // 2
+        size = half // self.parts
+        rows = pl.ds(pl.multiple_of(way * half + part * size, 16), size)
+        there = self.refs[full].at[owner, rows]
         return pltpu.make_async_remote_copy(
-            src_ref=self.shard_refs[array].at[rows] if first else there,
+            src_ref=self.refs[shard].at[rows] if first else there,
             dst_ref=there,
-            send_sem=self.send_sem.at[array, way, part, step],
-            recv_sem=self.recv_sem.at[array, way, part, step],
+            send_sem=self.send_sem.at[self.order[full], way, part, step],
+            recv_sem=self.recv_sem.at[self.order[full], way, part, step],
             device_id=(self.ahead if way == 0 else self.behind, self.column),
             device_id_type=MESH,
         )
 
-    def own(self, array):
-        there = self.full_refs[array].at[lax.axis_index("seq")]
-        return pltpu.make_async_copy(self.shard_refs[array], there, self.own_sem.at[array])
-
-    def peers(self):
-        return [(self.ahead, self.column), (self.behind, self.column)]
-
-    def prepare(self):
-        pass
+    def own(self, shard, full):
+        there = self.refs[full].at[lax.axis_index("seq")]
+        return pltpu.make_async_copy(self.refs[shard], there, self.own_sem.at[self.order[full]])
+
+    def pieces(self, group):
+        return [(shard, full, way) for shard, full in self.groups[group] for way in range(2)]
+
+    def begin(self, group):
+        for part in range(self.parts):
+            for shard, full, way in self.pieces(group):
+                self.copy(shard, full, way, part, 0, True).start()
+        for shard, full in self.groups[group]:
+            self.own(shard, full).start()
+
+    def tick(self, group, index):
+        step, part = 1 + index // self.parts, index % self.parts
+        for shard, full, way in self.pieces(group):
+            self.copy(shard, full, way, part, step - 1).wait_recv()
+            self.copy(shard, full, way, part, step).start()
+
+    def settle(self, group):
+        for part in range(self.parts):
+            for shard, full, way in self.pieces(group):
+                self.copy(shard, full, way, part, self.count - 2).wait_recv()
+        for shard, full in self.groups[group]:
+            self.own(shard, full).wait()
+
+    def finish(self):
+        def sent(step, carry):
+            for group in range(len(self.groups)):
+                for part in range(self.parts):
+                    for shard, full, way in self.pieces(group):
+                        self.copy(shard, full, way, part, step).wait_send()
+            return carry
+
+        lax.fori_loop(0, self.count - 1, sent, 0)
+
+
+class PeerCopies:
+    def __init__(self, source, target):
+        self.source, self.target = source, target
+        columns = lax.axis_size("tp")
+        self.scratch = [pltpu.SemaphoreType.DMA((columns,)), pltpu.SemaphoreType.DMA((columns,))]
+
+    def bind(self, refs, scratch):
+        self.source_ref, self.target_ref = refs[self.source], refs[self.target]
+        self.send_sem, self.recv_sem = scratch
+        self.columns = lax.axis_size("tp")
+        self.seq, self.column = lax.axis_index("seq"), lax.axis_index("tp")
+
+    def block(self, peer):
+        if len(self.source_ref.shape) == len(self.target_ref.shape):
+            return self.source_ref.at[peer]
+        return self.source_ref
+
+    def own(self):
+        return pltpu.make_async_copy(
+            self.block(self.column), self.target_ref.at[self.column], self.send_sem.at[0]
+        )
+
+    def copy(self, step):
+        peer = (self.column + step) % self.columns
+        return pltpu.make_async_remote_copy(
+            src_ref=self.block(peer),
+            dst_ref=self.target_ref.at[self.column],
+            send_sem=self.send_sem.at[step],
+            recv_sem=self.recv_sem.at[step],
+            device_id=(self.seq, peer),
+            device_id_type=MESH,
+        )
 
     def start(self):
-        for part in range(self.parts):
-            for array, way in self.pieces():
-                self.copy(array, way, part, 0, True).start()
-        for array in range(self.arrays):
-            self.own(array).start()
-
-    def tick(self, index):
-        step, part = 1 + index // self.parts, index % self.parts
-        for array, way in self.pieces():
-            self.copy(array, way, part, step - 1).wait_recv()
-            self.copy(array, way, part, step).start()
+        for step in range(1, self.columns):
+            self.copy(step).start()
+        self.own().start()
+
+    def wait(self):
+        self.own().wait()
+        for step in range(1, self.columns):
+            self.copy(step).wait_recv()
 
     def finish(self):
-        for part in range(self.parts):
-            for array, way in self.pieces():
-                self.copy(array, way, part, self.count - 2).wait_recv()
-
-        def sent(step, carry):
-            for part in range(self.parts):
-                for array, way in self.pieces():
-                    self.copy(array, way, part, step).wait_send()
-            return carry
-
-        lax.fori_loop(0, self.count - 1, sent, 0)
-        for array in range(self.arrays):
-            self.own(array).wait()
+        for step in range(1, self.columns):
+            self.copy(step).wait_send()
 
 
 class ScatterRing:
@@ -281,7 +322,10 @@
 
 
 class NoJob:
-    inputs, out_shapes, scratch, tiles, flops = [], [], [], 0, 0
+    inputs, out_shapes, scratch, kept, tiles, flops = [], [], [], [], 0, 0
+
+    def hold(self, refs):
+        pass
 
     def bind(self, ins, outs, scratch):
         pass
@@ -298,6 +342,10 @@
 
 class Job:
     wide = 256
+    kept = []
+
+    def hold(self, refs):
+        pass
 
     def __init__(self, whole, tiled, outs, tiles, flops):
         self.whole, self.tiled = whole, tiled
@@ -446,6 +494,11 @@
 
 
 class MixerJob:
+    kept = []
+
+    def hold(self, refs):
+        self.kept_refs = refs
+
     def __init__(self, inputs, outs, extra, phases, flops):
         self.inputs = list(inputs)
         self.out_shapes = [jax.ShapeDtypeStruct(shape, dtype) for shape, dtype in outs]
@@ -459,15 +512,14 @@
             + [
                 pltpu.SemaphoreType.DMA((len(self.inputs),)),
                 pltpu.SemaphoreType.DMA((len(outs),)),
-                pltpu.SemaphoreType.DMA((2,)),
             ]
         )
 
     def bind(self, ins, outs, scratch):
         self.in_refs, self.out_refs = ins, outs
-        extra = len(scratch) - len(ins) - len(outs) - 3
+        extra = len(scratch) - len(ins) - len(outs) - 2
         self.ins_v, self.outs_v, self.extra_v = split(scratch, [len(ins), len(outs), extra])
-        self.in_sem, self.out_sem, self.pass_sem = scratch[-3:]
+        self.in_sem, self.out_sem = scratch[-2:]
         self.count = lax.axis_size("seq")
         self.seq = lax.axis_index("seq")
         self.column = lax.axis_index("tp")
@@ -488,8 +540,8 @@
         return pltpu.make_async_remote_copy(
             src_ref=source,
             dst_ref=target,
-            send_sem=self.pass_sem.at[0],
-            recv_sem=self.pass_sem.at[1],
+            send_sem=self.kept_refs[1].at[0],
+            recv_sem=self.kept_refs[1].at[1],
             device_id=((self.seq + step) % self.count, self.column),
             device_id_type=MESH,
         )
@@ -536,7 +588,9 @@
 
 
 class EntryJob(MixerJob):
-    def __init__(self, tokens, gains, entry_full, exit_full, taps, bound):
+    then = None
+
+    def __init__(self, tokens, wide, entry_full, exit_full, bound):
         parts, rows, own = tokens.shape
         width, columns = exit_full.shape
         self.rows, self.columns, self.own = rows, columns, own
@@ -547,16 +601,17 @@
             ((rows, columns), LOW),
             ((16, columns), LOW),
             ((rows, columns), LOW),
-            ((parts * rows, own), LOW),
+            ((parts, rows, own), LOW),
             ((rows, 128), jnp.float32),
             ((width, rows), LOW),
         ]
         phases = [rows // 256, 3 * columns // 256, 1, columns // 128, width // 256]
         flops = 2 * rows * (entry_full.size + exit_full.size)
-        super().__init__([tokens, gains, entry_full, exit_full, taps, bound], outs, [], phases, flops)
+        super().__init__([tokens, wide, entry_full, exit_full, bound], outs, [], phases, flops)
+        self.kept = [pltpu.VMEM((16, columns), LOW), pltpu.SemaphoreType.DMA((2,))]
 
     def halo(self):
-        return self.passing(self.outs_v[2].at[pl.ds(self.rows - 16, 16)], self.outs_v[3], True)
+        return self.passing(self.outs_v[2].at[pl.ds(self.rows - 16, 16)], self.kept_refs[0], True)
 
     def before(self, phase):
         if phase == 0:
@@ -567,9 +622,9 @@
             self.store(7).start()
             self.load(2).wait()
         if phase == 3:
-            for which in (4, 5):
-                self.load(which).wait()
+            self.load(4).wait()
             self.halo().wait_recv()
+            self.outs_v[3][...] = self.kept_refs[0][...]
             self.store(3).start()
         if phase == 4:
             self.load(3).wait()
@@ -587,11 +642,16 @@
             self.store(5).start()
 
     def finish(self):
+        self.store(5).wait()
+        if self.then:
+            self.then.start()
         self.halo().wait_send()
-        super().finish()
+        for which in (0, 1, 2, 3, 4, 6, 7):
+            self.store(which).wait()
 
     def work(self, phase, index):
-        tokens, gains, entry, exits, taps, bound = self.ins_v
+        tokens, wide, entry, exits, bound = self.ins_v
+        taps = wide.at[self.column]
         projected, conv, gated, halo, mixer, term, scales, turned_rows = self.outs_v
         columns = self.columns
         if phase == 0:
@@ -601,7 +661,7 @@
             scale = lax.rsqrt(total / D + EPSILON)
             scales[rows, :] = jnp.broadcast_to(scale, (256, 128))
             for part, value in enumerate(values):
-                normed = (value * scale * gains[part, 0:1, :]).astype(LOW)
+                normed = (value * scale * wide[part, 3:4, :]).astype(LOW)
                 tokens[part, rows, :] = normed
                 turned_rows[part * self.own : (part + 1) * self.own, rows] = normed.T
         if phase == 1:
@@ -625,12 +685,13 @@
             mixer[:, span] = (projected[:, middle] * total).astype(LOW)
         if phase == 4:
             features = pl.ds(pl.multiple_of(index * 256, 256), 256)
-            window = owner_window(index, 256, self.own, self.rows)
-            term[window] = contract_cols(mixer[...], exits[features, :]).astype(LOW)
+            owner, inner = index // (self.own // 256), index % (self.own // 256)
+            span = pl.ds(pl.multiple_of(inner * 256, 256), 256)
+            term[owner, :, span] = contract_cols(mixer[...], exits[features, :]).astype(LOW)
 
 
 class MixerGradJob(MixerJob):
-    def __init__(self, branch, exit_full, entry_full, projected, conv, gated, halo, taps, bound):
+    def __init__(self, branch, exit_full, entry_full, projected, conv, gated, halo, wide, bound):
         parts, rows, own = branch.shape
         width, columns = exit_full.shape
         self.rows, self.columns, self.own = rows, columns, own
@@ -638,15 +699,15 @@
         extra = [
             pltpu.VMEM((rows, columns), jnp.float32),
             pltpu.VMEM((8, columns), jnp.float32),
-            pltpu.VMEM((8, columns), jnp.float32),
         ]
+        self.kept = [pltpu.VMEM((8, columns), jnp.float32), pltpu.SemaphoreType.DMA((2,))]
         phases = [columns // 256, 1, columns // 128, width // 256]
         flops = 2 * rows * (entry_full.size + exit_full.size)
-        inputs = [branch, exit_full, entry_full, projected, conv, gated, halo, taps, bound]
+        inputs = [branch, exit_full, entry_full, projected, conv, gated, halo, wide, bound]
         super().__init__(inputs, outs, extra, phases, flops)
 
     def back(self):
-        return self.passing(self.extra_v[1], self.extra_v[2], False)
+        return self.passing(self.extra_v[1], self.kept_refs[0], False)
 
     def before(self, phase):
         if phase == 0:
@@ -676,9 +737,11 @@
         super().finish()
 
     def work(self, phase, index):
-        branch, exits, entry, projected, conv, gated, halo, taps, bound = self.ins_v
+        branch, exits, entry, projected, conv, gated, halo, wide, bound = self.ins_v
+        taps = wide.at[self.column]
         grads, term, taps_grad = self.outs_v
-        conv_grad, sent, returned = self.extra_v
+        conv_grad, sent = self.extra_v
+        returned = self.kept_refs[0]
         columns, height = self.columns, self.rows
         if phase == 0:
             span = pl.ds(pl.multiple_of(index * 256, 256), 256)
@@ -729,8 +792,13 @@
         self.inputs = [item for job in jobs for item in job.inputs]
         self.out_shapes = [item for job in jobs for item in job.out_shapes]
         self.scratch = [item for job in jobs for item in job.scratch]
+        self.kept = [item for job in jobs for item in job.kept]
         self.tiles = sum(job.tiles for job in jobs)
         self.flops = sum(job.flops for job in jobs)
+
+    def hold(self, refs):
+        for job, own in zip(self.jobs, split(refs, [len(job.kept) for job in self.jobs])):
+            job.hold(own)
 
     def bind(self, ins, outs, scratch):
         groups = zip(
@@ -826,25 +894,29 @@
 class SmallGatherJob:
     tiles, flops = 1, 0
 
-    def __init__(self, own):
+    def __init__(self, own, seen):
         self.inputs = [own]
+        self.seen = seen
         devices, columns = lax.axis_size("seq"), lax.axis_size("tp")
-        whole = (devices, columns) + own.shape
-        self.out_shapes = [jax.ShapeDtypeStruct(whole, own.dtype)]
-        self.scratch = [
-            pltpu.VMEM(whole, own.dtype),
-            pltpu.SemaphoreType.DMA((2,)),
+        wide = (columns, 8, devices * seen)
+        self.out_shapes = [jax.ShapeDtypeStruct(wide, jnp.float32)]
+        self.scratch = [pltpu.VMEM(wide, jnp.float32), pltpu.SemaphoreType.DMA((2,))]
+        self.kept = [
+            pltpu.VMEM((devices, columns) + own.shape, own.dtype),
             pltpu.SemaphoreType.DMA((columns,)),
             pltpu.SemaphoreType.DMA((columns,)),
             pltpu.SemaphoreType.DMA((devices,)),
             pltpu.SemaphoreType.DMA((devices,)),
         ]
 
+    def hold(self, refs):
+        self.whole, self.near_send, self.near_recv, self.far_send, self.far_recv = refs
+        self.devices, self.columns = lax.axis_size("seq"), lax.axis_size("tp")
+        self.seq, self.column = lax.axis_index("seq"), lax.axis_index("tp")
+
     def bind(self, ins, outs, scratch):
         self.source, self.target = ins[0], outs[0]
-        self.whole, self.local_sem, self.near_send, self.near_recv, self.far_send, self.far_recv = scratch
-        self.devices, self.columns = lax.axis_size("seq"), lax.axis_size("tp")
-        self.seq, self.column = lax.axis_index("seq"), lax.axis_index("tp")
+        self.wide, self.local_sem = scratch
 
     def peers(self):
         near = [(self.seq, (self.column + step) % self.columns) for step in range(1, self.columns)]
@@ -896,7 +968,16 @@
             return carry
 
         lax.fori_loop(1, self.devices, end, 0)
-        store = pltpu.make_async_copy(self.whole, self.target, self.local_sem.at[1])
+        each = LANES // self.seen
+        for column in range(self.columns):
+            for start in range(0, self.devices, each):
+                total = None
+                for inner in range(each):
+                    piece = self.whole[start + inner, column, :, :].astype(jnp.float32)[:8]
+                    piece = pltpu.roll(piece, inner * self.seen, 1) if inner else piece
+                    total = piece if total is None else total + piece
+                self.wide[column, :, start * self.seen : start * self.seen + LANES] = total
+        store = pltpu.make_async_copy(self.wide, self.target, self.local_sem.at[1])
         store.start()
         store.wait()
 
@@ -907,23 +988,23 @@
     def __init__(self, inputs, outs, extra, rows, flops):
         self.columns = lax.axis_size("tp")
         blocks = rows // self.block
-        exchange = [
+        self.kept = [
             pltpu.VMEM((self.columns, blocks, self.block), jnp.float32),
-            pltpu.VMEM((blocks, self.block), jnp.float32),
             pltpu.SemaphoreType.DMA((self.columns,)),
             pltpu.SemaphoreType.DMA((self.columns,)),
         ]
-        super().__init__(inputs, outs, exchange + extra, [blocks, 1, blocks], flops)
+        totals = pltpu.VMEM((blocks, self.block), jnp.float32)
+        super().__init__(inputs, outs, [totals] + extra, [blocks, 1, blocks], flops)
 
     def peers(self):
         return [(self.seq, (self.column + step) % self.columns) for step in range(1, self.columns)]
 
     def share(self, step):
         return pltpu.make_async_remote_copy(
-            src_ref=self.extra_v[0].at[0],
-            dst_ref=self.extra_v[0].at[step],
-            send_sem=self.extra_v[2].at[step],
-            recv_sem=self.extra_v[3].at[step],
+            src_ref=self.kept_refs[0].at[0],
+            dst_ref=self.kept_refs[0].at[step],
+            send_sem=self.kept_refs[1].at[step],
+            recv_sem=self.kept_refs[2].at[step],
             device_id=(self.seq, (self.column + step) % self.columns),
             device_id_type=MESH,
         )
@@ -948,7 +1029,7 @@
 
     def work(self, phase, index):
         block = self.block
-        slots, totals = self.extra_v[:2]
+        slots, totals = self.kept_refs[0], self.extra_v[0]
         rows = pl.ds(pl.multiple_of(index * block, block), block)
         if phase == 0:
             part = jnp.sum(self.values(rows), axis=1, keepdims=True)
@@ -962,13 +1043,17 @@
 
 
 class NormJob(RowSumJob):
-    def __init__(self, rows_in, branch, gain):
+    then = None
+
+    def __init__(self, rows_in, terms, wide):
         rows, own = rows_in.shape
         outs = [((rows, own), jnp.float32), ((rows, own), LOW), ((rows, 128), jnp.float32)]
-        super().__init__([rows_in, branch, gain], outs, [], rows, 0)
+        super().__init__([rows_in, terms, wide], outs, [], rows, 0)
 
     def values(self, rows):
-        residual = self.ins_v[0][rows, :].astype(jnp.float32) + self.ins_v[1][rows, :].astype(jnp.float32)
+        rows_in, terms, _ = self.ins_v
+        residual = sum(terms[part, rows, :].astype(jnp.float32) for part in range(self.columns))
+        residual = rows_in[rows, :].astype(jnp.float32) + residual
         self.outs_v[0][rows, :] = residual
         return residual * residual
 
@@ -976,23 +1061,35 @@
         residual, normed, scales = self.outs_v
         scale = lax.rsqrt(total / D + EPSILON)
         scales[rows, :] = scale
-        normed[rows, :] = (residual[rows, :] * scale[:, 0:1] * self.ins_v[2][0:1, :]).astype(LOW)
+        gain = self.ins_v[2].at[self.column]
+        normed[rows, :] = (residual[rows, :] * scale[:, 0:1] * gain[4:5, :]).astype(LOW)
+
+    def finish(self):
+        self.store(1).wait()
+        if self.then:
+            self.then.start()
+        for step in range(1, self.columns):
+            self.share(step).wait_send()
+        for which in (0, 2):
+            self.store(which).wait()
 
 
 class NormBackJob(RowSumJob):
-    def __init__(self, grad, kept, scales, gain, base, rounded):
+    def __init__(self, grad, kept, scales, wide, row, base, rounded):
         rows, own = grad.shape
         outs = [((rows, own), jnp.float32), ((8, own), jnp.float32)]
         outs = outs + [((rows, own), LOW)] if rounded else outs
-        super().__init__([grad, kept, scales, gain, base], outs, [], rows, 0)
+        self.row = row
+        super().__init__([grad, kept, scales, wide, base], outs, [], rows, 0)
 
     def parts(self, rows):
-        grad, kept, scales, gain, base = self.ins_v
+        grad, kept, scales, wide, base = self.ins_v
+        gain = wide.at[self.column]
         return (
             grad[rows, :].astype(jnp.float32),
             kept[rows, :].astype(jnp.float32),
             scales[rows, 0:1],
-            gain[0:1, :],
+            gain[self.row : self.row + 1, :],
         )
 
     def before(self, phase):
@@ -1024,19 +1121,19 @@
         shape = taps_grad.shape
         self.before = before
         self.out_shapes = [jax.ShapeDtypeStruct(shape, jnp.float32)]
-        self.scratch = [
-            pltpu.VMEM(shape, jnp.float32),
-            pltpu.VMEM(shape, jnp.float32),
+        self.scratch = [pltpu.VMEM(shape, jnp.float32)] * 3 + [pltpu.SemaphoreType.DMA((3,))]
+        self.kept = [
             pltpu.VMEM((count,) + shape, jnp.float32),
-            pltpu.VMEM(shape, jnp.float32),
-            pltpu.SemaphoreType.DMA((3,)),
             pltpu.SemaphoreType.DMA((count,)),
             pltpu.SemaphoreType.DMA((count,)),
         ]
 
+    def hold(self, refs):
+        self.slots, self.send_sem, self.recv_sem = refs
+
     def bind(self, ins, outs, scratch):
         self.sources, self.target = ins, outs[0]
-        self.taps, self.gain, self.slots, self.total, self.local_sem, self.send_sem, self.recv_sem = scratch
+        self.taps, self.gain, self.total, self.local_sem = scratch
         self.count = lax.axis_size("seq")
         self.seq = lax.axis_index("seq")
         self.column = lax.axis_index("tp")
@@ -1098,35 +1195,182 @@
         store.wait()
 
 
+def with_ticks(job, ticks, tick, rest=None, ready=None):
+    rest = max(ticks // 6, 1) if rest is None else ticks * rest // 12
+    active = ticks - rest
+    each = -(-job.tiles // active)
+
+    def step(index, carry):
+        late = index - rest
+        if ready:
+            pl.when(late == -1)(ready)
+
+        first, after = late * job.tiles // active, (late + 1) * job.tiles // active
+        for inner in range(each):
+            tile = first + inner
+
+            @pl.when((late >= 0) & (tile < after))
+            def _(tile=tile):
+                job.tile(tile)
+
+        tick(index)
+        return carry
+
+    lax.fori_loop(0, ticks, step, 0)
+
+
 def ring_kernel(ring, job, *refs):
-    sizes = [len(group) for group in (ring.inputs, job.inputs, ring.out_shapes, job.out_shapes, ring.scratch, job.scratch)]
-    ring_in, job_in, ring_out, job_out, ring_scratch, job_scratch = split(refs, sizes)
+    parts = (ring.inputs, job.inputs, ring.out_shapes, job.out_shapes, ring.scratch, job.scratch, job.kept)
+    ring_in, job_in, ring_out, job_out, ring_scratch, job_scratch, job_kept = split(refs, [len(part) for part in parts])
     ring.bind(ring_in, ring_out, ring_scratch)
+    job.hold(job_kept)
     job.bind(job_in, job_out, job_scratch)
     ring.prepare()
     greet(ring.peers() + job.peers())
     ring.start()
     job.start()
-    rest = max(ring.ticks // 6, 1)
-    active = ring.ticks - rest
-    each = -(-job.tiles // active)
-
-    def step(index, carry):
-        late = index - rest
-        first, after = late * job.tiles // active, (late + 1) * job.tiles // active
-        for inner in range(each):
-            tile = first + inner
-
-            @pl.when((late >= 0) & (tile < after))
-            def _(tile=tile):
-                job.tile(tile)
-
-        ring.tick(index)
-        return carry
-
-    lax.fori_loop(0, ring.ticks, step, 0)
+    with_ticks(job, ring.ticks, ring.tick)
     ring.finish()
     job.finish()
+
+
+def run_forward(arrays, seen):
+    count, columns = lax.axis_size("seq"), lax.axis_size("tp")
+    shapes = {name: jax.ShapeDtypeStruct(array.shape, array.dtype) for name, array in arrays.items()}
+    inputs = list(shapes)
+    sections = []
+
+    def define(name, shape, dtype):
+        shapes[name] = jax.ShapeDtypeStruct(shape, dtype)
+
+    def add(job, ins, outs):
+        for name, shape in zip(outs, job.out_shapes):
+            shapes[name] = shape
+        return job, ins, outs
+
+    def flat_of(full):
+        shape = shapes[full].shape
+        return jax.ShapeDtypeStruct((shape[0] * shape[1], shape[2]), LOW)
+
+    rows, own = arrays["tokens"].shape
+    for name in ("tokens_blocks", "cot_blocks", "branch_terms", "normed_blocks"):
+        define(name, (columns, rows, own), LOW)
+    low = ["gate_low0", "up_low0", "gate_low1", "up_low1", "shrink_low0", "shrink_low1"]
+    small_job = SmallGatherJob(shapes["small"], seen)
+    cast_job = CastJob(shapes["pairs"], shapes["shrink"])
+    first = [add(small_job, ["small"], ["wide"]), add(cast_job, ["pairs", "shrink"], low)]
+    groups = [[("entry_low", "entry_full"), ("exit_low", "exit_full")]]
+    groups += [[(name, name.replace("low", "full"))] for name in low]
+    for group in groups:
+        for shard, full in group:
+            define(full, (count,) + shapes[shard].shape, LOW)
+    ring = GatherRing(groups, shapes)
+    tokens_sent = PeerCopies("tokens", "tokens_blocks")
+    cot_sent = PeerCopies("cotangent", "cot_blocks")
+    branch_sent = PeerCopies("term", "branch_terms")
+    normed_sent = PeerCopies("normed_own", "normed_blocks")
+    exchanges = [tokens_sent, cot_sent, branch_sent, normed_sent]
+
+    entry_job = EntryJob(
+        shapes["tokens_blocks"], shapes["wide"], flat_of("entry_full"), flat_of("exit_full"), shapes["bound"]
+    )
+    entry_job.then = branch_sent
+    entry_outs = ["projected", "conv_out", "gated", "halo", "mixer", "term", "scale_one", "normed_one"]
+    norm_job = NormJob(shapes["tokens"], shapes["branch_terms"], shapes["wide"])
+    norm_job.then = normed_sent
+    turn_cot = add(TurnJob(shapes["cot_blocks"]), ["cot_blocks"], ["cot_full"])
+    expands = []
+    for half in "01":
+        job = ExpandJob(shapes["normed_blocks"], flat_of("gate_full" + half), flat_of("up_full" + half))
+        names = ["normed_blocks", "gate_full" + half, "up_full" + half]
+        expands.append(add(job, names, ["gate_rows" + half, "up_rows" + half, "activation" + half]))
+    hidden_job = HiddenGradJob(shapes["cot_blocks"], flat_of("shrink_full0"), shapes["gate_rows0"], shapes["up_rows0"])
+    hidden = add(hidden_job, ["cot_blocks", "shrink_full0", "gate_rows0", "up_rows0"], ["gate_grad0", "up_grad0"])
+    turn_normed = add(TurnJob(shapes["normed_blocks"]), ["normed_blocks"], ["normed_two"])
+    entry = add(entry_job, ["tokens_blocks", "wide", "entry_full", "exit_full", "bound"], entry_outs)
+    norm = add(norm_job, ["tokens", "branch_terms", "wide"], ["residual", "normed_own", "scale_two"])
+    rests = [2, 1, 2, 4, 2, 4, 2]
+    sections = [
+        (first, []),
+        ([entry], [tokens_sent]),
+        ([turn_cot], [cot_sent]),
+        ([norm], [branch_sent]),
+        ([], []),
+        (expands, [normed_sent]),
+        ([hidden, turn_normed], []),
+    ]
+    outputs = [name for name in shapes if name not in inputs]
+    together = [Jobs(*[job for job, _, _ in jobs]) for jobs, _ in sections]
+    kept = [item for jobs in together for item in jobs.kept]
+    exchange_scratch = [item for exchange in exchanges for item in exchange.scratch]
+    weights_full = {full for group in groups for _, full in group}
+
+    def kernel(*all_refs):
+        in_refs, out_refs, ring_scratch, sems, kept_refs = split(
+            all_refs, [len(inputs), len(outputs), len(ring.scratch), len(exchange_scratch), len(kept)]
+        )
+        refs = dict(zip(inputs + outputs, in_refs + out_refs))
+        ring.bind(refs, ring_scratch)
+        for place, exchange in enumerate(exchanges):
+            exchange.bind(refs, sems[2 * place : 2 * place + 2])
+        for jobs, own in zip(together, split(kept_refs, [len(jobs.kept) for jobs in together])):
+            jobs.hold(own)
+        greet(small_job.peers())
+        ring.begin(0)
+        tokens_sent.start()
+        for group, (jobs, waits) in enumerate(sections):
+            job_ins = [rows_of(refs[name], name in weights_full) for _, ins, _ in jobs for name in ins]
+            job_outs = [refs[name] for _, _, outs in jobs for name in outs]
+
+            work = together[group]
+
+            def ready():
+                for exchange in waits:
+                    exchange.wait()
+                work.start()
+
+            def section(*scratch):
+                work.bind(job_ins, job_outs, list(scratch))
+                if not waits:
+                    work.start()
+                tick = functools.partial(ring.tick, group)
+                with_ticks(work, ring.ticks, tick, rests[group], ready if waits else None)
+                if group == 0:
+                    work.finish()
+                    cot_sent.start()
+                if group + 1 < len(sections):
+                    ring.begin(group + 1)
+                if group > 0:
+                    work.finish()
+
+            pl.run_scoped(section, *work.scratch)
+            ring.settle(group)
+        ring.finish()
+        for exchange in exchanges:
+            exchange.finish()
+
+    flops = sum(job.flops for jobs, _ in sections for job, _, _ in jobs)
+    results = pl.pallas_call(
+        kernel,
+        out_shape=[shapes[name] for name in outputs],
+        in_specs=[pl.BlockSpec(memory_space=pl.ANY)] * len(inputs),
+        out_specs=[pl.BlockSpec(memory_space=pl.ANY)] * len(outputs),
+        scratch_shapes=ring.scratch + exchange_scratch + kept,
+        compiler_params=pltpu.CompilerParams(
+            collective_id=0, has_side_effects=True, vmem_limit_bytes=VMEM_BYTES
+        ),
+        cost_estimate=pl.CostEstimate(flops=flops, bytes_accessed=10**9, transcendentals=0),
+        name="forward",
+    )(*arrays.values())
+    named = dict(zip(outputs, results))
+    return {name: flat(array) if name in weights_full else array for name, array in named.items()}
+
+
+def rows_of(ref, gathered):
+    if not gathered:
+        return ref
+    count, rows, columns = ref.shape
+    return ref.reshape(count * rows, columns)
 
 
 def run_ring(ring, job, collective):
@@ -1137,7 +1381,7 @@
         out_shape=outs,
         in_specs=[pl.BlockSpec(memory_space=pl.ANY)] * len(inputs),
         out_specs=[pl.BlockSpec(memory_space=pl.ANY)] * len(outs),
-        scratch_shapes=ring.scratch + job.scratch,
+        scratch_shapes=ring.scratch + job.scratch + job.kept,
         compiler_params=pltpu.CompilerParams(
             collective_id=collective, has_side_effects=True, vmem_limit_bytes=VMEM_BYTES
         ),
@@ -1291,57 +1535,36 @@
     gain_second,
 ):
     channels = tokens.shape[1]
-    count = lax.axis_size("seq")
     idle = NoJob()
     seen = conv_kernel.shape[1]
     small = jnp.concatenate([conv_kernel, norm_gains], axis=0)
-    small = jnp.pad(small, ((0, 16 - small.shape[0]), (0, 128 - seen))).astype(LOW)
+    small = jnp.pad(small, ((0, 16 - small.shape[0]), (0, LANES - seen))).astype(LOW)
     entry_low = entry_weight.reshape(entry_weight.shape[0], 3 * channels).astype(LOW)
     bound = jnp.broadcast_to(bounds[0], (8, 128))
-
-    tokens_blocks = gather_blocks(tokens)
-    cast = CastJob(paired(expand_weight), shrink_weight)
-    entry_full, exit_full, small_full, *low = run_ring(
-        GatherRing([entry_low, exit_weight.astype(LOW)]), Jobs(SmallGatherJob(small), cast), 0
-    )
-    entry_full, exit_full = flat(entry_full), flat(exit_full)
-    gate_low, up_low, shrink_low = low[0:4:2], low[1:4:2], low[4:6]
-    small_wide = small_full[:, :, :8, :seen].transpose(1, 2, 0, 3).reshape(-1, 8, channels).astype(jnp.float32)
-    taps = lax.dynamic_index_in_dim(small_wide, lax.axis_index("tp"), 0, False)
-    gain_blocks = small_wide[:, 3:4] + jnp.zeros((1, 8, 1), jnp.float32)
-    gain_one = jnp.broadcast_to(taps[3:4], taps.shape)
-    gain_two = jnp.broadcast_to(taps[4:5], taps.shape)
-    gate_full, up_full, shrink_full = [None] * 2, [None] * 2, [None] * 2
+    made = run_forward(
+        {
+            "entry_low": entry_low,
+            "exit_low": exit_weight.astype(LOW),
+            "small": small,
+            "tokens": tokens,
+            "cotangent": cotangent,
+            "bound": bound,
+            "pairs": paired(expand_weight),
+            "shrink": shrink_weight,
+        },
+        seen,
+    )
+    entry_full, exit_full, wide = made["entry_full"], made["exit_full"], made["wide"]
+    gate_full, up_full, shrink_full, activation, gate_rows, up_rows = (
+        [made[name + half] for half in "01"]
+        for name in ("gate_full", "up_full", "shrink_full", "activation", "gate_rows", "up_rows")
+    )
+    cot_blocks, cot_full, normed_one, normed_two = (
+        made[name] for name in ("cot_blocks", "cot_full", "normed_one", "normed_two")
+    )
+    residual, scale_one, scale_two = made["residual"], made["scale_one"], made["scale_two"]
+    gate_grad_one, up_grad_one = made["gate_grad0"], made["up_grad0"]
     shrink_part, gate_part, up_part = [None] * 2, [None] * 2, [None] * 2
-
-    tokens_blocks, cotangent_rows, entry_full = tie(tokens_blocks, cotangent, entry_full)
-    cot_blocks = gather_blocks(cotangent_rows)
-    full, projected, conv_out, gated_rows, halo, mixer_rows, branch_term, scale_one, normed_one = run_ring(
-        GatherRing([gate_low[0]]), EntryJob(tokens_blocks, gain_blocks, entry_full, exit_full, taps, bound), 1
-    )
-    gate_full[0] = flat(full)
-    cot_blocks, branch_term, up_low[0] = tie(cot_blocks, branch_term, up_low[0])
-    full, cot_full = run_ring(GatherRing([up_low[0]]), TurnJob(cot_blocks), 2)
-    branch, up_full[0] = tie(reduce_branch(branch_term), flat(full))
-    full, residual, own_normed_two, scale_two = run_ring(
-        GatherRing([gate_low[1]]), NormJob(tokens, branch, gain_two), 3
-    )
-    own_normed_two, gate_full[1], up_low[1] = tie(own_normed_two, flat(full), up_low[1])
-    (full,) = run_ring(GatherRing([up_low[1]]), idle, 4)
-    normed_blocks, up_full[1] = tie(gather_blocks(own_normed_two), flat(full))
-    full, *expanded = run_ring(
-        GatherRing([shrink_low[0]]),
-        Jobs(*[ExpandJob(normed_blocks, gate_full[half], up_full[half]) for half in range(2)]),
-        5,
-    )
-    gate_rows, up_rows, activation = expanded[0::3], expanded[1::3], expanded[2::3]
-    shrink_full[0] = flat(full)
-    full, gate_grad_one, up_grad_one, normed_two = run_ring(
-        GatherRing([shrink_low[1]]),
-        Jobs(HiddenGradJob(cot_blocks, shrink_full[0], gate_rows[0], up_rows[0]), TurnJob(normed_blocks)),
-        6,
-    )
-    shrink_full[1] = flat(full)
     hidden = HiddenGradJob(cot_blocks, shrink_full[1], gate_rows[1], up_rows[1])
     width = WidthJob([gate_grad_one, up_grad_one], [gate_full[0], up_full[0], gate_full[1], up_full[1]], hidden)
     shrink_part[0], gate_grad_two, up_grad_two, two_term = run_ring(
@@ -1354,7 +1577,7 @@
     grad_normed_two, shrink_part[1], mixed_term = tie(reduce_branch(two_term), shrink_part[1], mixed_term)
     gate_part[0], residual_grad, gain_two_grad, branch_own = run_ring(
         ScatterRing([(normed_two, gate_grad[0])]),
-        NormBackJob(grad_normed_two, residual, scale_two, gain_two, cotangent, True),
+        NormBackJob(grad_normed_two, residual, scale_two, wide, 4, cotangent, True),
         9,
     )
     mixed_branch, branch_own, up_grad[0] = tie(reduce_branch(mixed_term), branch_own, up_grad[0])
@@ -1362,15 +1585,25 @@
     branch_blocks, up_part[0] = tie(gather_blocks(branch_own), up_part[0])
     gate_part[1], projected_grad, one_term, taps_grad = run_ring(
         ScatterRing([(normed_two, gate_grad[1])]),
-        MixerGradJob(branch_blocks, exit_full, entry_full, projected, conv_out, gated_rows, halo, taps, bound),
+        MixerGradJob(
+            branch_blocks,
+            exit_full,
+            entry_full,
+            made["projected"],
+            made["conv_out"],
+            made["gated"],
+            made["halo"],
+            wide,
+            bound,
+        ),
         11,
     )
     one_term, up_grad[1], gate_part[1] = tie(one_term, up_grad[1], gate_part[1])
     up_part[1], branch_full = run_ring(ScatterRing([(normed_two, up_grad[1])]), TurnJob(branch_blocks), 12)
     grad_normed_one, up_part[1] = tie(reduce_branch(one_term), up_part[1])
-    back = NormBackJob(grad_normed_one, tokens, scale_one, gain_one, residual_grad, False)
+    back = NormBackJob(grad_normed_one, tokens, scale_one, wide, 3, residual_grad, False)
     entry_part, exit_part, tokens_grad, _, small_part = run_ring(
-        ScatterRing([(normed_one, projected_grad), (branch_full, mixer_rows)]),
+        ScatterRing([(normed_one, projected_grad), (branch_full, made["mixer"])]),
         Jobs(back, SmallSumJob(taps_grad, gain_two_grad, back)),
         13,
     )

time: 796 us -> 790 us (level)
    pallas_call x0 -> x1, Pallas kernels: none -> 353 us  [run_forward(): pl.pallas_call(kernel, out_shape=[shapes[name] for name in outputs], in_s...]
    pallas_call x14 -> x7, Pallas kernels: 718 us -> 368 us  [run_ring(): pl.pallas_call(functools.partial(ring_kernel, ring, job), out_shape=outs,...]
  transfers between devices with their start and end apart: 8 -> 4, of which waited for: 3 -> 1; matrix products, arithmetic and copies ran while one was open for 1% -> 0% of each run, Pallas kernels for 52% -> 24%
where the time goes in v5:
time: 790 us; the launch traced here: 780 us
  Pallas kernels  754 us (95%)
  between operations  15.1 us (2%)
    pallas_call x7, Pallas kernels, run_ring(): pl.pallas_call(functools.partial(ring_kernel, ring, job), out_shape=outs,...  368 us
    pallas_call x1, Pallas kernels, run_forward(): pl.pallas_call(kernel, out_shape=[shapes[name] for name in outputs], in_s...  353 us
    pallas_call x3, Pallas kernels, adam_rows(): pl.pallas_call(functools.partial(adam_kernel, len(grads)), out_shape=[jax...  18.4 us
  transfers between devices with their start and end apart: 4, of which 1 were waited for; matrix products, arithmetic and copies ran while one was open for 0% of the time, Pallas kernels for 24%

profile of v5, /device:TPU:0, one launch (start us, length us, event | category | flops | bytes accessed | tf_op | source)
XLA Modules:
  0.0 780.3 jit_solution(6406547836881924753)
XLA Ops:
  7.2 0.0 reduce-scatter.4.cloned.1.call-start
  8.0 1.7 copy.48
  9.6 1.2 copy.50.all_refs_0_
  10.8 0.7 convert_element_type.19.all_refs_1_
  11.6 0.6 fusion.5.all_refs_2_
  12.2 0.6 broadcast_in_dim.3.all_refs_5_.refs_10_
  12.8 352.8 %forward.1 = (bf16[4,1024,512]{2,1,0:T(8,128)(2,1)}, bf16[4,1024,512]{2,1,0:T(8,128)(2,1)}, bf16[4,1024,512]{2,1,0:T(8,128)(2,1)}, bf16[4,1024,512]{2,1,0:T(8,12...) custom-call(bf16[256,1536]{1,0:T(8,128)(2,1)} %copy.50.all_refs_0_, ...), custom_call_target="tpu_custom_call" | custom-call | flops 30064771072 | bytes 1000000000 | tf_op jit(solution)/shard_map/forward/pallas_call | solution.py:1353
  365.6 52.8 %ring_scatter.7 = (f32[256,1024]{1,0:T(8,128)}, bf16[1024,1024]{1,0:T(8,128)(2,1)}, bf16[1024,1024]{1,0:T(8,128)(2,1)}, bf16[4096,512]{1,0:T(8,128)(2,1)}) custom-call(bf16[2048,1024]{1,0:T(8,128)(2,1)} %get-tuple-element.93.refs_0_, bf16[1024,1024]{1,0:T(8,128)(2,1)} %get-tuple-element.94.refs_1_.refs_2_, bf16[4,1024,512]{2,1,0:T(8,128)(2,1)} %get-tuple-element.95.refs_2_, ...), custom_call_target="tpu_custom_call" | custom-call | flops 25769803776 | bytes 83886080 | tf_op jit(solution)/shard_map/ring_scatter/pallas_call | solution.py:1379
  418.4 0.0 reduce-scatter.4.cloned.1.call-update
  418.4 0.2 reduce-scatter.6.cloned.1.call-start
  418.7 43.2 %ring_scatter.8 = (f32[256,1024]{1,0:T(8,128)}, bf16[4096,512]{1,0:T(8,128)(2,1)}) custom-call(bf16[2048,1024]{1,0:T(8,128)(2,1)} %get-tuple-element.93.refs_0_, bf16[1024,1024]{1,0:T(8,128)(2,1)} %get-tuple-element.106.refs_1_.refs_3_, bf16[1024,1024]{1,0:T(8,128)(2,1)} %get-tuple-element.94.refs_1_.refs_2_, ...), custom_call_target="tpu_custom_call" | custom-call | flops 12884901888 | bytes 83886080 | tf_op jit(solution)/shard_map/ring_scatter/pallas_call | solution.py:1379
  461.9 0.0 reduce-scatter.4.cloned.1.call-done.refs_2_
  461.9 0.0 reduce-scatter.6.cloned.1.call-update
  462.0 0.0 all-gather.2.cloned.1.call-start
  462.0 46.0 %ring_scatter.9 = (f32[256,1024]{1,0:T(8,128)}, f32[1024,512]{1,0:T(8,128)}, f32[8,512]{1,0:T(8,128)}, bf16[1024,512]{1,0:T(8,128)(2,1)}) custom-call(bf16[2048,1024]{1,0:T(8,128)(2,1)} %get-tuple-element.111.refs_0_, bf16[1024,1024]{1,0:T(8,128)(2,1)} %get-tuple-element.99.refs_6_.refs_1_, bf16[1024,512]{1,0:T(8,128)(2,1)} %reduce-scatter.4.cloned.1.call-done.refs_2_, ...), custom_call_target="tpu_custom_call" | custom-call | flops 4294967296 | bytes 83886080 | tf_op jit(solution)/shard_map/ring_scatter/pallas_call | solution.py:1379
  508.0 1.1 reduce-scatter.6.cloned.1.call-done
  509.1 0.0 reduce-scatter.8.cloned.1.call-start
  509.1 46.0 %ring_scatter.10.refs_4_ = f32[256,1024]{1,0:T(8,128)} custom-call(bf16[2048,1024]{1,0:T(8,128)(2,1)} %get-tuple-element.111.refs_0_, bf16[1024,1024]{1,0:T(8,128)(2,1)} %get-tuple-element.120.refs_7_.refs_1_), custom_call_target="tpu_custom_call" | custom-call | flops 4294967296 | bytes 83886080 | tf_op jit(solution)/shard_map/ring_scatter/pallas_call | solution.py:1379
  555.1 0.0 all-gather.2.cloned.1.call-done
  555.1 47.8 %ring_scatter.11 = (f32[256,1024]{1,0:T(8,128)}, bf16[1024,1536]{1,0:T(8,128)(2,1)}, bf16[4096,512]{1,0:T(8,128)(2,1)}, f32[8,512]{1,0:T(8,128)}) custom-call(bf16[2048,1024]{1,0:T(8,128)(2,1)} %get-tuple-element.111.refs_0_, bf16[1024,1024]{1,0:T(8,128)(2,1)} %get-tuple-element.118.refs_1_, bf16[4,1024,512]{2,1,0:T(8,128)(2,1)} %bitcast.68, ...), custom_call_target="tpu_custom_call" | custom-call | flops 12884901888 | bytes 83886080 | tf_op jit(solution)/shard_map/ring_scatter/pallas_call | solution.py:1379
  603.0 9.2 %adam_rows.5 = (f32[256,2048]{1,0:T(8,128)}, f32[256,2048]{1,0:T(8,128)}, f32[256,2048]{1,0:T(8,128)}) custom-call(f32[256,2048]{1,0:T(8,128)} %refs_0_.3, f32[256,2048]{1,0:T(8,128)} %refs_1_.3, f32[256,2048]{1,0:T(8,128)} %refs_2_.3, f32[256,1024]{1,0:T(8,128)} %get-tuple-element.158.refs_3_, f32[256,1024]{1,0:T(8,128)} %get-tuple-element.159.refs_4_), custom_call_target="tpu_custom_call" | custom-call | flops 10485760 | bytes 14680064 | tf_op jit(solution)/shard_map/adam_rows/pallas_call | solution.py:1453
  612.3 1.3 add_convert_fusion
  613.6 44.7 %ring_scatter.12 = (f32[256,1024]{1,0:T(8,128)}, bf16[2048,1024]{1,0:T(8,128)(2,1)}) custom-call(bf16[2048,1024]{1,0:T(8,128)(2,1)} %get-tuple-element.111.refs_0_, bf16[1024,1024]{1,0:T(8,128)(2,1)} %get-tuple-element.131.refs_1_, bf16[4,1024,512]{2,1,0:T(8,128)(2,1)} %bitcast.69), custom_call_target="tpu_custom_call" | custom-call | flops 4294967296 | bytes 83886080 | tf_op jit(solution)/shard_map/ring_scatter/pallas_call | solution.py:1379
  658.3 0.0 reduce-scatter.8.cloned.1.call-done.refs_4_
  658.3 87.4 %ring_scatter.13 = (f32[256,1536]{1,0:T(8,128)}, f32[256,512]{1,0:T(8,128)}, f32[1024,512]{1,0:T(8,128)}, f32[8,512]{1,0:T(8,128)}, f32[8,512]{1,0:T(8,128)}) custom-call(bf16[2048,1024]{1,0:T(8,128)(2,1)} %get-tuple-element.117.refs_0_, bf16[2048,1024]{1,0:T(8,128)(2,1)} %get-tuple-element.132.refs_1_, bf16[1024,1536]{1,0:T(8,128)(2,1)} %get-tuple-element.133.refs_2_, ...), custom_call_target="tpu_custom_call" | custom-call | flops 8589934592 | bytes 167772160 | tf_op jit(solution)/shard_map/ring_scatter/pallas_call | solution.py:1379
  745.7 0.8 constant_dynamic-slice_fusion
  746.5 0.6 multiply_subtract_fusion
  747.1 0.6 multiply_subtract_fusion.1
  747.7 2.6 adam_rows.4
  750.3 6.6 adam_rows.3
  756.8 15.2 %adam_pairs.1 = (f32[8192,128]{1,0:T(8,128)}, f32[8192,128]{1,0:T(8,128)}, f32[8192,128]{1,0:T(8,128)}) custom-call(f32[8192,128]{1,0:T(8,128)} %bitcast.62, f32[8192,128]{1,0:T(8,128)} %bitcast.63, f32[8192,128]{1,0:T(8,128)} %bitcast.64, f32[256,1024]{1,0:T(8,128)} %get-tuple-element.151.refs_3_, f32[256,1024]{1,0:T(8,128)} %ring_scatter.10.refs_4_, ...), custom_call_target="tpu_custom_call" | custom-call | flops 20971520 | bytes 29360128 | tf_op jit(solution)/shard_map/adam_pairs/pallas_call | solution.py:1489
  772.0 1.3 copy.58
  (24 shorter events, 0.1 us)
Async XLA Ops:
  7.2 3.6 copy-start.2
  7.2 4.3 copy-start.4
  7.2 4.3 copy-start.7
  7.2 454.7 %reduce-scatter.4.cloned.1.call-start = ((), (), s32[]{:S(2)}) async-start(), calls=%async_computation.3 | async-start | bytes 5242880 | tf_op jit(solution)/shard_map/reduce_scatter | solution.py:1422
  418.4 90.6 %reduce-scatter.6.cloned.1.call-start = ((), (), s32[]{:S(2)}) async-start(), calls=%async_computation.4 | async-start | bytes 5242880 | tf_op jit(solution)/shard_map/reduce_scatter | solution.py:1422
  462.0 93.2 %all-gather.2.cloned.1.call-start = ((), (), s32[]{:S(2)}) async-start(), calls=%async_computation.5 | async-start | bytes 5242880 | tf_op jit(solution)/shard_map/all_gather | solution.py:1414
  509.1 149.2 %reduce-scatter.8.cloned.1.call-start = ((), (), s32[]{:S(2)}) async-start(), calls=%async_computation.6 | async-start | bytes 5242880 | tf_op jit(solution)/shard_map/reduce_scatter | solution.py:1422
  603.0 9.3 %copy-start = (f32[1024,512]{1,0:T(8,128)S(1)}, f32[1024,512]{1,0:T(8,128)}, u32[]{:S(2)}) copy-start(f32[1024,512]{1,0:T(8,128)} %get-tuple-element.92.refs_3_) | copy-start | bytes 6291460
  603.0 9.3 %copy-start.3 = (bf16[1024,512]{1,0:T(8,128)(2,1)S(1)}, bf16[1024,512]{1,0:T(8,128)(2,1)}, u32[]{:S(2)}) copy-start(bf16[1024,512]{1,0:T(8,128)(2,1)} %reduce-scatter.6.cloned.1.call-done) | copy-start | bytes 3145732
  658.3 88.2 %copy-start.5 = (f32[3,64]{1,0:T(4,128)S(1)}, f32[3,64]{1,0:T(4,128)}, u32[]{:S(2)}) copy-start(f32[3,64]{1,0:T(4,128)} %param.37) | copy-start | bytes 2308
  658.3 88.2 %copy-start.6 = (f32[3,64]{1,0:T(4,128)S(1)}, f32[3,64]{1,0:T(4,128)}, u32[]{:S(2)}) copy-start(f32[3,64]{1,0:T(4,128)} %param.38) | copy-start | bytes 2308
  658.3 88.8 %copy-start.8 = (f32[2,64]{1,0:T(2,128)S(1)}, f32[2,64]{1,0:T(2,128)}, u32[]{:S(2)}) copy-start(f32[2,64]{1,0:T(2,128)} %param.40) | copy-start | bytes 1540
  658.3 88.7 %copy-start.9 = (f32[2,64]{1,0:T(2,128)S(1)}, f32[2,64]{1,0:T(2,128)}, u32[]{:S(2)}) copy-start(f32[2,64]{1,0:T(2,128)} %param.41) | copy-start | bytes 1540
  756.8 15.2 %copy-start.1 = (f32[1024,512]{1,0:T(8,128)S(1)}, f32[1024,512]{1,0:T(8,128)}, u32[]{:S(2)}) copy-start(f32[1024,512]{1,0:T(8,128)} %get-tuple-element.191) | copy-start | bytes 6291460
Sparse Core Ops, SparseCore 0:
  418.6 43.1 reduce-scatter.3
  464.4 44.6 reduce-scatter.5
  510.6 34.4 all-gather.1
  603.1 42.9 reduce-scatter.7

commit v6 on v5

--- a/solution.py
+++ b/solution.py
@@ -70,6 +70,7 @@
         arrays = len(self.rows)
         sems = pltpu.SemaphoreType.DMA((arrays, 2, self.parts, self.count - 1))
         self.scratch = [sems, sems, pltpu.SemaphoreType.DMA((arrays,))]
+        self.flops = 0
 
     def bind(self, refs, scratch):
         self.refs = refs
@@ -113,6 +114,16 @@
             self.copy(shard, full, way, part, step - 1).wait_recv()
             self.copy(shard, full, way, part, step).start()
 
+    def prepare(self):
+        pass
+
+    def turn(self, group):
+        self.begin(group)
+        self.settle(group - 1)
+
+    def settled(self, group):
+        pass
+
     def settle(self, group):
         for part in range(self.parts):
             for shard, full, way in self.pieces(group):
@@ -180,164 +191,144 @@
 
 
 class ScatterRing:
-    name = "ring_scatter"
-
-    def __init__(self, pairs):
-        self.count = count = lax.axis_size("seq")
-        lefts = [left for left, right in pairs]
-        rights = [right for left, right in pairs]
-        self.inputs = lefts + rights
-        self.arrays = len(pairs)
-        self.rows = [left.shape[0] // count for left in lefts]
-        self.columns = [right.shape[1] for right in rights]
-        self.parts = 2 if min(self.columns) % 512 == 0 else 1
-        self.ticks = (count - 2) * self.parts
-        self.out_shapes = [
-            jax.ShapeDtypeStruct((row, width), jnp.float32) for row, width in zip(self.rows, self.columns)
+    def __init__(self, groups, places, shapes, wide):
+        self.count = lax.axis_size("seq")
+        self.groups, self.places, self.wide = groups, places, wide
+        self.names = list(places)
+        left = shapes[self.names[0]]
+        features, tokens = left.shape
+        self.rows = features // self.count
+        self.parts = 2
+        self.ticks = (self.count - 2) * self.parts
+        sems = pltpu.SemaphoreType.DMA((len(groups), 2, self.parts, self.count - 1))
+        buffers = max(places.values()) + 1
+        self.scratch = [
+            pltpu.VMEM((buffers, features, tokens), LOW),
+            pltpu.VMEM((2, 2, tokens, wide), LOW),
+            pltpu.VMEM((2, 2, self.count, self.rows, wide), LOW),
+            pltpu.VMEM((2, self.rows, 2 * wide), jnp.float32),
+            sems,
+            sems,
+            pltpu.SemaphoreType.DMA((len(self.names),)),
+            pltpu.SemaphoreType.DMA((2, 2)),
+            pltpu.SemaphoreType.DMA((2,)),
         ]
-        sems = pltpu.SemaphoreType.DMA((self.arrays, 2, self.parts, count - 1))
-        self.scratch = (
-            [pltpu.VMEM(left.shape, left.dtype) for left in lefts]
-            + [pltpu.VMEM(right.shape, right.dtype) for right in rights]
-            + [pltpu.VMEM((2, count, row, width // 2), LOW) for row, width in zip(self.rows, self.columns)]
-            + [pltpu.VMEM((row, width), jnp.float32) for row, width in zip(self.rows, self.columns)]
-            + [sems, sems, pltpu.SemaphoreType.DMA((self.arrays, count + 1)), pltpu.SemaphoreType.DMA((self.arrays,))]
-        )
-        self.flops = sum(2 * left.size * width for left, width in zip(lefts, self.columns))
-        self.bytes = 20 * sum(left.shape[0] * width * 2 for left, width in zip(lefts, self.columns))
-
-    def bind(self, ins, outs, scratch):
-        arrays = self.arrays
-        self.in_refs, self.out_refs = ins, outs
-        self.lefts, self.rights, self.slots, self.finals = split(scratch, [arrays] * 4)
-        self.send_sem, self.recv_sem, self.load_sem, self.done_sem = scratch[4 * arrays :]
+        self.flops = 4 * len(groups) * features * tokens * wide
+        self.out_shapes = [jax.ShapeDtypeStruct((self.rows, 2 * wide), jnp.float32)] * len(groups)
+
+    def bind(self, refs, scratch):
+        self.refs, self.out_refs = refs, [refs[name] for name in self.outs]
+        self.lefts, self.rights, self.slots, self.finals = scratch[:4]
+        self.send_sem, self.recv_sem, self.left_sem, self.right_sem, self.done_sem = scratch[4:]
         self.column = lax.axis_index("tp")
         self.place, self.ahead, self.behind = ring_ends(self.count)
 
-    def pieces(self):
-        return [(array, way) for array in range(self.arrays) for way in range(2)]
-
-    def span(self, array, way, part):
-        half = self.columns[array] // 2
-        width = half // self.parts
-        inner = part * width
-        return way * half + inner, inner, width
-
-    def term(self, array, way, part, step):
+    def left_load(self, name):
+        return pltpu.make_async_copy(
+            self.refs[name], self.lefts.at[self.places[name]], self.left_sem.at[self.names.index(name)]
+        )
+
+    def right_load(self, group, way):
+        _, name, start = self.groups[group][way]
+        source = self.refs[name].at[:, pl.ds(start, self.wide)]
+        return pltpu.make_async_copy(source, self.rights.at[group % 2, way], self.right_sem.at[group % 2, way])
+
+    def fetch(self, group):
+        for way in range(2):
+            self.right_load(group, way).start()
+
+    def span(self, part):
+        width = self.wide // self.parts
+        return pl.ds(pl.multiple_of(part * width, 128), width)
+
+    def term(self, group, way, part, step):
         move = (self.place + 2 * self.count - 1 - step) if way == 0 else (self.place + 1 + step)
         owner = ring_index(move % self.count, self.count)
-        rows = self.rows[array]
-        start, _, width = self.span(array, way, part)
-        left = self.lefts[array][pl.ds(pl.multiple_of(owner * rows, 16), rows), :]
-        right = self.rights[array][:, pl.ds(pl.multiple_of(start, 128), width)]
+        rows = pl.ds(pl.multiple_of(owner * self.rows, 16), self.rows)
+        left = self.lefts[self.places[self.groups[group][way][0]], rows, :]
+        right = self.rights[group % 2, way, :, self.span(part)]
         return jnp.dot(left, right, preferred_element_type=jnp.float32)
 
-    def held(self, array, way, part, step):
-        _, inner, width = self.span(array, way, part)
-        return self.slots[array].at[way, step, :, pl.ds(pl.multiple_of(inner, 128), width)]
-
-    def copy(self, array, way, part, step):
+    def held(self, group, way, part, step):
+        return self.slots.at[group % 2, way, step, :, self.span(part)]
+
+    def copy(self, group, way, part, step):
         return pltpu.make_async_remote_copy(
-            src_ref=self.held(array, way, part, step),
-            dst_ref=self.held(array, way, part, step + 1),
-            send_sem=self.send_sem.at[array, way, part, step],
-            recv_sem=self.recv_sem.at[array, way, part, step],
+            src_ref=self.held(group, way, part, step),
+            dst_ref=self.held(group, way, part, step + 1),
+            send_sem=self.send_sem.at[group, way, part, step],
+            recv_sem=self.recv_sem.at[group, way, part, step],
             device_id=(self.ahead if way == 0 else self.behind, self.column),
             device_id_type=MESH,
         )
 
-    def right_load(self, array):
-        return pltpu.make_async_copy(
-            self.in_refs[array + self.arrays], self.rights[array], self.load_sem.at[array, self.count]
-        )
-
-    def left_load(self, array, step):
-        owner = ring_index((self.place + 2 * self.count - 1 - step) % self.count, self.count)
-        rows = pl.ds(pl.multiple_of(owner * self.rows[array], 16), self.rows[array])
-        return pltpu.make_async_copy(
-            self.in_refs[array].at[rows], self.lefts[array].at[rows], self.load_sem.at[array, step]
-        )
-
-    def peers(self):
-        return [(self.ahead, self.column), (self.behind, self.column)]
+    def store(self, group):
+        return pltpu.make_async_copy(self.finals.at[group % 2], self.out_refs[group], self.done_sem.at[group % 2])
 
     def prepare(self):
-        for array in range(self.arrays):
-            self.right_load(array).start()
-            for step in (0, self.count - 2):
-                self.left_load(array, step).start()
-
-    def start(self):
-        later = list(range(1, self.count - 2)) + [self.count - 1]
-        for array in range(self.arrays):
-            for step in later:
-                self.left_load(array, step).start()
-        for array in range(self.arrays):
-            self.right_load(array).wait()
-            for step in (0, self.count - 2):
-                self.left_load(array, step).wait()
+        self.left_load("cot_full").start()
+        self.fetch(0)
+        self.left_load("normed_two").start()
+
+    def turn(self, group):
+        self.begin(group)
+        self.settle(group - 1)
+        self.settled(group - 1)
+
+    def settled(self, group):
+        if group + 2 < len(self.groups):
+            self.fetch(group + 2)
+        if group == 1:
+            self.left_load("normed_one").start()
+        if group == 5:
+            self.left_load("branch_full").start()
+
+    def begin(self, group):
+        for name, first in (("cot_full", 0), ("normed_two", 2), ("normed_one", 6), ("branch_full", 7)):
+            if group == first:
+                self.left_load(name).wait()
+        for way in range(2):
+            self.right_load(group, way).wait()
+        for part in range(self.parts):
+            for way in range(2):
+                self.held(group, way, part, 0)[...] = self.term(group, way, part, 0).astype(LOW)
+                self.copy(group, way, part, 0).start()
+
+    def tick(self, group, index):
+        step, part = 1 + index // self.parts, index % self.parts
+        for way in range(2):
+            mine = self.term(group, way, part, step)
+            self.copy(group, way, part, step - 1).wait_recv()
+            held = self.held(group, way, part, step)
+            held[...] = (held[...].astype(jnp.float32) + mine).astype(LOW)
+            self.copy(group, way, part, step).start()
+
+    def settle(self, group):
+        last = self.count - 1
+        if group >= 2:
+            self.store(group - 2).wait()
+        for part in range(self.parts):
+            for way in range(2):
+                mine = self.term(group, way, part, last)
+                self.copy(group, way, part, last - 1).wait_recv()
+                width = self.wide // self.parts
+                start = way * self.wide + part * width
+                self.finals[group % 2, :, start : start + width] = (
+                    self.held(group, way, part, last)[...].astype(jnp.float32) + mine
+                )
+        self.store(group).start()
+
+        def sent(step, carry):
             for part in range(self.parts):
                 for way in range(2):
-                    self.held(array, way, part, 0)[...] = self.term(array, way, part, 0).astype(LOW)
-                    self.copy(array, way, part, 0).start()
-        for array in range(self.arrays):
-            for step in later:
-                self.left_load(array, step).wait()
-
-    def tick(self, index):
-        step, part = 1 + index // self.parts, index % self.parts
-        for array, way in self.pieces():
-            mine = self.term(array, way, part, step)
-            self.copy(array, way, part, step - 1).wait_recv()
-            held = self.held(array, way, part, step)
-            held[...] = (held[...].astype(jnp.float32) + mine).astype(LOW)
-            self.copy(array, way, part, step).start()
+                    self.copy(group, way, part, step).wait_send()
+            return carry
+
+        lax.fori_loop(0, last, sent, 0)
 
     def finish(self):
-        last = self.count - 1
-        for part in range(self.parts):
-            for array, way in self.pieces():
-                start, _, width = self.span(array, way, part)
-                mine = self.term(array, way, part, last)
-                self.copy(array, way, part, last - 1).wait_recv()
-                self.finals[array][:, start : start + width] = (
-                    self.held(array, way, part, last)[...].astype(jnp.float32) + mine
-                )
-        stores = [
-            pltpu.make_async_copy(self.finals[array], self.out_refs[array], self.done_sem.at[array])
-            for array in range(self.arrays)
-        ]
-        for store in stores:
-            store.start()
-
-        def sent(step, carry):
-            for part in range(self.parts):
-                for array, way in self.pieces():
-                    self.copy(array, way, part, step).wait_send()
-            return carry
-
-        lax.fori_loop(0, last, sent, 0)
-        for store in stores:
-            store.wait()
-
-
-class NoJob:
-    inputs, out_shapes, scratch, kept, tiles, flops = [], [], [], [], 0, 0
-
-    def hold(self, refs):
-        pass
-
-    def bind(self, ins, outs, scratch):
-        pass
-
-    def peers(self):
-        return []
-
-    def start(self):
-        pass
-
-    def finish(self):
-        pass
+        for group in range(max(len(self.groups) - 2, 0), len(self.groups)):
+            self.store(group).wait()
 
 
 class Job:
@@ -466,31 +457,31 @@
 
 
 class WidthJob(Job):
-    def __init__(self, lefts, weights, before=None):
+    then = None
+
+    def __init__(self, lefts, weights):
         rows, width = lefts[0].shape[0], weights[0].shape[0]
         flops = 2 * rows * sum(weight.size for weight in weights)
-        self.own = width // lax.axis_size("tp")
-        self.height = rows
-        self.before = before
-        out = ((rows * lax.axis_size("tp"), self.own), LOW)
+        parts = lax.axis_size("tp")
+        self.own = width // parts
+        out = ((parts, rows, self.own), LOW)
         super().__init__(lefts, [(weight, 0) for weight in weights], [out], width // self.wide, flops)
 
     def out_window(self, index):
-        return owner_window(index, self.wide, self.own, self.height)
+        each = self.own // self.wide
+        return index // each, slice(None), pl.ds(pl.multiple_of(index % each * self.wide, 128), self.wide)
 
     def compute(self, whole, tiles):
         total = None
-        lefts = list(whole) + (list(self.before.outs_v) if self.before else [])
-        for left, weight in zip(lefts, tiles):
+        for left, weight in zip(whole, tiles):
             term = contract_cols(left[...], weight)
             total = term if total is None else total + term
         return (total.astype(LOW),)
 
-
-def owner_window(index, wide, own, height):
-    each = own // wide
-    rows = pl.ds(pl.multiple_of(index // each * height, 16), height)
-    return rows, pl.ds(pl.multiple_of(index % each * wide, 128), wide)
+    def finish(self):
+        super().finish()
+        if self.then:
+            self.then.start()
 
 
 class MixerJob:
@@ -691,11 +682,13 @@
 
 
 class MixerGradJob(MixerJob):
+    then = None
+
     def __init__(self, branch, exit_full, entry_full, projected, conv, gated, halo, wide, bound):
         parts, rows, own = branch.shape
         width, columns = exit_full.shape
         self.rows, self.columns, self.own = rows, columns, own
-        outs = [((rows, 3 * columns), LOW), ((parts * rows, own), LOW), ((8, columns), jnp.float32)]
+        outs = [((rows, 3 * columns), LOW), ((parts, rows, own), LOW), ((8, columns), jnp.float32)]
         extra = [
             pltpu.VMEM((rows, columns), jnp.float32),
             pltpu.VMEM((8, columns), jnp.float32),
@@ -733,8 +726,12 @@
             self.store(1).start()
 
     def finish(self):
+        self.store(1).wait()
+        if self.then:
+            self.then.start()
         self.back().wait_send()
-        super().finish()
+        for which in (0, 2):
+            self.store(which).wait()
 
     def work(self, phase, index):
         branch, exits, entry, projected, conv, gated, halo, wide, bound = self.ins_v
@@ -782,8 +779,9 @@
             taps_grad[2:3, span] = jnp.sum(rows * own_rows, axis=0, keepdims=True)
         if phase == 3:
             features = pl.ds(pl.multiple_of(index * 256, 256), 256)
-            window = owner_window(index, 256, self.own, height)
-            term[window] = contract_cols(grads[...], entry[features, :]).astype(LOW)
+            owner, inner = index // (self.own // 256), index % (self.own // 256)
+            span = pl.ds(pl.multiple_of(inner * 256, 256), 256)
+            term[owner, :, span] = contract_cols(grads[...], entry[features, :]).astype(LOW)
 
 
 class Jobs:
@@ -1075,18 +1073,20 @@
 
 
 class NormBackJob(RowSumJob):
-    def __init__(self, grad, kept, scales, wide, row, base, rounded):
-        rows, own = grad.shape
+    then = None
+
+    def __init__(self, terms, kept, scales, wide, row, base, rounded):
+        _, rows, own = terms.shape
         outs = [((rows, own), jnp.float32), ((8, own), jnp.float32)]
         outs = outs + [((rows, own), LOW)] if rounded else outs
         self.row = row
-        super().__init__([grad, kept, scales, wide, base], outs, [], rows, 0)
+        super().__init__([terms, kept, scales, wide, base], outs, [], rows, 0)
 
     def parts(self, rows):
-        grad, kept, scales, wide, base = self.ins_v
+        terms, kept, scales, wide, base = self.ins_v
         gain = wide.at[self.column]
         return (
-            grad[rows, :].astype(jnp.float32),
+            sum(terms[part, rows, :].astype(jnp.float32) for part in range(self.columns)),
             kept[rows, :].astype(jnp.float32),
             scales[rows, 0:1],
             gain[self.row : self.row + 1, :],
@@ -1110,6 +1110,35 @@
         self.outs_v[0][rows, :] = result
         if len(self.outs_v) > 2:
             self.outs_v[2][rows, :] = result.astype(LOW)
+
+    def finish(self):
+        if self.then:
+            self.store(2).wait()
+            self.then.start()
+        for step in range(1, self.columns):
+            self.share(step).wait_send()
+        for which in range(len(self.out_shapes)):
+            if which != 2 or not self.then:
+                self.store(which).wait()
+
+
+class SumJob(MixerJob):
+    def __init__(self, base, terms):
+        rows, own = base.shape
+        super().__init__([base, terms], [((rows, own), LOW)], [], [rows // 128], 0)
+
+    def before(self, phase):
+        for which in range(2):
+            self.load(which).wait()
+
+    def after(self, phase):
+        self.store(0).start()
+
+    def work(self, phase, index):
+        base, terms = self.ins_v
+        rows = pl.ds(pl.multiple_of(index * 128, 128), 128)
+        total = sum(terms[part, rows, :].astype(jnp.float32) for part in range(terms.shape[0]))
+        self.outs_v[0][rows, :] = (base[rows, :] + total).astype(LOW)
 
 
 class SmallSumJob:
@@ -1195,175 +1224,265 @@
         store.wait()
 
 
-def with_ticks(job, ticks, tick, rest=None, ready=None):
-    rest = max(ticks // 6, 1) if rest is None else ticks * rest // 12
-    active = ticks - rest
-    each = -(-job.tiles // active)
-
-    def step(index, carry):
-        late = index - rest
-        if ready:
-            pl.when(late == -1)(ready)
-
-        first, after = late * job.tiles // active, (late + 1) * job.tiles // active
-        for inner in range(each):
-            tile = first + inner
-
-            @pl.when((late >= 0) & (tile < after))
-            def _(tile=tile):
-                job.tile(tile)
-
-        tick(index)
-        return carry
-
-    lax.fori_loop(0, ticks, step, 0)
-
-
-def ring_kernel(ring, job, *refs):
-    parts = (ring.inputs, job.inputs, ring.out_shapes, job.out_shapes, ring.scratch, job.scratch, job.kept)
-    ring_in, job_in, ring_out, job_out, ring_scratch, job_scratch, job_kept = split(refs, [len(part) for part in parts])
-    ring.bind(ring_in, ring_out, ring_scratch)
-    job.hold(job_kept)
-    job.bind(job_in, job_out, job_scratch)
-    ring.prepare()
-    greet(ring.peers() + job.peers())
-    ring.start()
-    job.start()
-    with_ticks(job, ring.ticks, ring.tick)
-    ring.finish()
-    job.finish()
+class Section:
+    def __init__(self, ranges, jobs=(), waits=(), rest=1, calls=(), early=True):
+        self.ranges, self.jobs, self.waits, self.rest, self.calls, self.early = ranges, jobs, waits, rest, calls, early
+        self.job = Jobs(*[job for job, _, _ in jobs])
+
+    def run(self, ring, ins, outs):
+        job = self.job
+        ranges = [(group, low * ring.ticks // 12, high * ring.ticks // 12) for group, low, high in self.ranges]
+        total = sum(high - low for _, low, high in ranges)
+        rest = self.rest * ring.ticks // 12
+        active = total - rest
+        each = -(-job.tiles // active)
+
+        def ready():
+            for exchange in self.waits:
+                exchange.wait()
+            job.start()
+
+        def body(*scratch):
+            job.bind(ins, outs, list(scratch))
+            if not self.waits:
+                job.start()
+            done = 0
+            for place, (group, low, high) in enumerate(ranges):
+                if low == 0 and group > 0 and place > 0:
+                    ring.turn(group)
+                if place == 0:
+                    for call in self.calls:
+                        call.start()
+
+                def step(index, carry, group=group, shift=done - low):
+                    late = index + shift - rest
+                    first, after = late * job.tiles // active, (late + 1) * job.tiles // active
+                    if self.waits:
+                        pl.when(late == -1)(ready)
+                    for inner in range(each):
+                        tile = first + inner
+
+                        @pl.when((late >= 0) & (tile < after))
+                        def _(tile=tile):
+                            job.tile(tile)
+
+                    ring.tick(group, index)
+                    return carry
+
+                lax.fori_loop(low, high, step, 0)
+                done += high - low
+            group, _, high = ranges[-1]
+            ends = high == ring.ticks and group + 1 < len(ring.groups)
+            if ends and self.early:
+                ring.begin(group + 1)
+            job.finish()
+            if ends and not self.early:
+                ring.begin(group + 1)
+
+        pl.run_scoped(body, *job.scratch)
+        group, _, high = ranges[-1]
+        if high == ring.ticks:
+            ring.settle(group)
+            ring.settled(group)
+
+
+class Plan:
+    def __init__(self, arrays):
+        self.arrays = arrays
+        self.shapes = {name: jax.ShapeDtypeStruct(array.shape, array.dtype) for name, array in arrays.items()}
+        self.inputs = list(self.shapes)
+        self.weights = set()
+
+    def define(self, name, shape, dtype):
+        self.shapes[name] = jax.ShapeDtypeStruct(shape, dtype)
+
+    def add(self, job, ins, outs):
+        for name, shape in zip(outs, job.out_shapes):
+            self.shapes[name] = shape
+        return job, ins, outs
+
+    def flat(self, full):
+        shape = self.shapes[full].shape
+        return jax.ShapeDtypeStruct((shape[0] * shape[1], shape[2]), LOW)
+
+    def run(self, ring, sections, exchanges, peers, start, name, collective):
+        inputs = self.inputs
+        outputs = [made for made in self.shapes if made not in inputs]
+        kept = [item for section in sections for item in section.job.kept]
+        sems = [item for exchange in exchanges for item in exchange.scratch]
+
+        def kernel(*all_refs):
+            in_refs, out_refs, ring_scratch, sem_refs, kept_refs = split(
+                all_refs, [len(inputs), len(outputs), len(ring.scratch), len(sems), len(kept)]
+            )
+            refs = dict(zip(inputs + outputs, in_refs + out_refs))
+            ring.bind(refs, ring_scratch)
+            for place, exchange in enumerate(exchanges):
+                exchange.bind(refs, sem_refs[2 * place : 2 * place + 2])
+            for section, own in zip(sections, split(kept_refs, [len(section.job.kept) for section in sections])):
+                section.job.hold(own)
+            ring.prepare()
+            greet(peers())
+            ring.begin(0)
+            ring.settled(-1)
+            for exchange in start:
+                exchange.start()
+            for section in sections:
+                ins = [rows_of(refs[made], made in self.weights) for _, names, _ in section.jobs for made in names]
+                outs = [refs[made] for _, _, names in section.jobs for made in names]
+                section.run(ring, ins, outs)
+            ring.finish()
+            for exchange in exchanges:
+                exchange.finish()
+
+        flops = ring.flops + sum(section.job.flops for section in sections)
+        results = pl.pallas_call(
+            kernel,
+            out_shape=[self.shapes[made] for made in outputs],
+            in_specs=[pl.BlockSpec(memory_space=pl.ANY)] * len(inputs),
+            out_specs=[pl.BlockSpec(memory_space=pl.ANY)] * len(outputs),
+            scratch_shapes=ring.scratch + sems + kept,
+            compiler_params=pltpu.CompilerParams(
+                collective_id=collective, has_side_effects=True, vmem_limit_bytes=VMEM_BYTES
+            ),
+            cost_estimate=pl.CostEstimate(flops=flops, bytes_accessed=10**9, transcendentals=0),
+            name=name,
+        )(*self.arrays.values())
+        named = dict(zip(outputs, results))
+        return {made: flat(array) if made in self.weights else array for made, array in named.items()}
+
+
+def row_and_column_peers():
+    seq, column = lax.axis_index("seq"), lax.axis_index("tp")
+    devices, columns = lax.axis_size("seq"), lax.axis_size("tp")
+    near = [(seq, (column + step) % columns) for step in range(1, columns)]
+    return near + [((seq + step) % devices, column) for step in range(1, devices)]
 
 
 def run_forward(arrays, seen):
     count, columns = lax.axis_size("seq"), lax.axis_size("tp")
-    shapes = {name: jax.ShapeDtypeStruct(array.shape, array.dtype) for name, array in arrays.items()}
-    inputs = list(shapes)
-    sections = []
-
-    def define(name, shape, dtype):
-        shapes[name] = jax.ShapeDtypeStruct(shape, dtype)
-
-    def add(job, ins, outs):
-        for name, shape in zip(outs, job.out_shapes):
-            shapes[name] = shape
-        return job, ins, outs
-
-    def flat_of(full):
-        shape = shapes[full].shape
-        return jax.ShapeDtypeStruct((shape[0] * shape[1], shape[2]), LOW)
-
+    plan = Plan(arrays)
+    shapes, add = plan.shapes, plan.add
     rows, own = arrays["tokens"].shape
     for name in ("tokens_blocks", "cot_blocks", "branch_terms", "normed_blocks"):
-        define(name, (columns, rows, own), LOW)
+        plan.define(name, (columns, rows, own), LOW)
     low = ["gate_low0", "up_low0", "gate_low1", "up_low1", "shrink_low0", "shrink_low1"]
-    small_job = SmallGatherJob(shapes["small"], seen)
-    cast_job = CastJob(shapes["pairs"], shapes["shrink"])
-    first = [add(small_job, ["small"], ["wide"]), add(cast_job, ["pairs", "shrink"], low)]
+    small = add(SmallGatherJob(shapes["small"], seen), ["small"], ["wide"])
+    cast = add(CastJob(shapes["pairs"], shapes["shrink"]), ["pairs", "shrink"], low)
     groups = [[("entry_low", "entry_full"), ("exit_low", "exit_full")]]
     groups += [[(name, name.replace("low", "full"))] for name in low]
     for group in groups:
         for shard, full in group:
-            define(full, (count,) + shapes[shard].shape, LOW)
+            plan.define(full, (count,) + shapes[shard].shape, LOW)
+            plan.weights.add(full)
     ring = GatherRing(groups, shapes)
     tokens_sent = PeerCopies("tokens", "tokens_blocks")
     cot_sent = PeerCopies("cotangent", "cot_blocks")
     branch_sent = PeerCopies("term", "branch_terms")
     normed_sent = PeerCopies("normed_own", "normed_blocks")
-    exchanges = [tokens_sent, cot_sent, branch_sent, normed_sent]
 
     entry_job = EntryJob(
-        shapes["tokens_blocks"], shapes["wide"], flat_of("entry_full"), flat_of("exit_full"), shapes["bound"]
+        shapes["tokens_blocks"], shapes["wide"], plan.flat("entry_full"), plan.flat("exit_full"), shapes["bound"]
     )
     entry_job.then = branch_sent
-    entry_outs = ["projected", "conv_out", "gated", "halo", "mixer", "term", "scale_one", "normed_one"]
+    entry = add(
+        entry_job,
+        ["tokens_blocks", "wide", "entry_full", "exit_full", "bound"],
+        ["projected", "conv_out", "gated", "halo", "mixer", "term", "scale_one", "normed_one"],
+    )
+    turn_cot = add(TurnJob(shapes["cot_blocks"]), ["cot_blocks"], ["cot_full"])
     norm_job = NormJob(shapes["tokens"], shapes["branch_terms"], shapes["wide"])
     norm_job.then = normed_sent
-    turn_cot = add(TurnJob(shapes["cot_blocks"]), ["cot_blocks"], ["cot_full"])
+    norm = add(norm_job, ["tokens", "branch_terms", "wide"], ["residual", "normed_own", "scale_two"])
     expands = []
     for half in "01":
-        job = ExpandJob(shapes["normed_blocks"], flat_of("gate_full" + half), flat_of("up_full" + half))
+        job = ExpandJob(shapes["normed_blocks"], plan.flat("gate_full" + half), plan.flat("up_full" + half))
         names = ["normed_blocks", "gate_full" + half, "up_full" + half]
         expands.append(add(job, names, ["gate_rows" + half, "up_rows" + half, "activation" + half]))
-    hidden_job = HiddenGradJob(shapes["cot_blocks"], flat_of("shrink_full0"), shapes["gate_rows0"], shapes["up_rows0"])
+    hidden_job = HiddenGradJob(shapes["cot_blocks"], plan.flat("shrink_full0"), shapes["gate_rows0"], shapes["up_rows0"])
     hidden = add(hidden_job, ["cot_blocks", "shrink_full0", "gate_rows0", "up_rows0"], ["gate_grad0", "up_grad0"])
     turn_normed = add(TurnJob(shapes["normed_blocks"]), ["normed_blocks"], ["normed_two"])
-    entry = add(entry_job, ["tokens_blocks", "wide", "entry_full", "exit_full", "bound"], entry_outs)
-    norm = add(norm_job, ["tokens", "branch_terms", "wide"], ["residual", "normed_own", "scale_two"])
-    rests = [2, 1, 2, 4, 2, 4, 2]
     sections = [
-        (first, []),
-        ([entry], [tokens_sent]),
-        ([turn_cot], [cot_sent]),
-        ([norm], [branch_sent]),
-        ([], []),
-        (expands, [normed_sent]),
-        ([hidden, turn_normed], []),
+        Section([(0, 0, 12)], [small, cast], early=False),
+        Section([(1, 0, 12)], [entry], [tokens_sent], calls=[cot_sent]),
+        Section([(2, 0, 12)], [turn_cot], [cot_sent], rest=3),
+        Section([(3, 0, 12)], [norm], [branch_sent], rest=4),
+        Section([(4, 0, 12)]),
+        Section([(5, 0, 12)], expands, [normed_sent], rest=4),
+        Section([(6, 0, 12)], [hidden, turn_normed]),
     ]
-    outputs = [name for name in shapes if name not in inputs]
-    together = [Jobs(*[job for job, _, _ in jobs]) for jobs, _ in sections]
-    kept = [item for jobs in together for item in jobs.kept]
-    exchange_scratch = [item for exchange in exchanges for item in exchange.scratch]
-    weights_full = {full for group in groups for _, full in group}
-
-    def kernel(*all_refs):
-        in_refs, out_refs, ring_scratch, sems, kept_refs = split(
-            all_refs, [len(inputs), len(outputs), len(ring.scratch), len(exchange_scratch), len(kept)]
-        )
-        refs = dict(zip(inputs + outputs, in_refs + out_refs))
-        ring.bind(refs, ring_scratch)
-        for place, exchange in enumerate(exchanges):
-            exchange.bind(refs, sems[2 * place : 2 * place + 2])
-        for jobs, own in zip(together, split(kept_refs, [len(jobs.kept) for jobs in together])):
-            jobs.hold(own)
-        greet(small_job.peers())
-        ring.begin(0)
-        tokens_sent.start()
-        for group, (jobs, waits) in enumerate(sections):
-            job_ins = [rows_of(refs[name], name in weights_full) for _, ins, _ in jobs for name in ins]
-            job_outs = [refs[name] for _, _, outs in jobs for name in outs]
-
-            work = together[group]
-
-            def ready():
-                for exchange in waits:
-                    exchange.wait()
-                work.start()
-
-            def section(*scratch):
-                work.bind(job_ins, job_outs, list(scratch))
-                if not waits:
-                    work.start()
-                tick = functools.partial(ring.tick, group)
-                with_ticks(work, ring.ticks, tick, rests[group], ready if waits else None)
-                if group == 0:
-                    work.finish()
-                    cot_sent.start()
-                if group + 1 < len(sections):
-                    ring.begin(group + 1)
-                if group > 0:
-                    work.finish()
-
-            pl.run_scoped(section, *work.scratch)
-            ring.settle(group)
-        ring.finish()
-        for exchange in exchanges:
-            exchange.finish()
-
-    flops = sum(job.flops for jobs, _ in sections for job, _, _ in jobs)
-    results = pl.pallas_call(
-        kernel,
-        out_shape=[shapes[name] for name in outputs],
-        in_specs=[pl.BlockSpec(memory_space=pl.ANY)] * len(inputs),
-        out_specs=[pl.BlockSpec(memory_space=pl.ANY)] * len(outputs),
-        scratch_shapes=ring.scratch + exchange_scratch + kept,
-        compiler_params=pltpu.CompilerParams(
-            collective_id=0, has_side_effects=True, vmem_limit_bytes=VMEM_BYTES
-        ),
-        cost_estimate=pl.CostEstimate(flops=flops, bytes_accessed=10**9, transcendentals=0),
-        name="forward",
-    )(*arrays.values())
-    named = dict(zip(outputs, results))
-    return {name: flat(array) if name in weights_full else array for name, array in named.items()}
+    exchanges = [tokens_sent, cot_sent, branch_sent, normed_sent]
+    return plan.run(ring, sections, exchanges, row_and_column_peers, [tokens_sent], "forward", 0)
+
+
+def run_backward(arrays):
+    columns = lax.axis_size("tp")
+    plan = Plan(arrays)
+    shapes, add = plan.shapes, plan.add
+    rows, own = arrays["tokens"].shape
+    for name in ("two_terms", "mixed_terms", "branch_blocks", "one_terms"):
+        plan.define(name, (columns, rows, own), LOW)
+    two_sent = PeerCopies("two_term", "two_terms")
+    mixed_sent = PeerCopies("mixed_term", "mixed_terms")
+    branch_sent = PeerCopies("branch_own", "branch_blocks")
+    one_sent = PeerCopies("one_term", "one_terms")
+
+    hidden = add(
+        HiddenGradJob(shapes["cot_blocks"], shapes["shrink_full1"], shapes["gate_rows1"], shapes["up_rows1"]),
+        ["cot_blocks", "shrink_full1", "gate_rows1", "up_rows1"],
+        ["gate_grad1", "up_grad1"],
+    )
+    names = [["gate_grad0", "up_grad0", "gate_grad1", "up_grad1"], ["gate_full0", "up_full0", "gate_full1", "up_full1"]]
+    two_job = WidthJob(*[[shapes[name] for name in side] for side in names])
+    two_job.then = two_sent
+    two = add(two_job, names[0] + names[1], ["two_term"])
+    names = [["activation0", "activation1"], ["shrink_full0", "shrink_full1"]]
+    mixed = add(WidthJob(*[[shapes[name] for name in side] for side in names]), names[0] + names[1], ["mixed_term"])
+    back_two = NormBackJob(
+        shapes["two_terms"], shapes["residual"], shapes["scale_two"], shapes["wide"], 4, shapes["cotangent"], True
+    )
+    back_two.then = branch_sent
+    names = ["two_terms", "residual", "scale_two", "wide", "cotangent"]
+    norm_two = add(back_two, names, ["residual_grad", "gain_two_grad", "branch_own"])
+    names = ["branch_blocks", "exit_full", "entry_full", "projected", "conv_out", "gated", "halo", "wide", "bound"]
+    mixer_job = MixerGradJob(*[shapes[name] for name in names])
+    mixer_job.then = one_sent
+    mixer = add(mixer_job, names, ["projected_grad", "one_term", "taps_grad"])
+    turn = add(TurnJob(shapes["branch_blocks"]), ["branch_blocks"], ["branch_full"])
+    back_one = NormBackJob(
+        shapes["one_terms"], shapes["tokens"], shapes["scale_one"], shapes["wide"], 3, shapes["residual_grad"], False
+    )
+    names = ["one_terms", "tokens", "scale_one", "wide", "residual_grad"]
+    norm_one = add(back_one, names, ["tokens_grad", "gain_one_grad"])
+    small_job = SmallSumJob(shapes["taps_grad"], shapes["gain_two_grad"], back_one)
+    small = add(small_job, ["taps_grad", "gain_two_grad"], ["small_part"])
+    total = add(SumJob(shapes["residual"], shapes["mixed_terms"]), ["residual", "mixed_terms"], ["mixed"])
+
+    wide = own
+    halves = [("cot_full", "activation0"), ("cot_full", "activation1")]
+    halves += [("normed_two", name) for name in ("gate_grad0", "up_grad0", "gate_grad1", "up_grad1")]
+    halves += [("normed_one", "projected_grad")]
+    groups = [[(left, right, 0), (left, right, wide)] for left, right in halves]
+    groups += [[("normed_one", "projected_grad", 2 * wide), ("branch_full", "mixer", 0)]]
+    places = {"cot_full": 0, "normed_two": 1, "normed_one": 0, "branch_full": 2}
+    ring = ScatterRing(groups, places, shapes, wide)
+    sums = ["shrink0", "shrink1", "gate0", "up0", "gate1", "up1", "entry", "entry_exit"]
+    for name, shape in zip(sums, ring.out_shapes):
+        plan.shapes[name] = shape
+    ring.outs = sums
+    sections = [
+        Section([(0, 0, 5)], [hidden]),
+        Section([(0, 5, 12), (1, 0, 4)], [two]),
+        Section([(1, 4, 12), (2, 0, 5)], [mixed]),
+        Section([(2, 5, 12)], [norm_two], [two_sent]),
+        Section([(3, 0, 12)]),
+        Section([(4, 0, 12)], [mixer], [branch_sent], rest=2),
+        Section([(5, 0, 12)], [turn], calls=[mixed_sent]),
+        Section([(6, 0, 12)], [norm_one, small], [one_sent], rest=3),
+        Section([(7, 0, 12)], [total], [mixed_sent]),
+    ]
+    exchanges = [two_sent, mixed_sent, branch_sent, one_sent]
+    return plan.run(ring, sections, exchanges, row_and_column_peers, [], "backward", 1)
 
 
 def rows_of(ref, gathered):
@@ -1373,53 +1492,14 @@
     return ref.reshape(count * rows, columns)
 
 
-def run_ring(ring, job, collective):
-    inputs = ring.inputs + job.inputs
-    outs = ring.out_shapes + job.out_shapes
-    return pl.pallas_call(
-        functools.partial(ring_kernel, ring, job),
-        out_shape=outs,
-        in_specs=[pl.BlockSpec(memory_space=pl.ANY)] * len(inputs),
-        out_specs=[pl.BlockSpec(memory_space=pl.ANY)] * len(outs),
-        scratch_shapes=ring.scratch + job.scratch + job.kept,
-        compiler_params=pltpu.CompilerParams(
-            collective_id=collective, has_side_effects=True, vmem_limit_bytes=VMEM_BYTES
-        ),
-        cost_estimate=pl.CostEstimate(flops=ring.flops + job.flops, bytes_accessed=ring.bytes, transcendentals=0),
-        name=ring.name,
-    )(*inputs)
-
-
 def flat(full):
     return full.reshape(full.shape[0] * full.shape[1], full.shape[2])
-
-
-def contract_rows(left, right):
-    return lax.dot_general(
-        left, right, (((0,), (0,)), ((), ())), preferred_element_type=jnp.float32
-    )
 
 
 def contract_cols(left, right):
     return lax.dot_general(
         left, right, (((1,), (1,)), ((), ())), preferred_element_type=jnp.float32
     )
-
-
-def tie(*values):
-    return lax.optimization_barrier(values)
-
-
-def gather_rows(own):
-    return lax.all_gather(own, "tp", axis=0, tiled=True)
-
-
-def gather_blocks(own):
-    return gather_rows(own).reshape(-1, *own.shape)
-
-
-def reduce_branch(term):
-    return lax.psum_scatter(term, "tp", scatter_dimension=0, tiled=True)
 
 
 def adam_update(weight, first, second, grad, rate, decay):
@@ -1442,23 +1522,56 @@
             out[:, span] = result
 
 
-def adam_rows(weight, first, second, grads, planes=1):
-    rows, columns = weight.shape[0] // planes, weight.shape[1]
-    block = max(rows // 8, 8) if columns > 1024 else max(rows // 2, 8)
-    steps = rows // block
-    state = pl.BlockSpec((block, columns), lambda plane, step: (plane * steps + step, 0))
-    grad_specs = [
-        pl.BlockSpec((block, grad.shape[1] // planes), lambda plane, step: (step, plane)) for grad in grads
-    ]
+def adam_rows(weight, first, second, grads):
+    rows, columns = weight.shape
+    block = max(rows // 4, 8)
+    state = pl.BlockSpec((block, columns), lambda step: (step, 0))
+    grad_specs = [pl.BlockSpec((block, grad.shape[1]), lambda step: (step, 0)) for grad in grads]
     return pl.pallas_call(
         functools.partial(adam_kernel, len(grads)),
         out_shape=[jax.ShapeDtypeStruct(weight.shape, weight.dtype)] * 3,
-        grid=(planes, steps),
+        grid=(rows // block,),
         in_specs=[state] * 3 + grad_specs,
         out_specs=[state] * 3,
+        compiler_params=pltpu.CompilerParams(vmem_limit_bytes=VMEM_BYTES),
         cost_estimate=pl.CostEstimate(flops=20 * weight.size, bytes_accessed=28 * weight.size, transcendentals=0),
         name="adam_rows",
     )(weight, first, second, *grads)
+
+
+def adam_mixer_kernel(*refs):
+    entries, exits, grads, outs = refs[:3], refs[3:6], refs[6:8], refs[8:]
+    planes, _, columns = entries[0].shape
+    for plane in range(planes + 1):
+        grad = grads[plane // 2][:, plane % 2 * columns : (plane % 2 + 1) * columns]
+        state = [ref[plane] for ref in entries] if plane < planes else [ref[...] for ref in exits]
+        results = adam_update(*state, grad, RATE_WIDE, WEIGHT_DECAY)
+        for place, result in enumerate(results):
+            if plane < planes:
+                outs[place][plane] = result
+            else:
+                outs[3 + place][...] = result
+
+
+def adam_mixer(entries, exits, grad, last):
+    rows, planes, columns = entries[0].shape
+    block = max(rows // 4, 8)
+    entry_spec = pl.BlockSpec((planes, block, columns), lambda step: (0, step, 0))
+    exit_spec = pl.BlockSpec((block, columns), lambda step: (step, 0))
+    grad_spec = pl.BlockSpec((block, 2 * columns), lambda step: (step, 0))
+    size = entries[0].size + exits[0].size
+    results = pl.pallas_call(
+        adam_mixer_kernel,
+        out_shape=[jax.ShapeDtypeStruct((planes, rows, columns), jnp.float32)] * 3
+        + [jax.ShapeDtypeStruct((rows, columns), jnp.float32)] * 3,
+        grid=(rows // block,),
+        in_specs=[entry_spec] * 3 + [exit_spec] * 3 + [grad_spec] * 2,
+        out_specs=[entry_spec] * 3 + [exit_spec] * 3,
+        compiler_params=pltpu.CompilerParams(vmem_limit_bytes=VMEM_BYTES),
+        cost_estimate=pl.CostEstimate(flops=20 * size, bytes_accessed=28 * size, transcendentals=0),
+        name="adam_mixer",
+    )(*[array.transpose(1, 0, 2) for array in entries], *exits, grad, last)
+    return [result.transpose(1, 0, 2) for result in results[:3]] + list(results[3:])
 
 
 def adam_pairs_kernel(lanes, *refs):
@@ -1499,16 +1612,6 @@
     return [
         result.reshape(rows, deep, 2, LANES).transpose(0, 2, 1, 3).reshape(rows, 2, columns) for result in results
     ]
-
-
-def adam_planes(weight, first, second, grad):
-    rows, planes, columns = weight.shape
-
-    def seen(array):
-        return array.transpose(1, 0, 2).reshape(planes * rows, columns)
-
-    results = adam_rows(seen(weight), seen(first), seen(second), [grad], planes)
-    return [result.reshape(planes, rows, columns).transpose(1, 0, 2) for result in results]
 
 
 def shards(
@@ -1535,7 +1638,6 @@
     gain_second,
 ):
     channels = tokens.shape[1]
-    idle = NoJob()
     seen = conv_kernel.shape[1]
     small = jnp.concatenate([conv_kernel, norm_gains], axis=0)
     small = jnp.pad(small, ((0, 16 - small.shape[0]), (0, LANES - seen))).astype(LOW)
@@ -1554,72 +1656,34 @@
         },
         seen,
     )
-    entry_full, exit_full, wide = made["entry_full"], made["exit_full"], made["wide"]
-    gate_full, up_full, shrink_full, activation, gate_rows, up_rows = (
-        [made[name + half] for half in "01"]
-        for name in ("gate_full", "up_full", "shrink_full", "activation", "gate_rows", "up_rows")
-    )
-    cot_blocks, cot_full, normed_one, normed_two = (
-        made[name] for name in ("cot_blocks", "cot_full", "normed_one", "normed_two")
-    )
-    residual, scale_one, scale_two = made["residual"], made["scale_one"], made["scale_two"]
-    gate_grad_one, up_grad_one = made["gate_grad0"], made["up_grad0"]
-    shrink_part, gate_part, up_part = [None] * 2, [None] * 2, [None] * 2
-    hidden = HiddenGradJob(cot_blocks, shrink_full[1], gate_rows[1], up_rows[1])
-    width = WidthJob([gate_grad_one, up_grad_one], [gate_full[0], up_full[0], gate_full[1], up_full[1]], hidden)
-    shrink_part[0], gate_grad_two, up_grad_two, two_term = run_ring(
-        ScatterRing([(cot_full, activation[0])]), Jobs(hidden, width), 7
-    )
-    gate_grad, up_grad = [gate_grad_one, gate_grad_two], [up_grad_one, up_grad_two]
-    shrink_part[1], mixed_term = run_ring(
-        ScatterRing([(cot_full, activation[1])]), WidthJob(activation, shrink_full), 8
-    )
-    grad_normed_two, shrink_part[1], mixed_term = tie(reduce_branch(two_term), shrink_part[1], mixed_term)
-    gate_part[0], residual_grad, gain_two_grad, branch_own = run_ring(
-        ScatterRing([(normed_two, gate_grad[0])]),
-        NormBackJob(grad_normed_two, residual, scale_two, wide, 4, cotangent, True),
-        9,
-    )
-    mixed_branch, branch_own, up_grad[0] = tie(reduce_branch(mixed_term), branch_own, up_grad[0])
-    (up_part[0],) = run_ring(ScatterRing([(normed_two, up_grad[0])]), idle, 10)
-    branch_blocks, up_part[0] = tie(gather_blocks(branch_own), up_part[0])
-    gate_part[1], projected_grad, one_term, taps_grad = run_ring(
-        ScatterRing([(normed_two, gate_grad[1])]),
-        MixerGradJob(
-            branch_blocks,
-            exit_full,
-            entry_full,
-            made["projected"],
-            made["conv_out"],
-            made["gated"],
-            made["halo"],
-            wide,
-            bound,
-        ),
-        11,
-    )
-    one_term, up_grad[1], gate_part[1] = tie(one_term, up_grad[1], gate_part[1])
-    up_part[1], branch_full = run_ring(ScatterRing([(normed_two, up_grad[1])]), TurnJob(branch_blocks), 12)
-    grad_normed_one, up_part[1] = tie(reduce_branch(one_term), up_part[1])
-    back = NormBackJob(grad_normed_one, tokens, scale_one, wide, 3, residual_grad, False)
-    entry_part, exit_part, tokens_grad, _, small_part = run_ring(
-        ScatterRing([(normed_one, projected_grad), (branch_full, made["mixer"])]),
-        Jobs(back, SmallSumJob(taps_grad, gain_two_grad, back)),
-        13,
-    )
-    mixed = (residual + mixed_branch.astype(jnp.float32)).astype(LOW)
-    small_part = lax.dynamic_slice_in_dim(small_part, lax.axis_index("seq") * seen, seen, axis=1)
+    names = ["wide", "exit_full", "entry_full", "projected", "conv_out", "gated", "halo", "mixer", "residual"]
+    names += ["scale_one", "scale_two", "cot_blocks", "cot_full", "normed_one", "normed_two", "gate_grad0", "up_grad0"]
+    names += ["gate_rows1", "up_rows1", "activation0", "activation1"]
+    names += [name + half for name in ("gate_full", "up_full", "shrink_full") for half in "01"]
+    given = {"tokens": tokens, "cotangent": cotangent, "bound": bound}
+    grads = run_backward(given | {name: made[name] for name in names})
+    mixed, tokens_grad = grads["mixed"], grads["tokens_grad"]
+    small_part = lax.dynamic_slice_in_dim(grads["small_part"], lax.axis_index("seq") * seen, seen, axis=1)
     kernel_part = small_part[:3]
     gains_part = small_part[3:5]
-    entry_next, entry_first_next, entry_second_next = adam_planes(
-        entry_weight, entry_first, entry_second, entry_part
+    (
+        entry_next,
+        entry_first_next,
+        entry_second_next,
+        exit_next,
+        exit_first_next,
+        exit_second_next,
+    ) = adam_mixer(
+        (entry_weight, entry_first, entry_second),
+        (exit_weight, exit_first, exit_second),
+        grads["entry"],
+        grads["entry_exit"],
     )
-    exit_next, exit_first_next, exit_second_next = adam_rows(exit_weight, exit_first, exit_second, [exit_part])
     expand_next, expand_first_next, expand_second_next = adam_pairs(
-        expand_weight, expand_first, expand_second, [gate_part[0], up_part[0], gate_part[1], up_part[1]]
+        expand_weight, expand_first, expand_second, [grads[name] for name in ("gate0", "up0", "gate1", "up1")]
     )
     shrink_next, shrink_first_next, shrink_second_next = adam_rows(
-        shrink_weight, shrink_first, shrink_second, shrink_part
+        shrink_weight, shrink_first, shrink_second, [grads["shrink0"], grads["shrink1"]]
     )
     conv_next, conv_first_next, conv_second_next = adam_update(
         conv_kernel, conv_first, conv_second, kernel_part, RATE_CONV, 0.0

time: 790 us -> 769 us (0.973)
  between operations: 15.1 us -> 1.91 us
    pallas_call x3 -> x1, Pallas kernels: 18.4 us -> 6.86 us  [adam_rows(): pl.pallas_call(functools.partial(adam_kernel, len(grads)), out_shape=[jax...]
    pallas_call x8 -> x3, Pallas kernels: 721 us -> 727 us  [the longest x2 720 us: run(): pl.pallas_call(kernel, out_shape=[self.shapes[made] for made in outputs],...]
  transfers between devices with their start and end apart: 4 -> 0, of which waited for: 1 -> 0; matrix products, arithmetic and copies ran while one was open for 0% -> 0% of each run, Pallas kernels for 24% -> 0%
where the time goes in v6:
time: 769 us; the launch traced here: 760 us
  Pallas kernels  749 us (97%)
    pallas_call x2, Pallas kernels, run(): pl.pallas_call(kernel, out_shape=[self.shapes[made] for made in outputs],...  720 us

profile of v6, /device:TPU:0, one launch (start us, length us, event | category | flops | bytes accessed | tf_op | source)
XLA Modules:
  0.0 759.8 jit_solution(6979609338838035725)
XLA Ops:
  0.7 0.0 copy-start
  0.7 0.0 copy-start.3
  0.7 0.0 copy-start.6
  1.4 0.6 broadcast_in_dim.3.all_refs_5_.all_refs_2_
  2.0 1.7 copy.48
  3.7 1.2 copy.50.all_refs_0_
  4.8 0.0 copy-done
  4.8 0.7 convert_element_type.13.all_refs_1_
  5.6 0.0 copy-done.3
  5.6 0.0 copy-done.6
  5.6 0.6 fusion.5.all_refs_2_
  6.2 358.4 %forward.1 = (bf16[4,1024,512]{2,1,0:T(8,128)(2,1)}, bf16[4,1024,512]{2,1,0:T(8,128)(2,1)}, bf16[4,1024,512]{2,1,0:T(8,128)(2,1)}, bf16[4,1024,512]{2,1,0:T(8,12...) custom-call(bf16[256,1536]{1,0:T(8,128)(2,1)} %copy.50.all_refs_0_, ...), custom_call_target="tpu_custom_call" | custom-call | flops 30064771072 | bytes 1000000000 | tf_op jit(solution)/shard_map/forward/pallas_call | solution.py:1339
  364.6 361.5 %backward.1 = (bf16[4,1024,512]{2,1,0:T(8,128)(2,1)}, bf16[4,1024,512]{2,1,0:T(8,128)(2,1)}, bf16[4,1024,512]{2,1,0:T(8,128)(2,1)}, bf16[4,1024,512]{2,1,0:T(8,1...) custom-call(bf16[1024,512]{1,0:T(8,128)(2,1)} %all_refs_0_.1, ...), custom_call_target="tpu_custom_call" | custom-call | flops 73014444032 | bytes 1000000000 | tf_op jit(solution)/shard_map/backward/pallas_call | solution.py:1339
  726.1 6.9 adam_rows.1
  733.0 15.0 %adam_pairs.1 = (f32[8192,128]{1,0:T(8,128)}, f32[8192,128]{1,0:T(8,128)}, f32[8192,128]{1,0:T(8,128)}) custom-call(f32[8192,128]{1,0:T(8,128)} %bitcast.49, f32[8192,128]{1,0:T(8,128)} %bitcast.50, f32[8192,128]{1,0:T(8,128)} %bitcast.51, f32[256,1024]{1,0:T(8,128)} %get-tuple-element.107.refs_3_, f32[256,1024]{1,0:T(8,128)} %get-tuple-element.108.refs_4_, ...), custom_call_target="tpu_custom_call" | custom-call | flops 20971520 | bytes 29360128 | tf_op jit(solution)/shard_map/adam_pairs/pallas_call | solution.py:1602
  748.0 0.0 copy-start.5
  748.0 0.0 copy-start.7
  748.0 0.0 copy-start.8
  748.1 0.0 copy-start.2
  748.1 0.0 copy-start.1
  748.1 7.0 adam_mixer.1
  755.1 0.8 constant_dynamic-slice_fusion
  755.9 0.0 copy-done.4
  755.9 0.0 copy-done.5
  755.9 0.6 multiply_subtract_fusion
  756.5 0.0 copy-done.7
  756.5 0.0 copy-done.8
  756.5 0.6 multiply_subtract_fusion.1
  757.1 0.0 copy-done.2
  757.1 1.0 copy.59
  758.1 0.0 copy-done.1
  758.1 1.3 copy.60
  (3 shorter events, 0.0 us)
Async XLA Ops:
  0.7 4.2 copy-start
  0.7 4.9 copy-start.3
  0.7 4.9 copy-start.6
  748.0 7.9 %copy-start.4 = (f32[3,64]{1,0:T(4,128)S(1)}, f32[3,64]{1,0:T(4,128)}, u32[]{:S(2)}) copy-start(f32[3,64]{1,0:T(4,128)} %param.37) | copy-start | bytes 2308
  748.0 7.9 %copy-start.5 = (f32[3,64]{1,0:T(4,128)S(1)}, f32[3,64]{1,0:T(4,128)}, u32[]{:S(2)}) copy-start(f32[3,64]{1,0:T(4,128)} %param.38) | copy-start | bytes 2308
  748.0 8.5 %copy-start.7 = (f32[2,64]{1,0:T(2,128)S(1)}, f32[2,64]{1,0:T(2,128)}, u32[]{:S(2)}) copy-start(f32[2,64]{1,0:T(2,128)} %param.40) | copy-start | bytes 1540
  748.0 8.4 %copy-start.8 = (f32[2,64]{1,0:T(2,128)S(1)}, f32[2,64]{1,0:T(2,128)}, u32[]{:S(2)}) copy-start(f32[2,64]{1,0:T(2,128)} %param.41) | copy-start | bytes 1540
  748.1 9.0 %copy-start.2 = (bf16[1024,512]{1,0:T(8,128)(2,1)S(1)}, bf16[1024,512]{1,0:T(8,128)(2,1)}, u32[]{:S(2)}) copy-start(bf16[1024,512]{1,0:T(8,128)(2,1)} %get-tuple-element.146) | copy-start | bytes 3145732
  748.1 10.0 %copy-start.1 = (f32[1024,512]{1,0:T(8,128)S(1)}, f32[1024,512]{1,0:T(8,128)}, u32[]{:S(2)}) copy-start(f32[1024,512]{1,0:T(8,128)} %get-tuple-element.147) | copy-start | bytes 6291460

commit v7 on v6

--- a/solution.py
+++ b/solution.py
@@ -305,8 +305,8 @@
 
     def settle(self, group):
         last = self.count - 1
-        if group >= 2:
-            self.store(group - 2).wait()
+        if group >= 1:
+            self.store(group - 1).wait()
         for part in range(self.parts):
             for way in range(2):
                 mine = self.term(group, way, part, last)
@@ -327,13 +327,13 @@
         lax.fori_loop(0, last, sent, 0)
 
     def finish(self):
-        for group in range(max(len(self.groups) - 2, 0), len(self.groups)):
-            self.store(group).wait()
+        self.store(len(self.groups) - 1).wait()
 
 
 class Job:
     wide = 256
     kept = []
+    late = ()
 
     def hold(self, refs):
         pass
@@ -385,16 +385,18 @@
             self.outs_v[which].at[window], self.out_refs[which].at[window], self.out_sem.at[which, index]
         )
 
-    def start(self):
+    def start(self, late):
         for which in range(len(self.whole)):
-            self.whole_load(which).start()
+            if late == (which in self.late):
+                self.whole_load(which).start()
 
         def begin(index, carry):
             for which in range(len(self.tiled)):
                 self.tiled_load(which, index).start()
             return carry
 
-        lax.fori_loop(0, self.tiles, begin, 0)
+        if not late:
+            lax.fori_loop(0, self.tiles, begin, 0)
 
     def tile(self, index):
         @pl.when(index == 0)
@@ -428,6 +430,9 @@
 
 
 class ExpandJob(Job):
+
+    late = (0,)
+
     def __init__(self, normed, gate_full, up_full):
         rows, width = normed.shape[1], gate_full.shape[1]
         outs = [((rows, width), jnp.float32), ((rows, width), jnp.float32), ((rows, width), LOW)]
@@ -486,6 +491,7 @@
 
 class MixerJob:
     kept = []
+    late = ()
 
     def hold(self, refs):
         self.kept_refs = refs
@@ -537,9 +543,10 @@
             device_id_type=MESH,
         )
 
-    def start(self):
+    def start(self, late):
         for which in range(len(self.inputs)):
-            self.load(which).start()
+            if late == (which in self.late):
+                self.load(which).start()
 
     def tile(self, index):
         begin = 0
@@ -580,6 +587,7 @@
 
 class EntryJob(MixerJob):
     then = None
+    late = (0,)
 
     def __init__(self, tokens, wide, entry_full, exit_full, bound):
         parts, rows, own = tokens.shape
@@ -683,6 +691,7 @@
 
 class MixerGradJob(MixerJob):
     then = None
+    late = (0,)
 
     def __init__(self, branch, exit_full, entry_full, projected, conv, gated, halo, wide, bound):
         parts, rows, own = branch.shape
@@ -811,9 +820,9 @@
     def peers(self):
         return [peer for job in self.jobs for peer in job.peers()]
 
-    def start(self):
+    def start(self, late):
         for job in self.jobs:
-            job.start()
+            job.start(late)
 
     def tile(self, index):
         begin = 0
@@ -832,6 +841,8 @@
 
 
 class TurnJob(MixerJob):
+    late = (0,)
+
     def __init__(self, blocks):
         parts, rows, own = blocks.shape
         super().__init__([blocks], [((parts * own, rows), blocks.dtype)], [], [rows // 128], 0)
@@ -943,7 +954,9 @@
             device_id_type=MESH,
         )
 
-    def start(self):
+    def start(self, late):
+        if late:
+            return
         load = pltpu.make_async_copy(self.source, self.whole.at[self.seq, self.column], self.local_sem.at[0])
         load.start()
         load.wait()
@@ -1042,6 +1055,7 @@
 
 class NormJob(RowSumJob):
     then = None
+    late = (1,)
 
     def __init__(self, rows_in, terms, wide):
         rows, own = rows_in.shape
@@ -1074,6 +1088,7 @@
 
 class NormBackJob(RowSumJob):
     then = None
+    late = (0,)
 
     def __init__(self, terms, kept, scales, wide, row, base, rounded):
         _, rows, own = terms.shape
@@ -1123,6 +1138,8 @@
 
 
 class SumJob(MixerJob):
+    late = (1,)
+
     def __init__(self, base, terms):
         rows, own = base.shape
         super().__init__([base, terms], [((rows, own), LOW)], [], [rows // 128], 0)
@@ -1186,7 +1203,9 @@
             for which in range(2)
         ]
 
-    def start(self):
+    def start(self, late):
+        if late:
+            return
         for load in self.loads():
             load.start()
 
@@ -1240,12 +1259,13 @@
         def ready():
             for exchange in self.waits:
                 exchange.wait()
-            job.start()
+            job.start(True)
 
         def body(*scratch):
             job.bind(ins, outs, list(scratch))
+            job.start(False)
             if not self.waits:
-                job.start()
+                job.start(True)
             done = 0
             for place, (group, low, high) in enumerate(ranges):
                 if low == 0 and group > 0 and place > 0:
@@ -1305,7 +1325,7 @@
         shape = self.shapes[full].shape
         return jax.ShapeDtypeStruct((shape[0] * shape[1], shape[2]), LOW)
 
-    def run(self, ring, sections, exchanges, peers, start, name, collective):
+    def run(self, ring, sections, exchanges, peers, name, collective):
         inputs = self.inputs
         outputs = [made for made in self.shapes if made not in inputs]
         kept = [item for section in sections for item in section.job.kept]
@@ -1325,8 +1345,6 @@
             greet(peers())
             ring.begin(0)
             ring.settled(-1)
-            for exchange in start:
-                exchange.start()
             for section in sections:
                 ins = [rows_of(refs[made], made in self.weights) for _, names, _ in section.jobs for made in names]
                 outs = [refs[made] for _, _, names in section.jobs for made in names]
@@ -1403,7 +1421,7 @@
     hidden = add(hidden_job, ["cot_blocks", "shrink_full0", "gate_rows0", "up_rows0"], ["gate_grad0", "up_grad0"])
     turn_normed = add(TurnJob(shapes["normed_blocks"]), ["normed_blocks"], ["normed_two"])
     sections = [
-        Section([(0, 0, 12)], [small, cast], early=False),
+        Section([(0, 0, 12)], [small, cast], calls=[tokens_sent], early=False),
         Section([(1, 0, 12)], [entry], [tokens_sent], calls=[cot_sent]),
         Section([(2, 0, 12)], [turn_cot], [cot_sent], rest=3),
         Section([(3, 0, 12)], [norm], [branch_sent], rest=4),
@@ -1412,7 +1430,7 @@
         Section([(6, 0, 12)], [hidden, turn_normed]),
     ]
     exchanges = [tokens_sent, cot_sent, branch_sent, normed_sent]
-    return plan.run(ring, sections, exchanges, row_and_column_peers, [tokens_sent], "forward", 0)
+    return plan.run(ring, sections, exchanges, row_and_column_peers, "forward", 0)
 
 
 def run_backward(arrays):
@@ -1472,17 +1490,17 @@
     ring.outs = sums
     sections = [
         Section([(0, 0, 5)], [hidden]),
-        Section([(0, 5, 12), (1, 0, 4)], [two]),
+        Section([(0, 5, 12), (1, 0, 4)], [two], rest=2),
         Section([(1, 4, 12), (2, 0, 5)], [mixed]),
-        Section([(2, 5, 12)], [norm_two], [two_sent]),
+        Section([(2, 5, 12)], [norm_two], [two_sent], rest=3),
         Section([(3, 0, 12)]),
-        Section([(4, 0, 12)], [mixer], [branch_sent], rest=2),
+        Section([(4, 0, 12)], [mixer], [branch_sent], rest=3),
         Section([(5, 0, 12)], [turn], calls=[mixed_sent]),
         Section([(6, 0, 12)], [norm_one, small], [one_sent], rest=3),
         Section([(7, 0, 12)], [total], [mixed_sent]),
     ]
     exchanges = [two_sent, mixed_sent, branch_sent, one_sent]
-    return plan.run(ring, sections, exchanges, row_and_column_peers, [], "backward", 1)
+    return plan.run(ring, sections, exchanges, row_and_column_peers, "backward", 1)
 
 
 def rows_of(ref, gathered):

time: 769 us -> 742 us (0.965)
  Pallas kernels: 749 us -> 722 us
    pallas_call x2, Pallas kernels: 720 us -> 693 us  [run(): pl.pallas_call(kernel, out_shape=[self.shapes[made] for made in outputs],...]
where the time goes in v7:
time: 742 us; the launch traced here: 733 us
  Pallas kernels  722 us (97%)
    pallas_call x2, Pallas kernels, run(): pl.pallas_call(kernel, out_shape=[self.shapes[made] for made in outputs],...  693 us
    pallas_call x1, Pallas kernels, adam_pairs(): pl.pallas_call(functools.partial(adam_pairs_kernel, LANES), out_shape=[ja...  15 us

profile of v7, /device:TPU:0, one launch (start us, length us, event | category | flops | bytes accessed | tf_op | source)
XLA Modules:
  0.0 732.7 jit_solution(17549731550478104227)
XLA Ops:
  0.7 0.0 copy-start
  0.7 0.0 copy-start.3
  0.7 0.0 copy-start.6
  1.4 0.6 broadcast_in_dim.3.all_refs_5_.all_refs_2_
  2.0 1.7 copy.48
  3.7 1.2 copy.50.all_refs_0_
  4.8 0.0 copy-done
  4.8 0.7 convert_element_type.13.all_refs_1_
  5.6 0.0 copy-done.3
  5.6 0.0 copy-done.6
  5.6 0.6 fusion.5.all_refs_2_
  6.2 335.0 %forward.1 = (bf16[4,1024,512]{2,1,0:T(8,128)(2,1)}, bf16[4,1024,512]{2,1,0:T(8,128)(2,1)}, bf16[4,1024,512]{2,1,0:T(8,128)(2,1)}, bf16[4,1024,512]{2,1,0:T(8,12...) custom-call(bf16[256,1536]{1,0:T(8,128)(2,1)} %copy.50.all_refs_0_, ...), custom_call_target="tpu_custom_call" | custom-call | flops 30064771072 | bytes 1000000000 | tf_op jit(solution)/shard_map/forward/pallas_call | solution.py:1357
  341.2 357.9 %backward.1 = (bf16[4,1024,512]{2,1,0:T(8,128)(2,1)}, bf16[4,1024,512]{2,1,0:T(8,128)(2,1)}, bf16[4,1024,512]{2,1,0:T(8,128)(2,1)}, bf16[4,1024,512]{2,1,0:T(8,1...) custom-call(bf16[1024,512]{1,0:T(8,128)(2,1)} %all_refs_0_.1, ...), custom_call_target="tpu_custom_call" | custom-call | flops 73014444032 | bytes 1000000000 | tf_op jit(solution)/shard_map/backward/pallas_call | solution.py:1357
  699.0 6.9 adam_rows.1
  705.9 15.0 %adam_pairs.1 = (f32[8192,128]{1,0:T(8,128)}, f32[8192,128]{1,0:T(8,128)}, f32[8192,128]{1,0:T(8,128)}) custom-call(f32[8192,128]{1,0:T(8,128)} %bitcast.49, f32[8192,128]{1,0:T(8,128)} %bitcast.50, f32[8192,128]{1,0:T(8,128)} %bitcast.51, f32[256,1024]{1,0:T(8,128)} %get-tuple-element.107.refs_3_, f32[256,1024]{1,0:T(8,128)} %get-tuple-element.108.refs_4_, ...), custom_call_target="tpu_custom_call" | custom-call | flops 20971520 | bytes 29360128 | tf_op jit(solution)/shard_map/adam_pairs/pallas_call | solution.py:1620
  720.9 0.0 copy-start.5
  720.9 0.0 copy-start.7
  720.9 0.0 copy-start.8
  721.0 0.0 copy-start.2
  721.0 0.0 copy-start.1
  721.0 7.0 adam_mixer.1
  728.0 0.8 constant_dynamic-slice_fusion
  728.8 0.0 copy-done.4
  728.8 0.0 copy-done.5
  728.8 0.6 multiply_subtract_fusion
  729.4 0.0 copy-done.7
  729.4 0.0 copy-done.8
  729.4 0.6 multiply_subtract_fusion.1
  730.0 0.0 copy-done.2
  730.0 1.0 copy.59
  731.0 0.0 copy-done.1
  731.0 1.3 copy.60
  (3 shorter events, 0.0 us)
Async XLA Ops:
  0.7 4.2 copy-start
  0.7 4.9 copy-start.3
  0.7 4.9 copy-start.6
  720.9 7.9 %copy-start.4 = (f32[3,64]{1,0:T(4,128)S(1)}, f32[3,64]{1,0:T(4,128)}, u32[]{:S(2)}) copy-start(f32[3,64]{1,0:T(4,128)} %param.37) | copy-start | bytes 2308
  720.9 7.9 %copy-start.5 = (f32[3,64]{1,0:T(4,128)S(1)}, f32[3,64]{1,0:T(4,128)}, u32[]{:S(2)}) copy-start(f32[3,64]{1,0:T(4,128)} %param.38) | copy-start | bytes 2308
  720.9 8.5 %copy-start.7 = (f32[2,64]{1,0:T(2,128)S(1)}, f32[2,64]{1,0:T(2,128)}, u32[]{:S(2)}) copy-start(f32[2,64]{1,0:T(2,128)} %param.40) | copy-start | bytes 1540
  720.9 8.4 %copy-start.8 = (f32[2,64]{1,0:T(2,128)S(1)}, f32[2,64]{1,0:T(2,128)}, u32[]{:S(2)}) copy-start(f32[2,64]{1,0:T(2,128)} %param.41) | copy-start | bytes 1540
  721.0 9.0 %copy-start.2 = (bf16[1024,512]{1,0:T(8,128)(2,1)S(1)}, bf16[1024,512]{1,0:T(8,128)(2,1)}, u32[]{:S(2)}) copy-start(bf16[1024,512]{1,0:T(8,128)(2,1)} %get-tuple-element.146) | copy-start | bytes 3145732
  721.0 10.0 %copy-start.1 = (f32[1024,512]{1,0:T(8,128)S(1)}, f32[1024,512]{1,0:T(8,128)}, u32[]{:S(2)}) copy-start(f32[1024,512]{1,0:T(8,128)} %get-tuple-element.147) | copy-start | bytes 6291460

commit v8 on v7

--- a/solution.py
+++ b/solution.py
@@ -1244,8 +1244,9 @@
 
 
 class Section:
-    def __init__(self, ranges, jobs=(), waits=(), rest=1, calls=(), early=True):
+    def __init__(self, ranges, jobs=(), waits=(), rest=1, calls=(), early=True, then=()):
         self.ranges, self.jobs, self.waits, self.rest, self.calls, self.early = ranges, jobs, waits, rest, calls, early
+        self.then = then
         self.job = Jobs(*[job for job, _, _ in jobs])
 
     def run(self, ring, ins, outs):
@@ -1259,6 +1260,8 @@
         def ready():
             for exchange in self.waits:
                 exchange.wait()
+            for exchange in self.then:
+                exchange.start()
             job.start(True)
 
         def body(*scratch):
@@ -1494,9 +1497,9 @@
         Section([(1, 4, 12), (2, 0, 5)], [mixed]),
         Section([(2, 5, 12)], [norm_two], [two_sent], rest=3),
         Section([(3, 0, 12)]),
-        Section([(4, 0, 12)], [mixer], [branch_sent], rest=3),
-        Section([(5, 0, 12)], [turn], calls=[mixed_sent]),
-        Section([(6, 0, 12)], [norm_one, small], [one_sent], rest=3),
+        Section([(4, 0, 12)], [mixer], [branch_sent], rest=3, then=[mixed_sent]),
+        Section([(5, 0, 12)], [turn]),
+        Section([(6, 0, 12)], [norm_one, small], [one_sent], rest=5),
         Section([(7, 0, 12)], [total], [mixed_sent]),
     ]
     exchanges = [two_sent, mixed_sent, branch_sent, one_sent]

time: 742 us -> 719 us (0.969)
  Pallas kernels: 722 us -> 699 us
    pallas_call x2, Pallas kernels: 693 us -> 670 us  [run(): pl.pallas_call(kernel, out_shape=[self.shapes[made] for made in outputs],...]
where the time goes in v8:
time: 719 us; the launch traced here: 710 us
  Pallas kernels  699 us (97%)
    pallas_call x2, Pallas kernels, run(): pl.pallas_call(kernel, out_shape=[self.shapes[made] for made in outputs],...  670 us
    pallas_call x1, Pallas kernels, adam_pairs(): pl.pallas_call(functools.partial(adam_pairs_kernel, LANES), out_shape=[ja...  15 us

profile of v8, /device:TPU:0, one launch (start us, length us, event | category | flops | bytes accessed | tf_op | source)
XLA Modules:
  0.0 710.0 jit_solution(13809823364602769140)
XLA Ops:
  0.7 0.0 copy-start
  0.7 0.0 copy-start.3
  0.7 0.0 copy-start.6
  1.4 0.6 broadcast_in_dim.3.all_refs_5_.all_refs_2_
  2.0 1.7 copy.48
  3.7 1.2 copy.50.all_refs_0_
  4.8 0.0 copy-done
  4.8 0.7 convert_element_type.13.all_refs_1_
  5.6 0.0 copy-done.3
  5.6 0.0 copy-done.6
  5.6 0.6 fusion.5.all_refs_2_
  6.2 335.0 %forward.1 = (bf16[4,1024,512]{2,1,0:T(8,128)(2,1)}, bf16[4,1024,512]{2,1,0:T(8,128)(2,1)}, bf16[4,1024,512]{2,1,0:T(8,128)(2,1)}, bf16[4,1024,512]{2,1,0:T(8,12...) custom-call(bf16[256,1536]{1,0:T(8,128)(2,1)} %copy.50.all_refs_0_, ...), custom_call_target="tpu_custom_call" | custom-call | flops 30064771072 | bytes 1000000000 | tf_op jit(solution)/shard_map/forward/pallas_call | solution.py:1360
  341.2 335.1 %backward.1 = (bf16[4,1024,512]{2,1,0:T(8,128)(2,1)}, bf16[4,1024,512]{2,1,0:T(8,128)(2,1)}, bf16[4,1024,512]{2,1,0:T(8,128)(2,1)}, bf16[4,1024,512]{2,1,0:T(8,1...) custom-call(bf16[1024,512]{1,0:T(8,128)(2,1)} %all_refs_0_.1, ...), custom_call_target="tpu_custom_call" | custom-call | flops 73014444032 | bytes 1000000000 | tf_op jit(solution)/shard_map/backward/pallas_call | solution.py:1360
  676.3 6.9 adam_rows.1
  683.1 15.0 %adam_pairs.1 = (f32[8192,128]{1,0:T(8,128)}, f32[8192,128]{1,0:T(8,128)}, f32[8192,128]{1,0:T(8,128)}) custom-call(f32[8192,128]{1,0:T(8,128)} %bitcast.49, f32[8192,128]{1,0:T(8,128)} %bitcast.50, f32[8192,128]{1,0:T(8,128)} %bitcast.51, f32[256,1024]{1,0:T(8,128)} %get-tuple-element.107.refs_3_, f32[256,1024]{1,0:T(8,128)} %get-tuple-element.108.refs_4_, ...), custom_call_target="tpu_custom_call" | custom-call | flops 20971520 | bytes 29360128 | tf_op jit(solution)/shard_map/adam_pairs/pallas_call | solution.py:1623
  698.2 0.0 copy-start.5
  698.2 0.0 copy-start.7
  698.2 0.0 copy-start.8
  698.2 0.0 copy-start.2
  698.2 0.0 copy-start.1
  698.2 7.0 adam_mixer.1
  705.3 0.8 constant_dynamic-slice_fusion
  706.0 0.0 copy-done.4
  706.0 0.0 copy-done.5
  706.0 0.6 multiply_subtract_fusion
  706.6 0.0 copy-done.7
  706.6 0.0 copy-done.8
  706.6 0.6 multiply_subtract_fusion.1
  707.2 0.0 copy-done.2
  707.2 1.0 copy.59
  708.2 0.0 copy-done.1
  708.2 1.3 copy.60
  (3 shorter events, 0.0 us)
Async XLA Ops:
  0.7 4.2 copy-start
  0.7 4.9 copy-start.3
  0.7 4.9 copy-start.6
  698.1 7.9 %copy-start.4 = (f32[3,64]{1,0:T(4,128)S(1)}, f32[3,64]{1,0:T(4,128)}, u32[]{:S(2)}) copy-start(f32[3,64]{1,0:T(4,128)} %param.37) | copy-start | bytes 2308
  698.2 7.9 %copy-start.5 = (f32[3,64]{1,0:T(4,128)S(1)}, f32[3,64]{1,0:T(4,128)}, u32[]{:S(2)}) copy-start(f32[3,64]{1,0:T(4,128)} %param.38) | copy-start | bytes 2308
  698.2 8.5 %copy-start.7 = (f32[2,64]{1,0:T(2,128)S(1)}, f32[2,64]{1,0:T(2,128)}, u32[]{:S(2)}) copy-start(f32[2,64]{1,0:T(2,128)} %param.40) | copy-start | bytes 1540
  698.2 8.4 %copy-start.8 = (f32[2,64]{1,0:T(2,128)S(1)}, f32[2,64]{1,0:T(2,128)}, u32[]{:S(2)}) copy-start(f32[2,64]{1,0:T(2,128)} %param.41) | copy-start | bytes 1540
  698.2 9.0 %copy-start.2 = (bf16[1024,512]{1,0:T(8,128)(2,1)S(1)}, bf16[1024,512]{1,0:T(8,128)(2,1)}, u32[]{:S(2)}) copy-start(bf16[1024,512]{1,0:T(8,128)(2,1)} %get-tuple-element.146) | copy-start | bytes 3145732
  698.2 10.0 %copy-start.1 = (f32[1024,512]{1,0:T(8,128)S(1)}, f32[1024,512]{1,0:T(8,128)}, u32[]{:S(2)}) copy-start(f32[1024,512]{1,0:T(8,128)} %get-tuple-element.147) | copy-start | bytes 6291460

commit v9 on v8

--- a/solution.py
+++ b/solution.py
@@ -1158,6 +1158,81 @@
         self.outs_v[0][rows, :] = (base[rows, :] + total).astype(LOW)
 
 
+class AdamJob(MixerJob):
+    deep = 1
+
+    def __init__(self, weight, grads, extra=()):
+        rows = grads[0].shape[0]
+        self.block = max(rows // 8, 8)
+        tiles = rows // self.block
+        outs = [(weight.shape, jnp.float32)] * 3
+        super().__init__([weight] * 3 + list(grads), outs, list(extra), [tiles], 0)
+        self.scratch[-1] = pltpu.SemaphoreType.DMA((3, tiles))
+
+    def peers(self):
+        return []
+
+    def before(self, phase):
+        for which in range(len(self.inputs)):
+            self.load(which).wait()
+
+    def after(self, phase):
+        pass
+
+    def piece(self, which, index):
+        size = self.block * self.deep
+        rows = pl.ds(pl.multiple_of(index * size, 8), size)
+        return pltpu.make_async_copy(
+            self.outs_v[which].at[rows], self.out_refs[which].at[rows], self.out_sem.at[which, index]
+        )
+
+    def work(self, phase, index):
+        rows = pl.ds(pl.multiple_of(index * self.block, 8), self.block)
+        start = 0
+        for grad in self.ins_v[3:]:
+            span = slice(start, start + grad.shape[1])
+            start += grad.shape[1]
+            state = [ref[rows, span] for ref in self.ins_v[:3]]
+            for out, result in zip(self.outs_v, adam_update(*state, grad[rows, :], RATE_WIDE, WEIGHT_DECAY)):
+                out[rows, span] = result
+        for which in range(3):
+            self.piece(which, index).start()
+
+    def finish(self):
+        def end(index, carry):
+            for which in range(3):
+                self.piece(which, index).wait()
+            return carry
+
+        lax.fori_loop(0, self.tiles, end, 0)
+
+
+class AdamPairsJob(AdamJob):
+    def __init__(self, weight, grads):
+        rows = grads[0].shape[0]
+        self.deep = weight.shape[0] // rows
+        size = max(rows // 8, 8) * self.deep
+        super().__init__(weight, grads, [pltpu.VMEM((size, LANES), jnp.float32)])
+
+    def work(self, phase, index):
+        size = self.block * self.deep
+        rows = pl.ds(pl.multiple_of(index * self.block, 8), self.block)
+        seen = pl.ds(pl.multiple_of(index * size, 8), size)
+        mixed = self.extra_v[0]
+        for which, grad in enumerate(self.ins_v[3:]):
+            half, side = which // 2, which % 2
+            tiles = grad.shape[1] // LANES
+            for tile in range(tiles):
+                place = (half * tiles + tile) * 2 + side
+                picked = grad[rows, tile * LANES : (tile + 1) * LANES]
+                mixed[pl.ds(place, self.block, stride=self.deep), :] = picked
+        state = [ref[seen, :] for ref in self.ins_v[:3]]
+        for out, result in zip(self.outs_v, adam_update(*state, mixed[...], RATE_WIDE, WEIGHT_DECAY)):
+            out[seen, :] = result
+        for which in range(3):
+            self.piece(which, index).start()
+
+
 class SmallSumJob:
     tiles, flops = 1, 0
 
@@ -1491,16 +1566,22 @@
     for name, shape in zip(sums, ring.out_shapes):
         plan.shapes[name] = shape
     ring.outs = sums
+    names = [["shrink_weight", "shrink_first", "shrink_second"], ["shrink0", "shrink1"]]
+    shrink_job = AdamJob(shapes["shrink_weight"], [shapes[name] for name in names[1]])
+    adam_shrink = add(shrink_job, names[0] + names[1], ["shrink_next", "shrink_first_next", "shrink_second_next"])
+    names = [["expand_weight", "expand_first", "expand_second"], ["gate0", "up0", "gate1", "up1"]]
+    expand_job = AdamPairsJob(shapes["expand_weight"], [shapes[name] for name in names[1]])
+    adam_expand = add(expand_job, names[0] + names[1], ["expand_next", "expand_first_next", "expand_second_next"])
     sections = [
         Section([(0, 0, 5)], [hidden]),
         Section([(0, 5, 12), (1, 0, 4)], [two], rest=2),
         Section([(1, 4, 12), (2, 0, 5)], [mixed]),
         Section([(2, 5, 12)], [norm_two], [two_sent], rest=3),
-        Section([(3, 0, 12)]),
+        Section([(3, 0, 12)], [adam_shrink], rest=2),
         Section([(4, 0, 12)], [mixer], [branch_sent], rest=3, then=[mixed_sent]),
         Section([(5, 0, 12)], [turn]),
-        Section([(6, 0, 12)], [norm_one, small], [one_sent], rest=5),
-        Section([(7, 0, 12)], [total], [mixed_sent]),
+        Section([(6, 0, 12)], [norm_one, small, total], [one_sent, mixed_sent], rest=5),
+        Section([(7, 0, 12)], [adam_expand], rest=2),
     ]
     exchanges = [two_sent, mixed_sent, branch_sent, one_sent]
     return plan.run(ring, sections, exchanges, row_and_column_peers, "backward", 1)
@@ -1529,35 +1610,6 @@
     corrected = first_next / (1.0 - BETA_ONE**STEP)
     spread = jnp.sqrt(second_next / (1.0 - BETA_TWO**STEP)) + ADAM_EPSILON
     return (weight - rate * (corrected / spread + decay * weight), first_next, second_next)
-
-
-def adam_kernel(pieces, *refs):
-    weight, first, second = refs[:3]
-    grads, outs = refs[3 : 3 + pieces], refs[3 + pieces :]
-    start = 0
-    for grad in grads:
-        span = slice(start, start + grad.shape[1])
-        start += grad.shape[1]
-        results = adam_update(weight[:, span], first[:, span], second[:, span], grad[...], RATE_WIDE, WEIGHT_DECAY)
-        for out, result in zip(outs, results):
-            out[:, span] = result
-
-
-def adam_rows(weight, first, second, grads):
-    rows, columns = weight.shape
-    block = max(rows // 4, 8)
-    state = pl.BlockSpec((block, columns), lambda step: (step, 0))
-    grad_specs = [pl.BlockSpec((block, grad.shape[1]), lambda step: (step, 0)) for grad in grads]
-    return pl.pallas_call(
-        functools.partial(adam_kernel, len(grads)),
-        out_shape=[jax.ShapeDtypeStruct(weight.shape, weight.dtype)] * 3,
-        grid=(rows // block,),
-        in_specs=[state] * 3 + grad_specs,
-        out_specs=[state] * 3,
-        compiler_params=pltpu.CompilerParams(vmem_limit_bytes=VMEM_BYTES),
-        cost_estimate=pl.CostEstimate(flops=20 * weight.size, bytes_accessed=28 * weight.size, transcendentals=0),
-        name="adam_rows",
-    )(weight, first, second, *grads)
 
 
 def adam_mixer_kernel(*refs):
@@ -1595,44 +1647,14 @@
     return [result.transpose(1, 0, 2) for result in results[:3]] + list(results[3:])
 
 
-def adam_pairs_kernel(lanes, *refs):
-    weight, first, second = refs[:3]
-    grads, outs, mixed = refs[3:7], refs[7:10], refs[10]
-    rows = grads[0].shape[0]
-    tiles = grads[0].shape[1] // lanes
-    for which, grad in enumerate(grads):
-        half, side = which // 2, which % 2
-        for tile in range(tiles):
-            place = (half * tiles + tile) * 2 + side
-            mixed[pl.ds(place, rows, stride=4 * tiles), :] = grad[:, tile * lanes : (tile + 1) * lanes]
-    results = adam_update(weight[...], first[...], second[...], mixed[...], RATE_WIDE, WEIGHT_DECAY)
-    for out, result in zip(outs, results):
-        out[...] = result
-
-
 def paired(array):
     rows, _, columns = array.shape
     return array.reshape(rows, 2, columns // LANES, LANES).transpose(0, 2, 1, 3).reshape(-1, LANES)
 
 
-def adam_pairs(weight, first, second, grads):
-    rows, _, columns = weight.shape
-    deep = columns // LANES
-    block = max(rows // 8, 8)
-    state = pl.BlockSpec((block * deep * 2, LANES), lambda step: (step, 0))
-    results = pl.pallas_call(
-        functools.partial(adam_pairs_kernel, LANES),
-        out_shape=[jax.ShapeDtypeStruct((rows * deep * 2, LANES), weight.dtype)] * 3,
-        grid=(rows // block,),
-        in_specs=[state] * 3 + [pl.BlockSpec((block, columns // 2), lambda step: (step, 0))] * 4,
-        out_specs=[state] * 3,
-        scratch_shapes=[pltpu.VMEM((block * deep * 2, LANES), jnp.float32)],
-        cost_estimate=pl.CostEstimate(flops=20 * weight.size, bytes_accessed=28 * weight.size, transcendentals=0),
-        name="adam_pairs",
-    )(paired(weight), paired(first), paired(second), *grads)
-    return [
-        result.reshape(rows, deep, 2, LANES).transpose(0, 2, 1, 3).reshape(rows, 2, columns) for result in results
-    ]
+def unpaired(array, shape):
+    rows, _, columns = shape
+    return array.reshape(rows, columns // LANES, 2, LANES).transpose(0, 2, 1, 3).reshape(shape)
 
 
 def shards(
@@ -1682,6 +1704,9 @@
     names += ["gate_rows1", "up_rows1", "activation0", "activation1"]
     names += [name + half for name in ("gate_full", "up_full", "shrink_full") for half in "01"]
     given = {"tokens": tokens, "cotangent": cotangent, "bound": bound}
+    given |= {"shrink_weight": shrink_weight, "shrink_first": shrink_first, "shrink_second": shrink_second}
+    given["expand_weight"] = paired(expand_weight)
+    given["expand_first"], given["expand_second"] = paired(expand_first), paired(expand_second)
     grads = run_backward(given | {name: made[name] for name in names})
     mixed, tokens_grad = grads["mixed"], grads["tokens_grad"]
     small_part = lax.dynamic_slice_in_dim(grads["small_part"], lax.axis_index("seq") * seen, seen, axis=1)
@@ -1700,11 +1725,11 @@
         grads["entry"],
         grads["entry_exit"],
     )
-    expand_next, expand_first_next, expand_second_next = adam_pairs(
-        expand_weight, expand_first, expand_second, [grads[name] for name in ("gate0", "up0", "gate1", "up1")]
+    shrink_next, shrink_first_next, shrink_second_next = (
+        grads["shrink" + name] for name in ("_next", "_first_next", "_second_next")
     )
-    shrink_next, shrink_first_next, shrink_second_next = adam_rows(
-        shrink_weight, shrink_first, shrink_second, [grads["shrink0"], grads["shrink1"]]
+    expand_next, expand_first_next, expand_second_next = (
+        unpaired(grads["expand" + name], expand_weight.shape) for name in ("_next", "_first_next", "_second_next")
     )
     conv_next, conv_first_next, conv_second_next = adam_update(
         conv_kernel, conv_first, conv_second, kernel_part, RATE_CONV, 0.0

time: 719 us -> 713 us (level)
  Pallas kernels: 699 us -> 678 us
  local copies, waits for them, and re-layouts: 6.51 us -> 22.2 us
    pallas_call x2 -> x0, Pallas kernels: 21.9 us -> none  [the longest x1 15 us: adam_pairs(): pl.pallas_call(functools.partial(adam_pairs_kernel, LANES), out_shape=[ja...]
    unnamed x21 -> x39, local copies, waits for them, and re-layouts: 4.01 us -> 19.5 us
where the time goes in v9:
time: 713 us; the launch traced here: 704 us
  Pallas kernels  678 us (95%)
  local copies, waits for them, and re-layouts  22.2 us (3%)
    pallas_call x2, Pallas kernels, run(): pl.pallas_call(kernel, out_shape=[self.shapes[made] for made in outputs],...  671 us
    unnamed x39, local copies, waits for them, and re-layouts  19.5 us

profile of v9, /device:TPU:0, one launch (start us, length us, event | category | flops | bytes accessed | tf_op | source)
XLA Modules:
  0.0 704.3 jit_solution(12919366098356857992)
XLA Ops:
  0.7 0.0 copy-start.3
  1.4 0.6 broadcast_in_dim.3.all_refs_5_.all_refs_2_
  2.0 1.7 copy.51
  3.7 1.2 copy.52.all_refs_0_
  4.8 0.7 convert_element_type.13.all_refs_1_
  5.6 0.6 fusion.5.all_refs_2_
  6.2 335.0 %forward.1 = (bf16[4,1024,512]{2,1,0:T(8,128)(2,1)}, bf16[4,1024,512]{2,1,0:T(8,128)(2,1)}, bf16[4,1024,512]{2,1,0:T(8,128)(2,1)}, bf16[4,1024,512]{2,1,0:T(8,12...) custom-call(bf16[256,1536]{1,0:T(8,128)(2,1)} %copy.52.all_refs_0_, ...), custom_call_target="tpu_custom_call" | custom-call | flops 30064771072 | bytes 1000000000 | tf_op jit(solution)/shard_map/forward/pallas_call | solution.py:1435
  341.2 335.6 %backward.1 = (bf16[4,1024,512]{2,1,0:T(8,128)(2,1)}, bf16[4,1024,512]{2,1,0:T(8,128)(2,1)}, bf16[4,1024,512]{2,1,0:T(8,128)(2,1)}, bf16[4,1024,512]{2,1,0:T(8,1...) custom-call(bf16[1024,512]{1,0:T(8,128)(2,1)} %all_refs_0_.1, ...), custom_call_target="tpu_custom_call" | custom-call | flops 73014444032 | bytes 1000000000 | tf_op jit(solution)/shard_map/backward/pallas_call | solution.py:1435
  676.8 0.0 copy-start.10
  676.8 0.0 copy-start.11
  676.8 0.0 copy-start.13
  676.9 0.0 copy-start.14
  676.9 7.0 adam_mixer.1
  683.9 0.0 copy-start.2
  683.9 0.9 constant_dynamic-slice_fusion
  684.9 0.0 copy-done.10
  684.9 0.6 multiply_subtract_fusion
  685.5 0.6 multiply_subtract_fusion.1
  686.1 0.0 copy-done.8
  686.1 1.0 copy.65
  687.0 0.0 copy-done.7
  687.0 1.3 copy.66
  688.4 2.1 copy.67
  690.5 1.6 copy-done.1
  692.1 2.1 copy.68
  694.2 1.6 copy-done
  695.8 2.1 copy.69
  697.9 1.0 copy-done.6
  698.9 1.3 copy.70
  700.2 1.0 copy-done.5
  701.2 1.3 copy.71
  702.5 1.3 copy.72
  (19 shorter events, 0.0 us)
Async XLA Ops:
  0.7 4.2 copy-start.3
  0.7 4.9 copy-start.9
  0.7 4.9 copy-start.12
  676.8 8.0 %copy-start.10 = (f32[3,64]{1,0:T(4,128)S(1)}, f32[3,64]{1,0:T(4,128)}, u32[]{:S(2)}) copy-start(f32[3,64]{1,0:T(4,128)} %param.37) | copy-start | bytes 2308
  676.8 8.0 %copy-start.11 = (f32[3,64]{1,0:T(4,128)S(1)}, f32[3,64]{1,0:T(4,128)}, u32[]{:S(2)}) copy-start(f32[3,64]{1,0:T(4,128)} %param.38) | copy-start | bytes 2308
  676.8 8.6 %copy-start.13 = (f32[2,64]{1,0:T(2,128)S(1)}, f32[2,64]{1,0:T(2,128)}, u32[]{:S(2)}) copy-start(f32[2,64]{1,0:T(2,128)} %param.40) | copy-start | bytes 1540
  676.9 8.6 %copy-start.14 = (f32[2,64]{1,0:T(2,128)S(1)}, f32[2,64]{1,0:T(2,128)}, u32[]{:S(2)}) copy-start(f32[2,64]{1,0:T(2,128)} %param.41) | copy-start | bytes 1540
  676.9 9.2 %copy-start.8 = (bf16[1024,512]{1,0:T(8,128)(2,1)S(1)}, bf16[1024,512]{1,0:T(8,128)(2,1)}, u32[]{:S(2)}) copy-start(bf16[1024,512]{1,0:T(8,128)(2,1)} %get-tuple-element.134) | copy-start | bytes 3145732
  676.9 10.2 %copy-start.7 = (f32[1024,512]{1,0:T(8,128)S(1)}, f32[1024,512]{1,0:T(8,128)}, u32[]{:S(2)}) copy-start(f32[1024,512]{1,0:T(8,128)} %get-tuple-element.135) | copy-start | bytes 6291460
  683.9 4.4 copy-start.2
  688.4 3.7 copy-start.1
  692.1 3.7 copy-start
  695.8 3.1 copy-start.6
  698.9 2.3 copy-start.5
  698.9 3.7 copy-start.4

commit v10 on v9

--- a/solution.py
+++ b/solution.py
@@ -872,6 +872,12 @@
         self.block = max(rows // 8, 16)
         outs = [((rows, columns // 2), LOW)] * 6
         super().__init__([pairs, plain], outs, [], [rows // self.block], 0)
+        self.scratch[0] = pltpu.VMEM((pairs.shape[0] + 2 * columns // lanes, lanes), pairs.dtype)
+        self.whole_rows = pairs.shape[0]
+
+    def load(self, which):
+        target = self.ins_v[which].at[pl.ds(0, self.whole_rows)] if which == 0 else self.ins_v[which]
+        return pltpu.make_async_copy(self.in_refs[which], target, self.in_sem.at[which])
 
     def peers(self):
         return []
@@ -1212,7 +1218,7 @@
         rows = grads[0].shape[0]
         self.deep = weight.shape[0] // rows
         size = max(rows // 8, 8) * self.deep
-        super().__init__(weight, grads, [pltpu.VMEM((size, LANES), jnp.float32)])
+        super().__init__(weight, grads, [pltpu.VMEM((size + self.deep, LANES), jnp.float32)])
 
     def work(self, phase, index):
         size = self.block * self.deep
@@ -1227,7 +1233,7 @@
                 picked = grad[rows, tile * LANES : (tile + 1) * LANES]
                 mixed[pl.ds(place, self.block, stride=self.deep), :] = picked
         state = [ref[seen, :] for ref in self.ins_v[:3]]
-        for out, result in zip(self.outs_v, adam_update(*state, mixed[...], RATE_WIDE, WEIGHT_DECAY)):
+        for out, result in zip(self.outs_v, adam_update(*state, mixed[0:size, :], RATE_WIDE, WEIGHT_DECAY)):
             out[seen, :] = result
         for which in range(3):
             self.piece(which, index).start()

time: 713 us -> 713 us (level)
  no operation moved by 1% of the time
where the time goes in v10:
time: 713 us; the launch traced here: 704 us
  Pallas kernels  678 us (95%)
  local copies, waits for them, and re-layouts  22.2 us (3%)
    pallas_call x2, Pallas kernels, run(): pl.pallas_call(kernel, out_shape=[self.shapes[made] for made in outputs],...  671 us
    unnamed x39, local copies, waits for them, and re-layouts  19.5 us

profile of v10, /device:TPU:0, one launch (start us, length us, event | category | flops | bytes accessed | tf_op | source)
XLA Modules:
  0.0 704.3 jit_solution(3847361904849540278)
XLA Ops:
  0.7 0.0 copy-start.3
  1.4 0.6 broadcast_in_dim.3.all_refs_5_.all_refs_2_
  2.0 1.7 copy.51
  3.7 1.2 copy.52.all_refs_0_
  4.8 0.7 convert_element_type.13.all_refs_1_
  5.6 0.6 fusion.5.all_refs_2_
  6.2 335.0 %forward.1 = (bf16[4,1024,512]{2,1,0:T(8,128)(2,1)}, bf16[4,1024,512]{2,1,0:T(8,128)(2,1)}, bf16[4,1024,512]{2,1,0:T(8,128)(2,1)}, bf16[4,1024,512]{2,1,0:T(8,12...) custom-call(bf16[256,1536]{1,0:T(8,128)(2,1)} %copy.52.all_refs_0_, ...), custom_call_target="tpu_custom_call" | custom-call | flops 30064771072 | bytes 1000000000 | tf_op jit(solution)/shard_map/forward/pallas_call | solution.py:1441
  341.2 335.6 %backward.1 = (bf16[4,1024,512]{2,1,0:T(8,128)(2,1)}, bf16[4,1024,512]{2,1,0:T(8,128)(2,1)}, bf16[4,1024,512]{2,1,0:T(8,128)(2,1)}, bf16[4,1024,512]{2,1,0:T(8,1...) custom-call(bf16[1024,512]{1,0:T(8,128)(2,1)} %all_refs_0_.1, ...), custom_call_target="tpu_custom_call" | custom-call | flops 73014444032 | bytes 1000000000 | tf_op jit(solution)/shard_map/backward/pallas_call | solution.py:1441
  676.8 0.0 copy-start.10
  676.8 0.0 copy-start.11
  676.8 0.0 copy-start.13
  676.9 0.0 copy-start.14
  676.9 7.0 adam_mixer.1
  683.9 0.0 copy-start.2
  683.9 0.9 constant_dynamic-slice_fusion
  684.9 0.0 copy-done.10
  684.9 0.6 multiply_subtract_fusion
  685.5 0.6 multiply_subtract_fusion.1
  686.1 0.0 copy-done.8
  686.1 1.0 copy.65
  687.0 0.0 copy-done.7
  687.0 1.3 copy.66
  688.4 2.1 copy.67
  690.5 1.6 copy-done.1
  692.1 2.1 copy.68
  694.2 1.6 copy-done
  695.8 2.1 copy.69
  697.9 1.0 copy-done.6
  698.9 1.3 copy.70
  700.2 1.0 copy-done.5
  701.2 1.3 copy.71
  702.5 1.3 copy.72
  (19 shorter events, 0.0 us)
Async XLA Ops:
  0.7 4.2 copy-start.3
  0.7 4.9 copy-start.9
  0.7 4.9 copy-start.12
  676.8 8.0 %copy-start.10 = (f32[3,64]{1,0:T(4,128)S(1)}, f32[3,64]{1,0:T(4,128)}, u32[]{:S(2)}) copy-start(f32[3,64]{1,0:T(4,128)} %param.37) | copy-start | bytes 2308
  676.8 8.0 %copy-start.11 = (f32[3,64]{1,0:T(4,128)S(1)}, f32[3,64]{1,0:T(4,128)}, u32[]{:S(2)}) copy-start(f32[3,64]{1,0:T(4,128)} %param.38) | copy-start | bytes 2308
  676.8 8.6 %copy-start.13 = (f32[2,64]{1,0:T(2,128)S(1)}, f32[2,64]{1,0:T(2,128)}, u32[]{:S(2)}) copy-start(f32[2,64]{1,0:T(2,128)} %param.40) | copy-start | bytes 1540
  676.9 8.6 %copy-start.14 = (f32[2,64]{1,0:T(2,128)S(1)}, f32[2,64]{1,0:T(2,128)}, u32[]{:S(2)}) copy-start(f32[2,64]{1,0:T(2,128)} %param.41) | copy-start | bytes 1540
  676.9 9.2 %copy-start.8 = (bf16[1024,512]{1,0:T(8,128)(2,1)S(1)}, bf16[1024,512]{1,0:T(8,128)(2,1)}, u32[]{:S(2)}) copy-start(bf16[1024,512]{1,0:T(8,128)(2,1)} %get-tuple-element.134) | copy-start | bytes 3145732
  676.9 10.2 %copy-start.7 = (f32[1024,512]{1,0:T(8,128)S(1)}, f32[1024,512]{1,0:T(8,128)}, u32[]{:S(2)}) copy-start(f32[1024,512]{1,0:T(8,128)} %get-tuple-element.135) | copy-start | bytes 6291460
  683.9 4.4 copy-start.2
  688.4 3.7 copy-start.1
  692.1 3.7 copy-start
  695.8 3.1 copy-start.6
  698.9 2.3 copy-start.5
  698.9 3.7 copy-start.4
